TPU v7x, 32 devices: a whole 2x2x4 slice. The times are simulated.
32 devices in a mesh: gx: 4 (over y, x), gy: 2 (over core), gz: 4 (over z).
Axes of the slice: x: 2, y: 2, z: 4, core: 2. Of those that a mesh axis runs over, the one named last changes fastest.
Arguments:
- offsets: float32 [4, 2, 4, 3, 128], P('gx', 'gy', 'gz'), may hold values from 0 to 10
- features: bfloat16 [4, 2, 4, 128, 256], P('gx', 'gy', 'gz'), may hold values from -6 to 6
- counts: int32 [4, 2, 4], P('gx', 'gy', 'gz'), may hold values from 64 to 128
- mask: int32 [4, 2, 4, 128], P('gx', 'gy', 'gz'), may hold values 0 or 1
- targets: float32 [4, 2, 4, 3, 128], P('gx', 'gy', 'gz'), may hold values from -6 to 6
- w_in: bfloat16 [256, 256], replicated, may hold values from -0.375 to 0.375
- radial: float32 [6, 256], replicated, may hold values from -5 to 5
- readout: float32 [256], replicated, may hold values from -0.375 to 0.375
Outputs:
- prediction: float32 [4, 2, 4, 3, 128], P('gx', 'gy', 'gz')
- grad_features: float32 [4, 2, 4, 128, 256], P('gx', 'gy', 'gz')
All inputs are finite; a program needn't handle non-finite values. No bound on the sum of `mask` on one device may be relied on, other than what follows from the above.
Results may differ from a plain program's by a relative error of at most 0.0065.
Values may be sent and summed in bfloat16 or wider, within the bound.
No kernel may reach another device: no remote copies, remote signals or barrier semaphores. Data moves between devices by JAX's collectives and lax.ppermute only.
A program may use at most 64 MiB of HBM per device.

v0:
```python
import jax
import jax.numpy as jnp
from jax import lax
from jax.sharding import PartitionSpec as P

EDGE = 10.0
CUT = 5.0
GAMMA = 20.0
LOSS_WEIGHT = 16.0


def padded(shard, sides, width):
    for axis, dim in sides:
        size, length = (lax.axis_size(axis), shard.shape[dim])
        up = [(i, (i + 1) % size) for i in range(size)]
        down = [(j, i) for i, j in up]
        last = lax.slice_in_dim(shard, length - width, length, axis=dim)
        leading = lax.slice_in_dim(shard, 0, width, axis=dim)
        before = lax.ppermute(last, axis, up)
        after = lax.ppermute(leading, axis, down)
        shard = jnp.concatenate([before, shard, after], axis=dim)
    return shard


def slot_shift(first, count):
    slot = first + jnp.arange(count, dtype=jnp.int32)
    step_x = slot // 9 - 1
    step_y = slot // 3 % 3 - 1
    step_z = slot % 3 - 1
    return jnp.stack([step_x, step_y, step_z], 1).astype(jnp.float32) * EDGE


def build_kernels(own, near, first, count, bases):
    atoms = own.shape[1]
    shift = slot_shift(first, count)
    placed = near[:, :3, :] + shift[:, :, None]
    placed = jnp.transpose(placed, (1, 0, 2)).reshape(3, count * atoms)
    weight_near = near[:, 3, :].reshape(count * atoms)
    apart = placed[:, None, :] - own[:3, :, None]
    ratio = (apart[0] * apart[0] + apart[1] * apart[1] + apart[2] * apart[2]) / (CUT * CUT)
    column = first * atoms + jnp.arange(count * atoms, dtype=jnp.int32)
    same = column[None, :] == (13 * atoms + jnp.arange(atoms, dtype=jnp.int32))[:, None]
    envelope = jnp.where(same, 0.0, jnp.square(jnp.maximum(1.0 - ratio, 0.0)))
    envelope = envelope * own[3][:, None] * weight_near[None, :]
    centers = jnp.arange(bases).astype(jnp.float32) / (bases - 1)
    radial_part = envelope[None] * jnp.exp(
        -GAMMA * jnp.square(ratio[None] - centers[:, None, None])
    )
    direction_part = envelope[None] * apart / CUT
    return jnp.concatenate([radial_part, direction_part], 0).astype(jnp.bfloat16)


def on_device(offsets, features, counts, mask, targets, w_in, radial, readout):
    atoms = features.shape[3]
    width = features.shape[4]
    bases = radial.shape[0]
    hp = lax.Precision.HIGHEST
    occ = (jnp.arange(atoms, dtype=jnp.int32) < counts[0, 0, 0]).astype(jnp.float32)
    own = jnp.concatenate([offsets[0, 0, 0], occ[None, :]], 0)
    near = padded(own.reshape(1, 1, 1, 4, atoms), (("gx", 0), ("gy", 1), ("gz", 2)), 1)
    near = near.reshape(27, 4, atoms)
    proj = jnp.dot(features[0, 0, 0], w_in, preferred_element_type=jnp.float32).astype(jnp.bfloat16)
    near_proj = padded(proj.reshape(1, 1, 1, atoms, width), (("gx", 0), ("gy", 1), ("gz", 2)), 1)
    near_proj = near_proj.reshape(27 * atoms, width)

    def forward_plane(total, plane):
        first = plane * 9
        kern = build_kernels(own, lax.dynamic_slice_in_dim(near, first, 9, 0), first, 9, bases)
        block = lax.dynamic_slice_in_dim(near_proj, first * atoms, 9 * atoms, 0)
        total = total + jnp.einsum("kij,jf->kif", kern, block, preferred_element_type=jnp.float32)
        return (total, kern)

    start = jnp.zeros((bases + 3, atoms, width), jnp.float32)
    msg, kept = lax.scan(forward_plane, start, jnp.arange(3, dtype=jnp.int32))
    pre = jnp.einsum("bf,bif->if", radial, msg[:bases], precision=hp)
    gate = jax.nn.sigmoid(pre)
    gates = readout[None, :] * gate
    gates_bf = gates.astype(jnp.bfloat16)
    vec = msg[bases:]
    pred = jnp.einsum("cif,if->ci", vec, gates, precision=hp)
    err = (
        LOSS_WEIGHT
        * mask[0, 0, 0].astype(jnp.float32)[None, :]
        * occ[None, :]
        * (pred - targets[0, 0, 0])
    )
    slope = (
        jnp.einsum("ci,cif->if", err, vec, precision=hp) * readout[None, :] * gate * (1.0 - gate)
    )
    slope = slope.astype(jnp.bfloat16)
    near_err = padded(err.reshape(1, 1, 1, 3, atoms), (("gx", 0), ("gy", 1), ("gz", 2)), 1)
    near_err = jnp.transpose(near_err.reshape(27, 3, atoms), (1, 0, 2)).reshape(3, 27 * atoms)
    stacked = jnp.concatenate([slope, gates_bf], 1).reshape(1, 1, 1, atoms, 2 * width)
    both = padded(stacked, (("gx", 0), ("gy", 1), ("gz", 2)), 1)
    both = both.reshape(27 * atoms, 2 * width)
    near_slope = both[:, :width]
    near_gates = both[:, width:]

    def backward_plane(total, plane):
        first = plane * 9
        kern = kept[plane]
        err_block = lax.dynamic_slice_in_dim(near_err, first * atoms, 9 * atoms, 1)
        slope_block = lax.dynamic_slice_in_dim(near_slope, first * atoms, 9 * atoms, 0)
        gate_block = lax.dynamic_slice_in_dim(near_gates, first * atoms, 9 * atoms, 0)
        wide = kern[bases:].astype(jnp.float32)
        pairs = (
            wide[0] * err_block[0][None, :]
            + wide[1] * err_block[1][None, :]
            + wide[2] * err_block[2][None, :]
        )
        pairs = pairs.astype(jnp.bfloat16)
        radial_sum = jnp.einsum(
            "bij,jf->bif", kern[:bases], slope_block, preferred_element_type=jnp.float32
        )
        cross = jnp.dot(pairs, gate_block, preferred_element_type=jnp.float32)
        return ((total[0] + radial_sum, total[1] + cross), None)

    begin = (jnp.zeros((bases, atoms, width), jnp.float32), jnp.zeros((atoms, width), jnp.float32))
    sums, unused = lax.scan(backward_plane, begin, jnp.arange(3, dtype=jnp.int32))
    back = jnp.einsum("bf,bif->if", radial, sums[0], precision=hp) - sums[1]
    grad = lax.dot_general(
        back.astype(jnp.bfloat16),
        w_in,
        (((1,), (1,)), ((), ())),
        preferred_element_type=jnp.float32,
    )
    return (pred.reshape(1, 1, 1, 3, atoms), grad.reshape(1, 1, 1, atoms, width))


def solution(mesh):
    in_specs = (
        P("gx", "gy", "gz", None, None),
        P("gx", "gy", "gz", None, None),
        P("gx", "gy", "gz"),
        P("gx", "gy", "gz", None),
        P("gx", "gy", "gz", None, None),
        P(),
        P(),
        P(),
    )
    out_specs = (P("gx", "gy", "gz", None, None), P("gx", "gy", "gz", None, None))
    return jax.shard_map(
        on_device, mesh=mesh, in_specs=in_specs, out_specs=out_specs, check_vma=False
    )
```

profile of v0, /device:TPU:0, one launch (start us, length us, event | category | flops | bytes accessed | tf_op | source)
XLA Modules:
  0.0 184.5 jit_solution(17815759855639468616)
XLA Ops:
  2.5 3.9 %collective-permute-start.7 = (bf16[1,1,1,128,256]{4,3,2,1,0:T(8,128)(2,1)S(1)}, bf16[1,1,1,128,256]{4,3,2,1,0:T(8,128)(2,1)S(1)}, u32[]{:S(2)}, u32[]{:S(2)}) collective-permute-start(bf16[1,1,1,128,256]{4,3,2,1,0:T(8,128)(2,1)S(1)} %fusion.43), channel_id=1, source_target_pairs={{8,0},{16,8},{24,16},{0,24},{9,1},{17,9},{25,17},{1,25},{10,2},{18... | collective-permute-start | bytes 196616 | tf_op jit(solution)/shard_map/ppermute | solution.py:20
  6.5 2.0 %collective-permute-done.7 = bf16[1,1,1,128,256]{4,3,2,1,0:T(8,128)(2,1)S(1)} collective-permute-done((bf16[1,1,1,128,256]{4,3,2,1,0:T(8,128)(2,1)S(1)}, bf16[1,1,1,128,256]{4,3,2,1,0:T(8,128)(2,1)S(1)}, u32[]{:S(2)}, u32[]{:S(2)}) %collective-permute-start.7) | collective-permute-done | bytes 65568 | tf_op jit(solution)/shard_map/ppermute | solution.py:20
  8.5 3.1 %collective-permute-done.6 = bf16[1,1,1,128,256]{4,3,2,1,0:T(8,128)(2,1)S(1)} collective-permute-done((bf16[1,1,1,128,256]{4,3,2,1,0:T(8,128)(2,1)S(1)}, bf16[1,1,1,128,256]{4,3,2,1,0:T(8,128)(2,1)S(1)}, u32[]{:S(2)}, u32[]{:S(2)}) %collective-permute-start.6) | collective-permute-done | bytes 65568 | tf_op jit(solution)/shard_map/ppermute | solution.py:19
  13.7 3.7 %collective-permute-start.11 = (bf16[3,3,1,128,256]{4,3,2,1,0:T(8,128)(2,1)S(1)}, bf16[3,3,1,128,256]{4,3,2,1,0:T(8,128)(2,1)S(1)}, u32[]{:S(2)}, u32[]{:S(2)}) collective-permute-start(bf16[3,3,1,128,256]{4,3,2,1,0:T(8,128)(2,1)S(1)} %pad_maximum_fusion.3), channel_id=1, source_target_pairs={{1,0},{2,1},{3,2},{0,3},{5,4},{6,5},{7,6},{4,7},{9,8},{10,9},{11,1... | collective-permute-start | bytes 1769480 | tf_op jit(solution)/shard_map/ppermute | solution.py:20
  17.7 1.8 collective-permute-start
  19.4 1.6 collective-permute-done.1
  23.5 3.8 %collective-permute-start.5 = (f32[3,3,1,4,128]{4,3,2,1,0:T(4,128)S(1)}, f32[3,3,1,4,128]{4,3,2,1,0:T(4,128)S(1)}, u32[]{:S(2)}, u32[]{:S(2)}) collective-permute-start(f32[3,3,1,4,128]{4,3,2,1,0:T(4,128)S(1)} %pad_maximum_fusion.8), channel_id=1, source_target_pairs={{1,0},{2,1},{3,2},{0,3},{5,4},{6,5},{7,6},{4,7},{9,8},{10,9},{11,1... | collective-permute-start | bytes 55304 | tf_op jit(solution)/shard_map/ppermute | solution.py:20
  27.3 16.1 %collective-permute-done.5 = f32[3,3,1,4,128]{4,3,2,1,0:T(4,128)S(1)} collective-permute-done((f32[3,3,1,4,128]{4,3,2,1,0:T(4,128)S(1)}, f32[3,3,1,4,128]{4,3,2,1,0:T(4,128)S(1)}, u32[]{:S(2)}, u32[]{:S(2)}) %collective-permute-start.5) | collective-permute-done | bytes 18464 | tf_op jit(solution)/shard_map/ppermute | solution.py:20
  44.6 1.4 pad_maximum_fusion.1
  46.0 37.7 %while.31 = (s32[]{:T(128)}, f32[9,128,256]{2,1,0:T(8,128)}, bf16[3,9,128,1152]{3,2,1,0:T(8,128)(2,1)}, s32[3]{0:T(128)S(1)}, f32[27,4,128]{2,1,0:T(4,128)S(1)},...) while((s32[]{:T(128)}, f32[9,128,256]{2,1,0:T(8,128)}, ...), condition=%wide.region_1.2_spmd.clone, body=%wide.region_0.1_spmd.clone.sunk | while | flops 695260416 | bytes 22856984 | solution.py:74
  50.5 2.2 %fusion.87 = (bf16[1,6,128,1152]{3,2,1,0:T(8,128)(2,1)S(1)}, bf16[6,128,1152]{2,1,0:T(8,128)(2,1)}) fusion(f32[6]{0:T(128)S(1)} %convert_multiply_fusion.2, f32[128,1152]{1,0:T(8,128)S(1)} %get-tuple-element.479, f32[128,1152]{1,0:T(8,128)S(1)} %get-tuple-element.477), kind=kLoop, calls=%fused_computation.45.clone.1 | loop fusion | flops 4423680 | bytes 4718616 | tf_op jit(solution)/shard_map/while/body/eval_jaxpr/concatenate | solution.py:50
  52.6 3.9 %fusion.88 = f32[9,128,256]{2,1,0:T(8,128)} fusion(bf16[3,128,1152]{2,1,0:T(8,128)(2,1)} %get-tuple-element.478, bf16[6,128,1152]{2,1,0:T(8,128)(2,1)} %get-tuple-element.480, f32[9,128,256]{2,1,0:T(8,128)} %get-tuple-element.510, bf16[3456,256]{1,0:T(8,128)(2,1)} %get-tuple-element.530, s32[]{:T(128)S(6)} %select_n.143, pred[]{:T(512)S(6)} %compare.6), kind=kOutput, calls=%fused_computation.8.clone.1 | convolution fusion | flops 681394176 | bytes 5603333 | tf_op jit(solution)/shard_map/while/body/eval_jaxpr/kij,jf->kif/dot_general | solution.py:70
  56.5 1.8 maximum_dynamic-update-slice_fusion.2
  62.7 2.2 %fusion.87 = (bf16[1,6,128,1152]{3,2,1,0:T(8,128)(2,1)S(1)}, bf16[6,128,1152]{2,1,0:T(8,128)(2,1)}) fusion(f32[6]{0:T(128)S(1)} %convert_multiply_fusion.2, f32[128,1152]{1,0:T(8,128)S(1)} %get-tuple-element.479, f32[128,1152]{1,0:T(8,128)S(1)} %get-tuple-element.477), kind=kLoop, calls=%fused_computation.45.clone.1 | loop fusion | flops 4423680 | bytes 4718616 | tf_op jit(solution)/shard_map/while/body/eval_jaxpr/concatenate | solution.py:50
  64.9 4.3 %fusion.88 = f32[9,128,256]{2,1,0:T(8,128)} fusion(bf16[3,128,1152]{2,1,0:T(8,128)(2,1)} %get-tuple-element.478, bf16[6,128,1152]{2,1,0:T(8,128)(2,1)} %get-tuple-element.480, f32[9,128,256]{2,1,0:T(8,128)} %get-tuple-element.510, bf16[3456,256]{1,0:T(8,128)(2,1)} %get-tuple-element.530, s32[]{:T(128)S(6)} %select_n.143, pred[]{:T(512)S(6)} %compare.6), kind=kOutput, calls=%fused_computation.8.clone.1 | convolution fusion | flops 681394176 | bytes 5603333 | tf_op jit(solution)/shard_map/while/body/eval_jaxpr/kij,jf->kif/dot_general | solution.py:70
  69.2 1.8 maximum_dynamic-update-slice_fusion.2
  75.5 2.2 %fusion.87 = (bf16[1,6,128,1152]{3,2,1,0:T(8,128)(2,1)S(1)}, bf16[6,128,1152]{2,1,0:T(8,128)(2,1)}) fusion(f32[6]{0:T(128)S(1)} %convert_multiply_fusion.2, f32[128,1152]{1,0:T(8,128)S(1)} %get-tuple-element.479, f32[128,1152]{1,0:T(8,128)S(1)} %get-tuple-element.477), kind=kLoop, calls=%fused_computation.45.clone.1 | loop fusion | flops 4423680 | bytes 4718616 | tf_op jit(solution)/shard_map/while/body/eval_jaxpr/concatenate | solution.py:50
  77.6 4.3 %fusion.88 = f32[9,128,256]{2,1,0:T(8,128)} fusion(bf16[3,128,1152]{2,1,0:T(8,128)(2,1)} %get-tuple-element.478, bf16[6,128,1152]{2,1,0:T(8,128)(2,1)} %get-tuple-element.480, f32[9,128,256]{2,1,0:T(8,128)} %get-tuple-element.510, bf16[3456,256]{1,0:T(8,128)(2,1)} %get-tuple-element.530, s32[]{:T(128)S(6)} %select_n.143, pred[]{:T(512)S(6)} %compare.6), kind=kOutput, calls=%fused_computation.8.clone.1 | convolution fusion | flops 681394176 | bytes 5603333 | tf_op jit(solution)/shard_map/while/body/eval_jaxpr/kij,jf->kif/dot_general | solution.py:70
  81.9 1.8 maximum_dynamic-update-slice_fusion.2
  89.1 1.8 collective-permute-start.12
  90.9 4.0 %collective-permute-done.13 = bf16[1,1,1,128,512]{4,3,2,1,0:T(8,128)(2,1)S(1)} collective-permute-done((bf16[1,1,1,128,512]{4,3,2,1,0:T(8,128)(2,1)S(1)}, bf16[1,1,1,128,512]{4,3,2,1,0:T(8,128)(2,1)S(1)}, u32[]{:S(2)}, u32[]{:S(2)}) %collective-permute-start.13) | collective-permute-done | bytes 131104 | tf_op jit(solution)/shard_map/ppermute | solution.py:20
  99.9 2.8 %collective-permute-start.17 = (bf16[3,3,1,128,512]{4,3,2,1,0:T(8,128)(2,1)}, bf16[3,3,1,128,512]{4,3,2,1,0:T(8,128)(2,1)}, u32[]{:S(2)}, u32[]{:S(2)}) collective-permute-start(bf16[3,3,1,128,512]{4,3,2,1,0:T(8,128)(2,1)} %pad_maximum_fusion.2), channel_id=1, source_target_pairs={{1,0},{2,1},{3,2},{0,3},{5,4},{6,5},{7,6},{4,7},{9,8},{10,9},{11,1... | collective-permute-start | bytes 3538952 | tf_op jit(solution)/shard_map/ppermute | solution.py:20
  104.7 1.6 collective-permute-done.19
  106.2 1.9 %collective-permute-done.18 = f32[1,1,1,3,128]{4,3,2,1,0:T(4,128)S(1)} collective-permute-done((f32[1,1,1,3,128]{4,3,2,1,0:T(4,128)S(1)}, f32[1,1,1,3,128]{4,3,2,1,0:T(4,128)S(1)}, u32[]{:S(2)}, u32[]{:S(2)}) %collective-permute-start.18) | collective-permute-done | bytes 1568 | tf_op jit(solution)/shard_map/ppermute | solution.py:19
  109.5 3.8 %collective-permute-start.23 = (f32[3,3,1,3,128]{4,3,2,1,0:T(4,128)S(1)}, f32[3,3,1,3,128]{4,3,2,1,0:T(4,128)S(1)}, u32[]{:S(2)}, u32[]{:S(2)}) collective-permute-start(f32[3,3,1,3,128]{4,3,2,1,0:T(4,128)S(1)} %pad_maximum_fusion.9), channel_id=1, source_target_pairs={{1,0},{2,1},{3,2},{0,3},{5,4},{6,5},{7,6},{4,7},{9,8},{10,9},{11,1... | collective-permute-start | bytes 41480 | tf_op jit(solution)/shard_map/ppermute | solution.py:20
  113.9 40.4 %collective-permute-done.23 = f32[3,3,1,3,128]{4,3,2,1,0:T(4,128)S(1)} collective-permute-done((f32[3,3,1,3,128]{4,3,2,1,0:T(4,128)S(1)}, f32[3,3,1,3,128]{4,3,2,1,0:T(4,128)S(1)}, u32[]{:S(2)}, u32[]{:S(2)}) %collective-permute-start.23) | collective-permute-done | bytes 13856 | tf_op jit(solution)/shard_map/ppermute | solution.py:20
  155.3 1.8 %pad_maximum_fusion = bf16[3,3,3,128,512]{4,3,2,1,0:T(8,128)(2,1)S(1)} fusion(bf16[3,3,1,128,512]{4,3,2,1,0:T(8,128)(2,1)} %collective-permute-done.17, bf16[3,1,1,128,512]{4,3,2,1,0:T(8,128)(2,1)S(1)} %collective-permute-done.15, bf16[1,1,1,128,512]{4,3,2,1,0:T(8,128)(2,1)S(1)} %collective-permute-done.13, ...), kind=kLoop, calls=%fused_computation.71 | loop fusion | flops 10616832 | bytes 7077888 | tf_op jit(solution)/shard_map/concatenate | solution.py:21
  157.1 2.1 %fusion.60 = (bf16[3456,256]{1,0:T(8,128)(2,1)}, bf16[3456,256]{1,0:T(8,128)(2,1)}) fusion(bf16[3456,512]{1,0:T(8,128)(2,1)S(1)} %bitcast.166), kind=kLoop, calls=%fused_computation.114 | loop fusion | bytes 7077888 | tf_op jit(solution)/shard_map/slice | solution.py:97
  159.2 24.4 %while.32 = (s32[]{:T(128)}, f32[6,128,256]{2,1,0:T(8,128)S(1)}, f32[128,256]{1,0:T(8,128)S(1)}, s32[3]{0:T(128)S(1)}, bf16[3,9,128,1152]{3,2,1,0:T(8,128)(2,1)}...) while((s32[]{:T(128)}, f32[6,128,256]{2,1,0:T(8,128)S(1)}, ...), condition=%wide.region_3.4_spmd.clone, body=%wide.region_2.3_spmd.clone.sunk | while | flops 530268160 | bytes 9249608 | solution.py:119
  162.1 2.5 %fusion.92 = f32[6,128,256]{2,1,0:T(8,128)S(1)} fusion(bf16[3,9,128,1152]{3,2,1,0:T(8,128)(2,1)} %get-tuple-element.575, s32[]{:T(128)S(6)} %select_n.144, f32[6,128,256]{2,1,0:T(8,128)S(1)} %get-tuple-element.556, bf16[3456,256]{1,0:T(8,128)(2,1)} %get-tuple-element.576, s32[]{:T(128)S(6)} %select_n.145, pred[]{:T(512)S(6)} %compare.7), kind=kOutput, calls=%fused_computation.48.clone.1 | convolution fusion | flops 453378048 | bytes 3932169 | tf_op jit(solution)/shard_map/while/body/eval_jaxpr/bij,jf->bif/dot_general | solution.py:112
  170.2 2.5 %fusion.92 = f32[6,128,256]{2,1,0:T(8,128)S(1)} fusion(bf16[3,9,128,1152]{3,2,1,0:T(8,128)(2,1)} %get-tuple-element.575, s32[]{:T(128)S(6)} %select_n.144, f32[6,128,256]{2,1,0:T(8,128)S(1)} %get-tuple-element.556, bf16[3456,256]{1,0:T(8,128)(2,1)} %get-tuple-element.576, s32[]{:T(128)S(6)} %select_n.145, pred[]{:T(512)S(6)} %compare.7), kind=kOutput, calls=%fused_computation.48.clone.1 | convolution fusion | flops 453378048 | bytes 3932169 | tf_op jit(solution)/shard_map/while/body/eval_jaxpr/bij,jf->bif/dot_general | solution.py:112
  178.3 2.5 %fusion.92 = f32[6,128,256]{2,1,0:T(8,128)S(1)} fusion(bf16[3,9,128,1152]{3,2,1,0:T(8,128)(2,1)} %get-tuple-element.575, s32[]{:T(128)S(6)} %select_n.144, f32[6,128,256]{2,1,0:T(8,128)S(1)} %get-tuple-element.556, bf16[3456,256]{1,0:T(8,128)(2,1)} %get-tuple-element.576, s32[]{:T(128)S(6)} %select_n.145, pred[]{:T(512)S(6)} %compare.7), kind=kOutput, calls=%fused_computation.48.clone.1 | convolution fusion | flops 453378048 | bytes 3932169 | tf_op jit(solution)/shard_map/while/body/eval_jaxpr/bij,jf->bif/dot_general | solution.py:112
  (137 shorter events, 42.7 us)
Async XLA Ops:
  0.6 0.9 copy-start
  0.6 26.6 %copy-start.4 = (s32[1,1,1,128]{3,2,1,0:T(1,128)S(1)}, s32[1,1,1,128]{3,2,1,0:T(1,128)}, u32[]{:S(2)}) copy-start(s32[1,1,1,128]{3,2,1,0:T(1,128)} %param.15) | copy-start | bytes 1540
  2.5 6.0 %collective-permute-start.7 = (bf16[1,1,1,128,256]{4,3,2,1,0:T(8,128)(2,1)S(1)}, bf16[1,1,1,128,256]{4,3,2,1,0:T(8,128)(2,1)S(1)}, u32[]{:S(2)}, u32[]{:S(2)}) collective-permute-start(bf16[1,1,1,128,256]{4,3,2,1,0:T(8,128)(2,1)S(1)} %fusion.43), channel_id=1, source_target_pairs={{8,0},{16,8},{24,16},{0,24},{9,1},{17,9},{25,17},{1,25},{10,2},{18... | collective-permute-start | bytes 196616 | tf_op jit(solution)/shard_map/ppermute | solution.py:20
  6.5 5.2 %collective-permute-start.6 = (bf16[1,1,1,128,256]{4,3,2,1,0:T(8,128)(2,1)S(1)}, bf16[1,1,1,128,256]{4,3,2,1,0:T(8,128)(2,1)S(1)}, u32[]{:S(2)}, u32[]{:S(2)}) collective-permute-start(bf16[1,1,1,128,256]{4,3,2,1,0:T(8,128)(2,1)S(1)} %fusion.43), channel_id=1, source_target_pairs={{0,8},{8,16},{16,24},{24,0},{1,9},{9,17},{17,25},{25,1},{2,10},{10... | collective-permute-start | bytes 196616 | tf_op jit(solution)/shard_map/ppermute | solution.py:19
  11.7 1.9 %collective-permute-start.9 = (bf16[3,1,1,128,256]{4,3,2,1,0:T(8,128)(2,1)S(1)}, bf16[3,1,1,128,256]{4,3,2,1,0:T(8,128)(2,1)S(1)}, u32[]{:S(2)}, u32[]{:S(2)}) collective-permute-start(bf16[3,1,1,128,256]{4,3,2,1,0:T(8,128)(2,1)S(1)} %pad_maximum_fusion.5), channel_id=1, source_target_pairs={{4,0},{0,4},{5,1},{1,5},{6,2},{2,6},{7,3},{3,7},{12,8},{8,12},{13,... | collective-permute-start | bytes 589832 | tf_op jit(solution)/shard_map/ppermute | solution.py:20
  11.8 1.8 collective-permute-start.8
  13.7 30.8 %collective-permute-start.11 = (bf16[3,3,1,128,256]{4,3,2,1,0:T(8,128)(2,1)S(1)}, bf16[3,3,1,128,256]{4,3,2,1,0:T(8,128)(2,1)S(1)}, u32[]{:S(2)}, u32[]{:S(2)}) collective-permute-start(bf16[3,3,1,128,256]{4,3,2,1,0:T(8,128)(2,1)S(1)} %pad_maximum_fusion.3), channel_id=1, source_target_pairs={{1,0},{2,1},{3,2},{0,3},{5,4},{6,5},{7,6},{4,7},{9,8},{10,9},{11,1... | collective-permute-start | bytes 1769480 | tf_op jit(solution)/shard_map/ppermute | solution.py:20
  17.3 27.2 %collective-permute-start.10 = (bf16[3,3,1,128,256]{4,3,2,1,0:T(8,128)(2,1)S(1)}, bf16[3,3,1,128,256]{4,3,2,1,0:T(8,128)(2,1)S(1)}, u32[]{:S(2)}, u32[]{:S(2)}) collective-permute-start(bf16[3,3,1,128,256]{4,3,2,1,0:T(8,128)(2,1)S(1)} %pad_maximum_fusion.3), channel_id=1, source_target_pairs={{0,1},{1,2},{2,3},{3,0},{4,5},{5,6},{6,7},{7,4},{8,9},{9,10},{10,1... | collective-permute-start | bytes 1769480 | tf_op jit(solution)/shard_map/ppermute | solution.py:19
  17.4 3.6 %collective-permute-start.1 = (f32[1,1,1,4,128]{4,3,2,1,0:T(4,128)S(1)}, f32[1,1,1,4,128]{4,3,2,1,0:T(4,128)S(1)}, u32[]{:S(2)}, u32[]{:S(2)}) collective-permute-start(f32[1,1,1,4,128]{4,3,2,1,0:T(4,128)S(1)} %maximum_bitcast_fusion.1), channel_id=1, source_target_pairs={{8,0},{16,8},{24,16},{0,24},{9,1},{17,9},{25,17},{1,25},{10,2},{18... | collective-permute-start | bytes 6152 | tf_op jit(solution)/shard_map/ppermute | solution.py:20
  17.7 4.5 %collective-permute-start = (f32[1,1,1,4,128]{4,3,2,1,0:T(4,128)S(1)}, f32[1,1,1,4,128]{4,3,2,1,0:T(4,128)S(1)}, u32[]{:S(2)}, u32[]{:S(2)}) collective-permute-start(f32[1,1,1,4,128]{4,3,2,1,0:T(4,128)S(1)} %maximum_bitcast_fusion.1), channel_id=1, source_target_pairs={{0,8},{8,16},{16,24},{24,0},{1,9},{9,17},{17,25},{25,1},{2,10},{10... | collective-permute-start | bytes 6152 | tf_op jit(solution)/shard_map/ppermute | solution.py:19
  22.2 1.2 collective-permute-start.3
  22.2 1.3 collective-permute-start.2
  23.5 19.9 %collective-permute-start.5 = (f32[3,3,1,4,128]{4,3,2,1,0:T(4,128)S(1)}, f32[3,3,1,4,128]{4,3,2,1,0:T(4,128)S(1)}, u32[]{:S(2)}, u32[]{:S(2)}) collective-permute-start(f32[3,3,1,4,128]{4,3,2,1,0:T(4,128)S(1)} %pad_maximum_fusion.8), channel_id=1, source_target_pairs={{1,0},{2,1},{3,2},{0,3},{5,4},{6,5},{7,6},{4,7},{9,8},{10,9},{11,1... | collective-permute-start | bytes 55304 | tf_op jit(solution)/shard_map/ppermute | solution.py:20
  27.3 17.2 %collective-permute-start.4 = (f32[3,3,1,4,128]{4,3,2,1,0:T(4,128)S(1)}, f32[3,3,1,4,128]{4,3,2,1,0:T(4,128)S(1)}, u32[]{:S(2)}, u32[]{:S(2)}) collective-permute-start(f32[3,3,1,4,128]{4,3,2,1,0:T(4,128)S(1)} %pad_maximum_fusion.8), channel_id=1, source_target_pairs={{0,1},{1,2},{2,3},{3,0},{4,5},{5,6},{6,7},{7,4},{8,9},{9,10},{10,1... | collective-permute-start | bytes 55304 | tf_op jit(solution)/shard_map/ppermute | solution.py:19
  46.0 38.7 %copy-start.1 = (f32[6,256]{1,0:T(8,128)S(1)}, f32[6,256]{1,0:T(8,128)}, u32[]{:S(2)}) copy-start(f32[6,256]{1,0:T(8,128)} %param.18) | copy-start | bytes 18436
  46.0 39.9 %copy-start.2 = (f32[256]{0:T(256)S(1)}, f32[256]{0:T(256)}, u32[]{:S(2)}) copy-start(f32[256]{0:T(256)} %param.19) | copy-start | bytes 3076
  83.7 3.7 %copy-start.3 = (f32[1,1,1,3,128]{4,2,3,1,0:T(1,128)S(1)}, f32[1,1,1,3,128]{4,2,3,1,0:T(1,128)}, u32[]{:S(2)}) copy-start(f32[1,1,1,3,128]{4,2,3,1,0:T(1,128)} %param.16) | copy-start | bytes 4612
  88.8 6.1 %collective-permute-start.13 = (bf16[1,1,1,128,512]{4,3,2,1,0:T(8,128)(2,1)S(1)}, bf16[1,1,1,128,512]{4,3,2,1,0:T(8,128)(2,1)S(1)}, u32[]{:S(2)}, u32[]{:S(2)}) collective-permute-start(bf16[1,1,1,128,512]{4,3,2,1,0:T(8,128)(2,1)S(1)} %maximum_bitcast_fusion), channel_id=1, source_target_pairs={{8,0},{16,8},{24,16},{0,24},{9,1},{17,9},{25,17},{1,25},{10,2},{18... | collective-permute-start | bytes 393224 | tf_op jit(solution)/shard_map/ppermute | solution.py:20
  89.1 7.1 %collective-permute-start.12 = (bf16[1,1,1,128,512]{4,3,2,1,0:T(8,128)(2,1)S(1)}, bf16[1,1,1,128,512]{4,3,2,1,0:T(8,128)(2,1)S(1)}, u32[]{:S(2)}, u32[]{:S(2)}) collective-permute-start(bf16[1,1,1,128,512]{4,3,2,1,0:T(8,128)(2,1)S(1)} %maximum_bitcast_fusion), channel_id=1, source_target_pairs={{0,8},{8,16},{16,24},{24,0},{1,9},{9,17},{17,25},{25,1},{2,10},{10... | collective-permute-start | bytes 393224 | tf_op jit(solution)/shard_map/ppermute | solution.py:19
  96.3 1.8 collective-permute-start.15
  96.4 2.3 %collective-permute-start.14 = (bf16[3,1,1,128,512]{4,3,2,1,0:T(8,128)(2,1)S(1)}, bf16[3,1,1,128,512]{4,3,2,1,0:T(8,128)(2,1)S(1)}, u32[]{:S(2)}, u32[]{:S(2)}) collective-permute-start(bf16[3,1,1,128,512]{4,3,2,1,0:T(8,128)(2,1)S(1)} %pad_maximum_fusion.4), channel_id=1, source_target_pairs={{0,4},{4,0},{1,5},{5,1},{2,6},{6,2},{3,7},{7,3},{8,12},{12,8},{9,1... | collective-permute-start | bytes 1179656 | tf_op jit(solution)/shard_map/ppermute | solution.py:19
  99.9 55.4 %collective-permute-start.17 = (bf16[3,3,1,128,512]{4,3,2,1,0:T(8,128)(2,1)}, bf16[3,3,1,128,512]{4,3,2,1,0:T(8,128)(2,1)}, u32[]{:S(2)}, u32[]{:S(2)}) collective-permute-start(bf16[3,3,1,128,512]{4,3,2,1,0:T(8,128)(2,1)} %pad_maximum_fusion.2), channel_id=1, source_target_pairs={{1,0},{2,1},{3,2},{0,3},{5,4},{6,5},{7,6},{4,7},{9,8},{10,9},{11,1... | collective-permute-start | bytes 3538952 | tf_op jit(solution)/shard_map/ppermute | solution.py:20
  102.6 52.6 %collective-permute-start.16 = (bf16[3,3,1,128,512]{4,3,2,1,0:T(8,128)(2,1)}, bf16[3,3,1,128,512]{4,3,2,1,0:T(8,128)(2,1)}, u32[]{:S(2)}, u32[]{:S(2)}) collective-permute-start(bf16[3,3,1,128,512]{4,3,2,1,0:T(8,128)(2,1)} %pad_maximum_fusion.2), channel_id=1, source_target_pairs={{0,1},{1,2},{2,3},{3,0},{4,5},{5,6},{6,7},{7,4},{8,9},{9,10},{10,1... | collective-permute-start | bytes 3538952 | tf_op jit(solution)/shard_map/ppermute | solution.py:19
  102.6 3.6 %collective-permute-start.19 = (f32[1,1,1,3,128]{4,3,2,1,0:T(4,128)S(1)}, f32[1,1,1,3,128]{4,3,2,1,0:T(4,128)S(1)}, u32[]{:S(2)}, u32[]{:S(2)}) collective-permute-start(f32[1,1,1,3,128]{4,3,2,1,0:T(4,128)S(1)} %get-tuple-element.370), channel_id=1, source_target_pairs={{8,0},{16,8},{24,16},{0,24},{9,1},{17,9},{25,17},{1,25},{10,2},{18... | collective-permute-start | bytes 4616 | tf_op jit(solution)/shard_map/ppermute | solution.py:20
  103.7 4.5 %collective-permute-start.18 = (f32[1,1,1,3,128]{4,3,2,1,0:T(4,128)S(1)}, f32[1,1,1,3,128]{4,3,2,1,0:T(4,128)S(1)}, u32[]{:S(2)}, u32[]{:S(2)}) collective-permute-start(f32[1,1,1,3,128]{4,3,2,1,0:T(4,128)S(1)} %get-tuple-element.370), channel_id=1, source_target_pairs={{0,8},{8,16},{16,24},{24,0},{1,9},{9,17},{17,25},{25,1},{2,10},{10... | collective-permute-start | bytes 4616 | tf_op jit(solution)/shard_map/ppermute | solution.py:19
  108.2 1.2 collective-permute-start.21
  108.2 1.3 collective-permute-start.20
  109.5 44.8 %collective-permute-start.23 = (f32[3,3,1,3,128]{4,3,2,1,0:T(4,128)S(1)}, f32[3,3,1,3,128]{4,3,2,1,0:T(4,128)S(1)}, u32[]{:S(2)}, u32[]{:S(2)}) collective-permute-start(f32[3,3,1,3,128]{4,3,2,1,0:T(4,128)S(1)} %pad_maximum_fusion.9), channel_id=1, source_target_pairs={{1,0},{2,1},{3,2},{0,3},{5,4},{6,5},{7,6},{4,7},{9,8},{10,9},{11,1... | collective-permute-start | bytes 41480 | tf_op jit(solution)/shard_map/ppermute | solution.py:20
  113.3 41.9 %collective-permute-start.22 = (f32[3,3,1,3,128]{4,3,2,1,0:T(4,128)S(1)}, f32[3,3,1,3,128]{4,3,2,1,0:T(4,128)S(1)}, u32[]{:S(2)}, u32[]{:S(2)}) collective-permute-start(f32[3,3,1,3,128]{4,3,2,1,0:T(4,128)S(1)} %pad_maximum_fusion.9), channel_id=1, source_target_pairs={{0,1},{1,2},{2,3},{3,0},{4,5},{5,6},{6,7},{7,4},{8,9},{9,10},{10,1... | collective-permute-start | bytes 41480 | tf_op jit(solution)/shard_map/ppermute | solution.py:19
where the time goes:
time: 185 us
  waiting for transfers between devices  78.7 us (43%)
  other arithmetic  29.3 us (16%)
  matrix products  28.3 us (15%)
  starting transfers between devices  26.3 us (14%)
  loops' own time  11.1 us (6%)
  local copies, waits for them, and re-layouts  9.36 us (5%)
    ppermute x12, waiting for transfers between devices, padded(): after = lax.ppermute(leading, axis, down)  68.3 us
    ppermute x12, starting transfers between devices, padded(): after = lax.ppermute(leading, axis, down)  19.8 us
    dot_general x3, matrix products, forward_plane(): jnp.einsum('kij,jf->kif', kern, block, preferred_element_type=jnp.float32)  12.4 us
    ppermute x12, waiting for transfers between devices, padded(): before = lax.ppermute(last, axis, up)  10.5 us
    concatenate x6, other arithmetic, build_kernels(): jnp.concatenate([radial_part, direction_part], 0).astype(jnp.bfloat16)  10.2 us
    dot_general x3, matrix products, backward_plane(): jnp.einsum('bij,jf->bif', kern[:bases], slope_block, preferred_element_ty...  7.43 us
    another operation x1, loops' own time, on_device(): lax.scan(backward_plane, begin, jnp.arange(3, dtype=jnp.int32))  6.93 us
    ppermute x12, starting transfers between devices, padded(): before = lax.ppermute(last, axis, up)  6.53 us
  transfers between devices with their start and end apart: 24, of which 18 were waited for; matrix products, arithmetic and copies ran while one was open for 1% of the time, Pallas kernels for 0%

commit v1 on v0

v1 whole, which is shorter than its diff:
```python
import functools
import itertools
import math

import jax
import jax.numpy as jnp
from jax import lax
from jax.experimental import pallas as pl
from jax.experimental.pallas import tpu as pltpu
from jax.sharding import PartitionSpec as P

EDGE = 10.0
CUT = 5.0
GAMMA = 20.0
LOSS_WEIGHT = 16.0
FAR = 1000.0
TAIL = 16


def steps_of(size):
    return (0, None) if size == 2 else (0, -1, 1)


def shift(block, axis, step):
    size = lax.axis_size(axis)
    return lax.ppermute(block, axis, [(i, (i + step) % size) for i in range(size)])


def spread(blocks, axis):
    parts = [blocks]
    for step in steps_of(lax.axis_size(axis))[1:]:
        parts.append(shift(blocks, axis, 1 if step is None else -step))
    return parts


def collect(blocks, axis):
    total = blocks[0]
    for part, step in zip(blocks[1:], steps_of(lax.axis_size(axis))[1:]):
        total = total + shift(part, axis, 1 if step is None else step)
    return total


def message_kernel(feat_ref, w_ref, offs_ref, occ_ref, out_ref):
    atoms, width = feat_ref.shape
    out_ref[:atoms, :] = jnp.dot(
        feat_ref[...], w_ref[...], preferred_element_type=jnp.float32
    ).astype(jnp.bfloat16)
    place = jnp.where(occ_ref[...] > 0.0, offs_ref[...], -FAR)
    high = place.astype(jnp.bfloat16)
    rest = place - high.astype(jnp.float32)
    middle = rest.astype(jnp.bfloat16)
    low = (rest - middle.astype(jnp.float32)).astype(jnp.bfloat16)
    rows = jnp.concatenate(
        [
            high.astype(jnp.float32),
            middle.astype(jnp.float32),
            low.astype(jnp.float32),
            jnp.zeros((TAIL - 9, atoms), jnp.float32),
        ],
        0,
    )
    out_ref[atoms:, :atoms] = rows.astype(jnp.bfloat16)
    if width > atoms:
        out_ref[atoms:, atoms:] = jnp.zeros((TAIL, width - atoms), jnp.bfloat16)


def across(row, count):
    return jnp.transpose(jnp.broadcast_to(row, (count, row.shape[1])))


def pair_kernel(
    slots, bases, offs_ref, occ_ref, mask_ref, targ_ref, radial_ref, readout_ref, *refs
):
    groups = len(refs) - 5
    near_refs, (pred_ref, mine_ref, theirs_ref, kern_ref, proj_ref) = refs[:groups], refs[groups:]
    atoms = offs_ref.shape[1]
    width = radial_ref.shape[1]
    columns = near_refs[0].shape[0]
    rate = 2.0 * GAMMA / (bases - 1)
    occ = occ_ref[...]
    own = [across(jnp.where(occ > 0.0, offs_ref[c : c + 1, :], FAR), atoms) for c in range(3)]
    for s, steps in enumerate(slots):
        group, place = divmod(s, columns)
        block = near_refs[group].at[place]
        proj_ref[s * atoms : (s + 1) * atoms, :] = block[:atoms, :]
        coded = block[atoms:, :atoms].astype(jnp.float32)
        apart = []
        for c in range(3):
            spot = coded[c : c + 1, :] + coded[3 + c : 4 + c, :] + coded[6 + c : 7 + c, :]
            if steps[c] is None:
                away = spot - own[c]
                apart.append(away + jnp.where(away < 0.0, EDGE, -EDGE))
            elif steps[c] == 0:
                apart.append(spot - own[c])
            else:
                apart.append((spot + steps[c] * EDGE) - own[c])
        ratio = (apart[0] * apart[0] + apart[1] * apart[1] + apart[2] * apart[2]) * (
            1.0 / (CUT * CUT)
        )
        ratio = jnp.minimum(ratio, 1.0)
        if steps == (0, 0, 0):
            same = lax.broadcasted_iota(jnp.int32, (atoms, atoms), 0) == lax.broadcasted_iota(
                jnp.int32, (atoms, atoms), 1
            )
            ratio = jnp.where(same, 1.0, ratio)
        envelope = jnp.square(1.0 - ratio)
        value = envelope * jnp.exp(-GAMMA * jnp.square(ratio))
        growth = jnp.exp(rate * ratio)
        lanes = slice(s * atoms, (s + 1) * atoms)
        for b in range(bases):
            kern_ref[b * atoms : (b + 1) * atoms, lanes] = value.astype(jnp.bfloat16)
            if b + 1 < bases:
                value = value * growth
        envelope = envelope * (1.0 / CUT)
        for c in range(3):
            kern_ref[(bases + c) * atoms : (bases + c + 1) * atoms, lanes] = (
                envelope * apart[c]
            ).astype(jnp.bfloat16)

    msg = jnp.dot(kern_ref[...], proj_ref[...], preferred_element_type=jnp.float32)
    fold = [math.exp(-GAMMA * (b / (bases - 1)) ** 2) for b in range(bases)]
    weight = [radial_ref[b : b + 1, :] * fold[b] for b in range(bases)]
    pre = weight[0] * msg[:atoms]
    for b in range(1, bases):
        pre = pre + weight[b] * msg[b * atoms : (b + 1) * atoms]
    gate = 1.0 / (1.0 + jnp.exp(-pre))
    readout = readout_ref[...]
    gates = readout * gate
    vec = [msg[(bases + c) * atoms : (bases + c + 1) * atoms] for c in range(3)]
    lean = jnp.zeros((atoms, width), jnp.float32)
    sides = []
    for c in range(3):
        pred = jnp.sum(gates * vec[c], axis=1, keepdims=True)
        pred = jnp.transpose(jnp.broadcast_to(pred, (atoms, atoms)))[0:1, :]
        pred_ref[c : c + 1, :] = pred
        err = LOSS_WEIGHT * mask_ref[...] * occ * (pred - targ_ref[c : c + 1, :])
        err = across(err, width)
        lean = lean + err * vec[c]
        sides.append((err * gates).astype(jnp.bfloat16))
    slope = lean * readout * gate * (1.0 - gate)
    right = jnp.concatenate([(weight[b] * slope).astype(jnp.bfloat16) for b in range(bases)] + sides, 0)
    for s, steps in enumerate(slots):
        lanes = slice(s * atoms, (s + 1) * atoms)
        back = lax.dot_general(
            right, kern_ref[:, lanes], (((0,), (0,)), ((), ())), preferred_element_type=jnp.float32
        ).astype(jnp.bfloat16)
        group, place = divmod(s, columns)
        if group == 0:
            mine_ref[place] = back
        else:
            theirs_ref[group - 1, place] = back


def on_device(offsets, features, counts, mask, targets, w_in, radial, readout):
    atoms = features.shape[3]
    width = features.shape[4]
    bases = radial.shape[0]
    offs = offsets[0, 0, 0]
    occ = (jnp.arange(atoms, dtype=jnp.int32) < counts[0, 0, 0]).astype(jnp.float32)[None, :]
    vmem = pl.BlockSpec(memory_space=pltpu.VMEM)
    message = pl.pallas_call(
        message_kernel,
        out_shape=jax.ShapeDtypeStruct((atoms + TAIL, width), jnp.bfloat16),
        in_specs=[vmem] * 4,
        out_specs=vmem,
        name="message",
    )(features[0, 0, 0], w_in, offs, occ)

    steps_x, steps_y, steps_z = (steps_of(lax.axis_size(a)) for a in ("gx", "gy", "gz"))
    near = message[None]
    near = jnp.concatenate(spread(near, "gz"), 0)
    near = jnp.concatenate(spread(near, "gx"), 0)
    near = spread(near, "gy")
    columns = len(steps_x) * len(steps_z)
    slots = [(x, y, z) for y, x, z in itertools.product(steps_y, steps_x, steps_z)]

    pred, mine, theirs = pl.pallas_call(
        functools.partial(pair_kernel, slots, bases),
        out_shape=(
            jax.ShapeDtypeStruct((3, atoms), jnp.float32),
            jax.ShapeDtypeStruct((columns, width, atoms), jnp.bfloat16),
            jax.ShapeDtypeStruct((len(steps_y) - 1, columns, width, atoms), jnp.bfloat16),
        ),
        in_specs=[vmem] * (6 + len(near)),
        out_specs=[vmem] * 3,
        scratch_shapes=[
            pltpu.VMEM(((bases + 3) * atoms, len(slots) * atoms), jnp.bfloat16),
            pltpu.VMEM((len(slots) * atoms, width), jnp.bfloat16),
        ],
        compiler_params=pltpu.CompilerParams(vmem_limit_bytes=40 * 1024 * 1024),
        name="pairs",
    )(
        offs,
        occ,
        mask[0, 0, 0].astype(jnp.float32)[None, :],
        targets[0, 0, 0],
        radial,
        readout[None, :],
        *near,
    )
    back = collect([mine] + [theirs[k] for k in range(len(steps_y) - 1)], "gy")
    back = back.reshape(len(steps_x), len(steps_z), width, atoms)
    back = collect([back[k] for k in range(len(steps_x))], "gx")
    back = collect([back[k] for k in range(len(steps_z))], "gz")
    grad = lax.dot_general(
        back, w_in, (((0,), (1,)), ((), ())), preferred_element_type=jnp.float32
    )
    return (pred.reshape(1, 1, 1, 3, atoms), grad.reshape(1, 1, 1, atoms, width))


def solution(mesh):
    in_specs = (
        P("gx", "gy", "gz", None, None),
        P("gx", "gy", "gz", None, None),
        P("gx", "gy", "gz"),
        P("gx", "gy", "gz", None),
        P("gx", "gy", "gz", None, None),
        P(),
        P(),
        P(),
    )
    out_specs = (P("gx", "gy", "gz", None, None), P("gx", "gy", "gz", None, None))
    return jax.shard_map(
        on_device, mesh=mesh, in_specs=in_specs, out_specs=out_specs, check_vma=False
    )
```

time: 185 us -> 59.2 us (0.32)
  waiting for transfers between devices: 78.7 us -> 30.8 us
  other arithmetic: 29.3 us -> 0.77 us
  matrix products: 28.3 us -> 0.86 us
  starting transfers between devices: 26.3 us -> 12 us
  loops' own time: 11.1 us -> 0 us
  Pallas kernels: 0 us -> 9.55 us
  local copies, waits for them, and re-layouts: 9.36 us -> 3.56 us
    ppermute x24 -> x10, waiting for transfers between devices: 78.7 us -> 30.8 us  [shift(): lax.ppermute(block, axis, [(i, (i + step) % size) for i in range(size)])]
    dot_general x13 -> x1, matrix products: 28.3 us -> 0.86 us  [on_device(): lax.dot_general(back, w_in, (((0,), (1,)), ((), ())), preferred_element_t...]
    concatenate x18 -> x1, other arithmetic: 14.9 us -> 0.03 us  [on_device(): near = jnp.concatenate(spread(near, 'gz'), 0)]
    ppermute x24 -> x10, starting transfers between devices: 26.3 us -> 12 us  [shift(): lax.ppermute(block, axis, [(i, (i + step) % size) for i in range(size)])]
    another operation x2 -> x0, loops' own time: 11.1 us -> none  [the longest x1 6.93 us: on_device(): lax.scan(backward_plane, begin, jnp.arange(3, dtype=jnp.int32))]
    pallas_call x0 -> x2, Pallas kernels: none -> 9.55 us  [the longest x1 7.84 us: on_device(): pl.pallas_call(functools.partial(pair_kernel, slots, bases), out_shape=(j...]
    dynamic_update_slice x3 -> x0, other arithmetic: 5.38 us -> none  [on_device(): msg, kept = lax.scan(forward_plane, start, jnp.arange(3, dtype=jnp.int32))]
    convert_element_type x4 -> x1, other arithmetic: 3.94 us -> 0.01 us  [on_device(): mask[0, 0, 0].astype(jnp.float32)[None, :]]
  transfers between devices with their start and end apart: 24 -> 10, of which waited for: 18 -> 9; matrix products, arithmetic and copies ran while one was open for 1% -> 3% of each run, Pallas kernels for 0% -> 0%
where the time goes in v1:
time: 59.2 us; the launch traced here: 58.9 us
  waiting for transfers between devices  30.8 us (52%)
  starting transfers between devices  12 us (20%)
  Pallas kernels  9.55 us (16%)
  local copies, waits for them, and re-layouts  3.56 us (6%)
  between operations  1.42 us (2%)
  matrix products  0.86 us (1%)
  other arithmetic  0.77 us (1%)
    ppermute x10, waiting for transfers between devices, shift(): lax.ppermute(block, axis, [(i, (i + step) % size) for i in range(size)])  30.8 us
    ppermute x10, starting transfers between devices, shift(): lax.ppermute(block, axis, [(i, (i + step) % size) for i in range(size)])  12 us
    pallas_call x1, Pallas kernels, on_device(): pl.pallas_call(functools.partial(pair_kernel, slots, bases), out_shape=(j...  7.84 us
    unnamed x25, local copies, waits for them, and re-layouts  3.5 us
    pallas_call x1, Pallas kernels, on_device(): pl.pallas_call(message_kernel, out_shape=jax.ShapeDtypeStruct((atoms + TA...  1.71 us
  transfers between devices with their start and end apart: 10, of which 9 were waited for; matrix products, arithmetic and copies ran while one was open for 3% of the time, Pallas kernels for 0%

profile of v1, /device:TPU:0, one launch (start us, length us, event | category | flops | bytes accessed | tf_op | source)
XLA Modules:
  0.0 58.9 jit_solution(5947234302304618962)
XLA Ops:
  1.3 0.5 compare_convert_fusion.occ_ref
  1.8 0.1 copy-done.6
  2.0 0.6 copy.16
  2.5 1.7 %message.1 = bf16[144,256]{1,0:T(8,128)(2,1)} custom-call(bf16[128,256]{1,0:T(8,128)(2,1)} %bitcast.39, bf16[256,256]{1,0:T(8,128)(2,1)} %w_ref.1, f32[3,128]{1,0:T(4,128)} %bitcast.30, f32[1,128]{1,0:T(1,128)} %compare_convert_fusion.occ_ref), custom_call_target="tpu_custom_call" | custom-call | tf_op jit(solution)/shard_map/message/pallas_call | solution.py:161
  4.2 5.0 %collective-permute-start.1 = (bf16[1,144,256]{2,1,0:T(8,128)(2,1)}, bf16[1,144,256]{2,1,0:T(8,128)(2,1)S(1)}, u32[]{:S(2)}, u32[]{:S(2)}) collective-permute-start(bf16[1,144,256]{2,1,0:T(8,128)(2,1)} %bitcast.36), channel_id=1, source_target_pairs={{0,3},{1,0},{2,1},{3,2},{4,7},{5,4},{6,5},{7,6},{8,11},{9,8},{10,9... | collective-permute-start | bytes 221192 | tf_op jit(solution)/shard_map/ppermute | solution.py:26
  9.3 1.0 %constant_dynamic-update-slice_fusion.4 = bf16[9,144,256]{2,1,0:T(8,128)(2,1)S(1)} fusion(bf16[144,256]{1,0:T(8,128)(2,1)} %message.1), kind=kLoop, calls=%fused_computation.13 | loop fusion | bytes 147456
  10.2 1.7 %collective-permute-done.1 = bf16[1,144,256]{2,1,0:T(8,128)(2,1)S(1)} collective-permute-done((bf16[1,144,256]{2,1,0:T(8,128)(2,1)}, bf16[1,144,256]{2,1,0:T(8,128)(2,1)S(1)}, u32[]{:S(2)}, u32[]{:S(2)}) %collective-permute-start.1) | collective-permute-done | bytes 73760 | tf_op jit(solution)/shard_map/ppermute | solution.py:26
  11.9 3.7 %collective-permute-done = bf16[1,144,256]{2,1,0:T(8,128)(2,1)S(1)} collective-permute-done((bf16[1,144,256]{2,1,0:T(8,128)(2,1)}, bf16[1,144,256]{2,1,0:T(8,128)(2,1)S(1)}, u32[]{:S(2)}, u32[]{:S(2)}) %collective-permute-start) | collective-permute-done | bytes 73760 | tf_op jit(solution)/shard_map/ppermute | solution.py:26
  15.7 2.5 %collective-permute-start.3 = (bf16[3,144,256]{2,1,0:T(8,128)(2,1)S(1)}, bf16[3,144,256]{2,1,0:T(8,128)(2,1)S(1)}, u32[]{:S(2)}, u32[]{:S(2)}) collective-permute-start(bf16[3,144,256]{2,1,0:T(8,128)(2,1)S(1)} %pad_maximum_fusion), channel_id=1, source_target_pairs={{0,24},{8,0},{16,8},{24,16},{1,25},{9,1},{17,9},{25,17},{2,26},{10... | collective-permute-start | bytes 663560 | tf_op jit(solution)/shard_map/ppermute | solution.py:26
  18.2 9.0 %collective-permute-done.2 = bf16[3,144,256]{2,1,0:T(8,128)(2,1)S(1)} collective-permute-done((bf16[3,144,256]{2,1,0:T(8,128)(2,1)S(1)}, bf16[3,144,256]{2,1,0:T(8,128)(2,1)S(1)}, u32[]{:S(2)}, u32[]{:S(2)}) %collective-permute-start.2) | collective-permute-done | bytes 221216 | tf_op jit(solution)/shard_map/ppermute | solution.py:26
  27.2 0.0 copy-start.7
  27.2 0.0 copy-start.1
  27.3 0.1 collective-permute-start.4
  27.3 0.5 copy-done.7
  27.9 0.0 copy-done.8
  27.9 1.5 %collective-permute-done.4.refs_1_ = bf16[9,144,256]{2,1,0:T(8,128)(2,1)S(1)} collective-permute-done((bf16[9,144,256]{2,1,0:T(8,128)(2,1)S(1)}, bf16[9,144,256]{2,1,0:T(8,128)(2,1)S(1)}, u32[]{:S(2)}, u32[]{:S(2)}) %collective-permute-start.4) | collective-permute-done | bytes 663584 | tf_op jit(solution)/shard_map/ppermute | solution.py:26
  29.4 0.6 %copy-done.2 = f32[1,128]{1,0:T(1,128)S(1)} copy-done((f32[1,128]{1,0:T(1,128)S(1)}, f32[1,128]{1,0:T(1,128)}, u32[]{:S(2)}) %copy-start.2) | copy-done | bytes 536
  30.1 0.0 copy-done.3
  30.1 7.8 %pairs.1 = (f32[3,128]{1,0:T(4,128)S(1)}, bf16[9,256,128]{2,1,0:T(8,128)(2,1)S(1)}, bf16[1,9,256,128]{3,2,1,0:T(8,128)(2,1)S(1)}) custom-call(f32[3,128]{1,0:T(4,128)S(1)} %bitcast.31, f32[1,128]{1,0:T(1,128)S(1)} %copy-done.2, f32[1,128]{1,0:T(1,128)S(1)} %convert_bitcast_fusion.mask_ref, f32[3,128]{1,0:T(4,128)S(1)} %bitcast.32, f32[6,256]{1,0:T(8,128)S(1)} %copy-done.1, ...), custom_call_target="tpu_custom_call" | custom-call | tf_op jit(solution)/shard_map/pairs/pallas_call | solution.py:177
  38.0 0.2 collective-permute-start.5
  38.2 1.9 %collective-permute-done.5 = bf16[9,256,128]{2,1,0:T(8,128)(2,1)S(1)} collective-permute-done((bf16[9,256,128]{2,1,0:T(8,128)(2,1)S(1)}, bf16[9,256,128]{2,1,0:T(8,128)(2,1)S(1)}, u32[]{:S(2)}, u32[]{:S(2)}) %collective-permute-start.5) | collective-permute-done | bytes 589856 | tf_op jit(solution)/shard_map/ppermute | solution.py:26
  40.0 0.2 add.15
  40.2 1.5 %collective-permute-start.6 = (bf16[3,256,128]{2,1,0:T(8,128)(2,1)S(1)}, bf16[3,256,128]{2,1,0:T(8,128)(2,1)S(1)}, u32[]{:S(2)}, u32[]{:S(2)}) collective-permute-start(bf16[3,256,128]{2,1,0:T(8,128)(2,1)S(1)} %get-tuple-element.10), channel_id=1, source_target_pairs={{0,24},{8,0},{16,8},{24,16},{1,25},{9,1},{17,9},{25,17},{2,26},{10... | collective-permute-start | bytes 589832 | tf_op jit(solution)/shard_map/ppermute | solution.py:26
  41.7 0.6 %collective-permute-start.7 = (bf16[3,256,128]{2,1,0:T(8,128)(2,1)S(1)}, bf16[3,256,128]{2,1,0:T(8,128)(2,1)S(1)}, u32[]{:S(2)}, u32[]{:S(2)}) collective-permute-start(bf16[3,256,128]{2,1,0:T(8,128)(2,1)S(1)} %get-tuple-element.11), channel_id=1, source_target_pairs={{0,8},{8,16},{16,24},{24,0},{1,9},{9,17},{17,25},{25,1},{2,10},{10... | collective-permute-start | bytes 589832 | tf_op jit(solution)/shard_map/ppermute | solution.py:26
  42.3 5.7 %collective-permute-done.6 = bf16[3,256,128]{2,1,0:T(8,128)(2,1)S(1)} collective-permute-done((bf16[3,256,128]{2,1,0:T(8,128)(2,1)S(1)}, bf16[3,256,128]{2,1,0:T(8,128)(2,1)S(1)}, u32[]{:S(2)}, u32[]{:S(2)}) %collective-permute-start.6) | collective-permute-done | bytes 196640 | tf_op jit(solution)/shard_map/ppermute | solution.py:26
  48.0 3.4 %collective-permute-done.7 = bf16[3,256,128]{2,1,0:T(8,128)(2,1)S(1)} collective-permute-done((bf16[3,256,128]{2,1,0:T(8,128)(2,1)S(1)}, bf16[3,256,128]{2,1,0:T(8,128)(2,1)S(1)}, u32[]{:S(2)}, u32[]{:S(2)}) %collective-permute-start.7) | collective-permute-done | bytes 196640 | tf_op jit(solution)/shard_map/ppermute | solution.py:26
  51.5 0.5 collective-permute-start.8
  52.0 1.6 %collective-permute-start.9 = (bf16[256,128]{1,0:T(8,128)(2,1)S(1)}, bf16[256,128]{1,0:T(8,128)(2,1)S(1)}, u32[]{:S(2)}, u32[]{:S(2)}) collective-permute-start(bf16[256,128]{1,0:T(8,128)(2,1)S(1)} %get-tuple-element.13), channel_id=1, source_target_pairs={{0,1},{1,2},{2,3},{3,0},{4,5},{5,6},{6,7},{7,4},{8,9},{9,10},{10,1... | collective-permute-start | bytes 196616 | tf_op jit(solution)/shard_map/ppermute | solution.py:26
  53.5 0.6 copy.10
  54.1 2.4 %collective-permute-done.8 = bf16[256,128]{1,0:T(8,128)(2,1)S(1)} collective-permute-done((bf16[256,128]{1,0:T(8,128)(2,1)S(1)}, bf16[256,128]{1,0:T(8,128)(2,1)S(1)}, u32[]{:S(2)}, u32[]{:S(2)}) %collective-permute-start.8) | collective-permute-done | bytes 65568 | tf_op jit(solution)/shard_map/ppermute | solution.py:26
  56.5 1.5 %collective-permute-done.9 = bf16[256,128]{1,0:T(8,128)(2,1)S(1)} collective-permute-done((bf16[256,128]{1,0:T(8,128)(2,1)S(1)}, bf16[256,128]{1,0:T(8,128)(2,1)S(1)}, u32[]{:S(2)}, u32[]{:S(2)}) %collective-permute-start.9) | collective-permute-done | bytes 65568 | tf_op jit(solution)/shard_map/ppermute | solution.py:26
  58.0 0.9 %convolution_bitcast_fusion = f32[1,1,1,128,256]{4,3,2,1,0:T(8,128)} fusion(bf16[256,256]{1,0:T(8,128)(2,1)S(1)} %copy-done.5, bf16[256,128]{1,0:T(8,128)(2,1)S(1)} %collective-permute-done.9, bf16[256,128]{1,0:T(8,128)(2,1)S(1)} %collective-permute-done.8, bf16[3,256,128]{2,1,0:T(8,128)(2,1)S(1)} %fusion), kind=kOutput, calls=%fused_computation | convolution fusion | flops 16842752 | bytes 458752 | tf_op jit(solution)/shard_map/dot_general | solution.py:205
  (24 shorter events, 0.2 us)
Async XLA Ops:
  1.3 0.7 %copy-start.6 = (f32[1,1,1,3,128]{4,2,3,1,0:T(1,128)S(1)}, f32[1,1,1,3,128]{4,2,3,1,0:T(1,128)}, u32[]{:S(2)}) copy-start(f32[1,1,1,3,128]{4,2,3,1,0:T(1,128)} %param.8) | copy-start | bytes 4612
  4.2 11.4 %copy-start.4 = (bf16[144,256]{1,0:T(8,128)(2,1)S(1)}, bf16[144,256]{1,0:T(8,128)(2,1)}, u32[]{:S(2)}) copy-start(bf16[144,256]{1,0:T(8,128)(2,1)} %message.1) | copy-start | bytes 221188
  4.2 7.7 %collective-permute-start.1 = (bf16[1,144,256]{2,1,0:T(8,128)(2,1)}, bf16[1,144,256]{2,1,0:T(8,128)(2,1)S(1)}, u32[]{:S(2)}, u32[]{:S(2)}) collective-permute-start(bf16[1,144,256]{2,1,0:T(8,128)(2,1)} %bitcast.36), channel_id=1, source_target_pairs={{0,3},{1,0},{2,1},{3,2},{4,7},{5,4},{6,5},{7,6},{8,11},{9,8},{10,9... | collective-permute-start | bytes 221192 | tf_op jit(solution)/shard_map/ppermute | solution.py:26
  9.3 6.4 %collective-permute-start = (bf16[1,144,256]{2,1,0:T(8,128)(2,1)}, bf16[1,144,256]{2,1,0:T(8,128)(2,1)S(1)}, u32[]{:S(2)}, u32[]{:S(2)}) collective-permute-start(bf16[1,144,256]{2,1,0:T(8,128)(2,1)} %bitcast.37), channel_id=1, source_target_pairs={{0,1},{1,2},{2,3},{3,0},{4,5},{5,6},{6,7},{7,4},{8,9},{9,10},{10,1... | collective-permute-start | bytes 221192 | tf_op jit(solution)/shard_map/ppermute | solution.py:26
  15.7 11.5 %collective-permute-start.3 = (bf16[3,144,256]{2,1,0:T(8,128)(2,1)S(1)}, bf16[3,144,256]{2,1,0:T(8,128)(2,1)S(1)}, u32[]{:S(2)}, u32[]{:S(2)}) collective-permute-start(bf16[3,144,256]{2,1,0:T(8,128)(2,1)S(1)} %pad_maximum_fusion), channel_id=1, source_target_pairs={{0,24},{8,0},{16,8},{24,16},{1,25},{9,1},{17,9},{25,17},{2,26},{10... | collective-permute-start | bytes 663560 | tf_op jit(solution)/shard_map/ppermute | solution.py:26
  18.2 9.0 %collective-permute-start.2 = (bf16[3,144,256]{2,1,0:T(8,128)(2,1)S(1)}, bf16[3,144,256]{2,1,0:T(8,128)(2,1)S(1)}, u32[]{:S(2)}, u32[]{:S(2)}) collective-permute-start(bf16[3,144,256]{2,1,0:T(8,128)(2,1)S(1)} %pad_maximum_fusion), channel_id=1, source_target_pairs={{0,8},{8,16},{16,24},{24,0},{1,9},{9,17},{17,25},{25,1},{2,10},{10... | collective-permute-start | bytes 663560 | tf_op jit(solution)/shard_map/ppermute | solution.py:26
  27.2 0.7 %copy-start.7 = (f32[1,1,1,3,128]{4,2,3,1,0:T(1,128)S(1)}, f32[1,1,1,3,128]{4,2,3,1,0:T(1,128)}, u32[]{:S(2)}) copy-start(f32[1,1,1,3,128]{4,2,3,1,0:T(1,128)} %param.12) | copy-start | bytes 4612
  27.2 2.2 %copy-start.1 = (f32[6,256]{1,0:T(8,128)S(1)}, f32[6,256]{1,0:T(8,128)}, u32[]{:S(2)}) copy-start(f32[6,256]{1,0:T(8,128)} %radial_ref.1) | copy-start | bytes 18436
  27.2 0.7 %copy-start.8 = (s32[1,1,1,128]{3,2,1,0:T(1,128)S(1)}, s32[1,1,1,128]{3,2,1,0:T(1,128)}, u32[]{:S(2)}) copy-start(s32[1,1,1,128]{3,2,1,0:T(1,128)} %param.11) | copy-start | bytes 1540
  27.3 2.2 %collective-permute-start.4 = (bf16[9,144,256]{2,1,0:T(8,128)(2,1)S(1)}, bf16[9,144,256]{2,1,0:T(8,128)(2,1)S(1)}, u32[]{:S(2)}, u32[]{:S(2)}) collective-permute-start(bf16[9,144,256]{2,1,0:T(8,128)(2,1)S(1)} %constant_dynamic-update-slice_fusion.refs_0_), channel_id=1, source_target_pairs={{0,4},{4,0},{1,5},{5,1},{2,6},{6,2},{3,7},{7,3},{8,12},{12,8},{9,1... | collective-permute-start | bytes 1990664 | tf_op jit(solution)/shard_map/ppermute | solution.py:26
  27.9 1.5 %copy-start = (f32[1,1,1,3,128]{4,3,2,1,0:T(4,128)S(1)}, f32[1,1,1,3,128]{4,3,2,1,0:T(4,128)}, u32[]{:S(2)}) copy-start(f32[1,1,1,3,128]{4,3,2,1,0:T(4,128)} %copy.16) | copy-start | bytes 4612
  29.4 0.6 %copy-start.2 = (f32[1,128]{1,0:T(1,128)S(1)}, f32[1,128]{1,0:T(1,128)}, u32[]{:S(2)}) copy-start(f32[1,128]{1,0:T(1,128)} %compare_convert_fusion.occ_ref) | copy-start | bytes 1540
  29.4 0.7 %copy-start.3 = (f32[256]{0:T(256)S(1)}, f32[256]{0:T(256)}, u32[]{:S(2)}) copy-start(f32[256]{0:T(256)} %param.15) | copy-start | bytes 3076
  38.0 2.1 %collective-permute-start.5 = (bf16[9,256,128]{2,1,0:T(8,128)(2,1)S(1)}, bf16[9,256,128]{2,1,0:T(8,128)(2,1)S(1)}, u32[]{:S(2)}, u32[]{:S(2)}) collective-permute-start(bf16[9,256,128]{2,1,0:T(8,128)(2,1)S(1)} %bitcast.35), channel_id=1, source_target_pairs={{0,4},{4,0},{1,5},{5,1},{2,6},{6,2},{3,7},{7,3},{8,12},{12,8},{9,1... | collective-permute-start | bytes 1769480 | tf_op jit(solution)/shard_map/ppermute | solution.py:26
  40.2 7.8 %collective-permute-start.6 = (bf16[3,256,128]{2,1,0:T(8,128)(2,1)S(1)}, bf16[3,256,128]{2,1,0:T(8,128)(2,1)S(1)}, u32[]{:S(2)}, u32[]{:S(2)}) collective-permute-start(bf16[3,256,128]{2,1,0:T(8,128)(2,1)S(1)} %get-tuple-element.10), channel_id=1, source_target_pairs={{0,24},{8,0},{16,8},{24,16},{1,25},{9,1},{17,9},{25,17},{2,26},{10... | collective-permute-start | bytes 589832 | tf_op jit(solution)/shard_map/ppermute | solution.py:26
  41.7 9.7 %collective-permute-start.7 = (bf16[3,256,128]{2,1,0:T(8,128)(2,1)S(1)}, bf16[3,256,128]{2,1,0:T(8,128)(2,1)S(1)}, u32[]{:S(2)}, u32[]{:S(2)}) collective-permute-start(bf16[3,256,128]{2,1,0:T(8,128)(2,1)S(1)} %get-tuple-element.11), channel_id=1, source_target_pairs={{0,8},{8,16},{16,24},{24,0},{1,9},{9,17},{17,25},{25,1},{2,10},{10... | collective-permute-start | bytes 589832 | tf_op jit(solution)/shard_map/ppermute | solution.py:26
  51.4 6.6 %copy-start.5 = (bf16[256,256]{1,0:T(8,128)(2,1)S(1)}, bf16[256,256]{1,0:T(8,128)(2,1)}, u32[]{:S(2)}) copy-start(bf16[256,256]{1,0:T(8,128)(2,1)} %w_ref.1) | copy-start | bytes 393220
  51.5 5.0 %collective-permute-start.8 = (bf16[256,128]{1,0:T(8,128)(2,1)S(1)}, bf16[256,128]{1,0:T(8,128)(2,1)S(1)}, u32[]{:S(2)}, u32[]{:S(2)}) collective-permute-start(bf16[256,128]{1,0:T(8,128)(2,1)S(1)} %get-tuple-element.12), channel_id=1, source_target_pairs={{0,3},{1,0},{2,1},{3,2},{4,7},{5,4},{6,5},{7,6},{8,11},{9,8},{10,9... | collective-permute-start | bytes 196616 | tf_op jit(solution)/shard_map/ppermute | solution.py:26
  52.0 6.1 %collective-permute-start.9 = (bf16[256,128]{1,0:T(8,128)(2,1)S(1)}, bf16[256,128]{1,0:T(8,128)(2,1)S(1)}, u32[]{:S(2)}, u32[]{:S(2)}) collective-permute-start(bf16[256,128]{1,0:T(8,128)(2,1)S(1)} %get-tuple-element.13), channel_id=1, source_target_pairs={{0,1},{1,2},{2,3},{3,0},{4,5},{5,6},{6,7},{7,4},{8,9},{9,10},{10,1... | collective-permute-start | bytes 196616 | tf_op jit(solution)/shard_map/ppermute | solution.py:26

commit v2 on v1

v2 whole, which is shorter than its diff:
```python
import functools
import itertools
import math

import jax
import jax.numpy as jnp
from jax import lax
from jax.experimental import pallas as pl
from jax.experimental.pallas import tpu as pltpu
from jax.sharding import PartitionSpec as P

EDGE = 10.0
CUT = 5.0
GAMMA = 20.0
LOSS_WEIGHT = 16.0
FAR = 1000.0
TAIL = 16


def steps_of(size):
    return (0, None) if size == 2 else (0, -1, 1)


def shift(block, axis, step):
    size = lax.axis_size(axis)
    return lax.ppermute(block, axis, [(i, (i + step) % size) for i in range(size)])


def spread(blocks, axis):
    parts = [blocks]
    for step in steps_of(lax.axis_size(axis))[1:]:
        parts.append(shift(blocks, axis, 1 if step is None else -step))
    return parts


def collect(blocks, axis):
    total = blocks[0]
    for part, step in zip(blocks[1:], steps_of(lax.axis_size(axis))[1:]):
        total = total + shift(part, axis, 1 if step is None else step)
    return total


def occupied(counts_ref, atoms):
    return lax.broadcasted_iota(jnp.int32, (1, atoms), 1) < counts_ref[0]


def message_kernel(feat_ref, w_ref, offs_ref, counts_ref, out_ref):
    atoms, width = feat_ref.shape
    place = jnp.where(occupied(counts_ref, atoms), offs_ref[:, 0, :], -FAR)
    out_ref[:atoms, :] = jnp.dot(
        feat_ref[...], w_ref[...], preferred_element_type=jnp.float32
    ).astype(jnp.bfloat16)
    high = place.astype(jnp.bfloat16)
    rest = place - high.astype(jnp.float32)
    middle = rest.astype(jnp.bfloat16)
    low = (rest - middle.astype(jnp.float32)).astype(jnp.bfloat16)
    rows = jnp.concatenate(
        [
            high.astype(jnp.float32),
            middle.astype(jnp.float32),
            low.astype(jnp.float32),
            jnp.zeros((TAIL - 9, atoms), jnp.float32),
        ],
        0,
    )
    out_ref[atoms:, :atoms] = rows.astype(jnp.bfloat16)
    if width > atoms:
        out_ref[atoms:, atoms:] = jnp.zeros((TAIL, width - atoms), jnp.bfloat16)


def across(row, count):
    return jnp.transpose(jnp.broadcast_to(row, (count, row.shape[1])))


def build(slots, bases, offs_ref, counts_ref, place_ref, blocks, kern_ref, proj_ref):
    atoms = offs_ref.shape[2]
    rate = 2.0 * GAMMA / (bases - 1)
    occ = occupied(counts_ref, atoms)
    own = [across(jnp.where(occ, offs_ref[c], FAR), atoms) for c in range(3)]
    turn = [None if axis is None else 1 - 2 * (place_ref[axis] & 1) for axis in (0, None, 1)]
    for s, steps in enumerate(slots):
        block = blocks[s]
        proj_ref[s * atoms : (s + 1) * atoms, :] = block[:atoms, :]
        coded = block[atoms:, :atoms].astype(jnp.float32)
        apart = []
        for c in range(3):
            spot = coded[c : c + 1, :] + coded[3 + c : 4 + c, :] + coded[6 + c : 7 + c, :]
            step = steps[c]
            if step is None:
                away = spot - own[c]
                apart.append(away + jnp.where(away < 0.0, EDGE, -EDGE))
            elif step == 0:
                apart.append(spot - own[c])
            elif isinstance(step, str):
                apart.append((spot + (turn[c] * int(step)).astype(jnp.float32) * EDGE) - own[c])
            else:
                apart.append((spot + step * EDGE) - own[c])
        ratio = (apart[0] * apart[0] + apart[1] * apart[1] + apart[2] * apart[2]) * (
            1.0 / (CUT * CUT)
        )
        ratio = jnp.minimum(ratio, 1.0)
        if steps == (0, 0, 0):
            same = lax.broadcasted_iota(jnp.int32, (atoms, atoms), 0) == lax.broadcasted_iota(
                jnp.int32, (atoms, atoms), 1
            )
            ratio = jnp.where(same, 1.0, ratio)
        envelope = jnp.square(1.0 - ratio)
        value = envelope * jnp.exp(-GAMMA * jnp.square(ratio))
        growth = jnp.exp(rate * ratio)
        lanes = slice(s * atoms, (s + 1) * atoms)
        for b in range(bases):
            kern_ref[b * atoms : (b + 1) * atoms, lanes] = value.astype(jnp.bfloat16)
            if b + 1 < bases:
                value = value * growth
        envelope = envelope * (1.0 / CUT)
        for c in range(3):
            kern_ref[(bases + c) * atoms : (bases + c + 1) * atoms, lanes] = (
                envelope * apart[c]
            ).astype(jnp.bfloat16)


def gather(kern_ref, proj_ref):
    rows = kern_ref.shape[0] // 3
    return [
        jnp.dot(kern_ref[m * rows : (m + 1) * rows, :], proj_ref[...], preferred_element_type=jnp.float32)
        for m in range(3)
    ]


def scatter(right, kern_ref, held_ref, other_refs):
    atoms = held_ref.shape[2]
    ways = 1 + len(other_refs)
    for k in range(held_ref.shape[0]):
        lanes = slice(k * ways * atoms, (k + 1) * ways * atoms)
        back = lax.dot_general(
            right, kern_ref[:, lanes], (((0,), (0,)), ((), ())), preferred_element_type=jnp.float32
        )
        held_ref[k] = back[:, :atoms]
        for way, ref in enumerate(other_refs):
            ref[k] = back[:, (way + 1) * atoms : (way + 2) * atoms].astype(jnp.bfloat16)


def pick(refs, count, ways):
    return [refs[way].at[k] for k in range(count) for way in range(ways)]


def early_kernel(slots, ways, bases, offs_ref, counts_ref, place_ref, *refs):
    near, (kern_ref, msg_ref, proj_ref) = refs[:ways], refs[ways:]
    blocks = pick(near, len(slots) // ways, ways)
    build(slots, bases, offs_ref, counts_ref, place_ref, blocks, kern_ref, proj_ref)
    rows = kern_ref.shape[0] // 3
    for m, part in enumerate(gather(kern_ref, proj_ref)):
        msg_ref[m * rows : (m + 1) * rows, :] = part


def main_kernel(slots, ways, bases, early, offs_ref, counts_ref, place_ref, mask_ref, targ_ref, radial_ref, readout_ref, *refs):
    near, refs = refs[:ways], refs[ways:]
    if early:
        before_ref, pred_ref, right_ref, held_ref = refs[:4]
        refs = refs[4:]
    else:
        pred_ref, held_ref = refs[:2]
        refs = refs[2:]
    others, (kern_ref, proj_ref) = refs[: ways - 1], refs[ways - 1 :]
    atoms = offs_ref.shape[2]
    width = radial_ref.shape[1]
    blocks = pick(near, len(slots) // ways, ways)
    build(slots, bases, offs_ref, counts_ref, place_ref, blocks, kern_ref, proj_ref)
    msg = jnp.concatenate(gather(kern_ref, proj_ref), 0)
    if early:
        msg = msg + before_ref[...]
    fold = [math.exp(-GAMMA * (b / (bases - 1)) ** 2) for b in range(bases)]
    weight = [radial_ref[b : b + 1, :] * fold[b] for b in range(bases)]
    pre = weight[0] * msg[:atoms]
    for b in range(1, bases):
        pre = pre + weight[b] * msg[b * atoms : (b + 1) * atoms]
    gate = 1.0 / (1.0 + jnp.exp(-pre))
    readout = readout_ref[...]
    gates = readout * gate
    vec = [msg[(bases + c) * atoms : (bases + c + 1) * atoms] for c in range(3)]
    chosen = jnp.where(occupied(counts_ref, atoms), mask_ref[...].astype(jnp.float32), 0.0)
    lean = jnp.zeros((atoms, width), jnp.float32)
    sides = []
    for c in range(3):
        pred = jnp.sum(gates * vec[c], axis=1, keepdims=True)
        pred = jnp.transpose(jnp.broadcast_to(pred, (atoms, atoms)))[0:1, :]
        pred_ref[c] = pred
        err = across(LOSS_WEIGHT * chosen * (pred - targ_ref[c]), width)
        lean = lean + err * vec[c]
        sides.append((err * gates).astype(jnp.bfloat16))
    slope = lean * readout * gate * (1.0 - gate)
    right = jnp.concatenate([(weight[b] * slope).astype(jnp.bfloat16) for b in range(bases)] + sides, 0)
    if early:
        right_ref[...] = right
    scatter(right, kern_ref, held_ref, others)


def late_kernel(right_ref, kern_ref, held_ref, *other_refs):
    scatter(right_ref[...], kern_ref, held_ref, other_refs)


VMEM = pl.BlockSpec(memory_space=pltpu.VMEM)
SMEM = pl.BlockSpec(memory_space=pltpu.SMEM)
LIMIT = pltpu.CompilerParams(vmem_limit_bytes=40 * 1024 * 1024)


def struct(*shape, dtype=jnp.bfloat16):
    return jax.ShapeDtypeStruct(shape, dtype)


def products(count, ways, width, atoms):
    return [struct(count, width, atoms, dtype=jnp.float32)] + [struct(count, width, atoms)] * (ways - 1)


def call_early(slots, ways, bases, common, near):
    atoms, width = near[0].shape[1] - TAIL, near[0].shape[2]
    rows, columns = (bases + 3) * atoms, len(slots) * atoms
    return pl.pallas_call(
        functools.partial(early_kernel, slots, ways, bases),
        out_shape=[struct(rows, columns), struct(rows, width, dtype=jnp.float32)],
        in_specs=[VMEM, SMEM, SMEM] + [VMEM] * ways,
        out_specs=[VMEM] * 2,
        scratch_shapes=[pltpu.VMEM((columns, width), jnp.bfloat16)],
        compiler_params=LIMIT,
        cost_estimate=pl.CostEstimate(
            flops=2 * rows * columns * width, bytes_accessed=2 * rows * columns, transcendentals=2 * atoms * columns
        ),
        name="early",
    )(*common, *near)


def call_main(slots, ways, bases, common, readouts, near, before=None):
    atoms, width = near[0].shape[1] - TAIL, near[0].shape[2]
    rows, columns = (bases + 3) * atoms, len(slots) * atoms
    early = [] if before is None else [before]
    out_shape = [struct(3, 1, atoms, dtype=jnp.float32)]
    if early:
        out_shape.append(struct(rows, width))
    out_shape += products(len(slots) // ways, ways, width, atoms)
    return pl.pallas_call(
        functools.partial(main_kernel, slots, ways, bases, bool(early)),
        out_shape=out_shape,
        in_specs=[VMEM, SMEM, SMEM] + [VMEM] * (len(readouts) + ways + len(early)),
        out_specs=[VMEM] * len(out_shape),
        scratch_shapes=[pltpu.VMEM((rows, columns), jnp.bfloat16), pltpu.VMEM((columns, width), jnp.bfloat16)],
        compiler_params=LIMIT,
        name="main",
    )(*common, *readouts, *near, *early)


def call_late(right, kern, ways, atoms):
    rows, width = right.shape
    columns = kern.shape[1]
    out_shape = products(columns // (ways * atoms), ways, width, atoms)
    return pl.pallas_call(
        late_kernel,
        out_shape=out_shape,
        in_specs=[VMEM] * 2,
        out_specs=[VMEM] * len(out_shape),
        compiler_params=LIMIT,
        cost_estimate=pl.CostEstimate(flops=2 * rows * columns * width, bytes_accessed=2 * rows * columns, transcendentals=0),
        name="late",
    )(right, kern)


AXES = ("gx", "gy", "gz")


def swap(block, axis, flip):
    sizes = [lax.axis_size(a) for a in AXES]
    pairs = []
    for place in itertools.product(*(range(n) for n in sizes)):
        other = [p ^ flip if a == axis else p for a, p in zip(AXES, place)]
        other[1] = other[1] ^ 1
        pairs.append(tuple((q[0] * sizes[1] + q[1]) * sizes[2] + q[2] for q in (place, other)))
    return lax.ppermute(block, AXES, pairs)


def core(block):
    return lax.ppermute(block, "gy", [(0, 1), (1, 0)])


def narrow(block):
    return block.astype(jnp.bfloat16)


def exchange_small(message, bases, common, readouts):
    atoms = message.shape[0] - TAIL
    x1 = swap(message, "gx", 1)
    z1 = swap(message, "gz", 1)
    z3 = swap(message, "gz", 3)
    x3 = swap(x1, "gx", 2)
    x1z1 = swap(z1, "gx", 1)
    x3z1 = swap(x1z1, "gx", 2)
    x1z3 = swap(z3, "gx", 1)
    x3z3 = swap(x1z3, "gx", 2)
    near = jnp.stack([message, x1, x3, z1, z3])
    near_other = core(near)
    far = jnp.stack([x1z1, x3z1, x1z3, x3z3])
    far_other = core(far)

    def both(x, z, hops):
        held, other = (0, None) if hops % 2 == 0 else (None, 0)
        return [(x, held, z), (x, other, z)]

    near_slots = both(0, 0, 0) + both("1", 0, 1) + both("-1", 0, 2) + both(0, "1", 1) + both(0, "-1", 1)
    far_slots = both("1", "1", 2) + both("-1", "1", 3) + both("1", "-1", 2) + both("-1", "-1", 3)
    kern, before = call_early(near_slots, 2, bases, common, [near, near_other])
    pred, right, far_held, far_sent = call_main(far_slots, 2, bases, common, readouts, [far, far_other], before)
    far_sum = far_held + core(far_sent)
    near_held, near_sent = call_late(right, kern, 2, atoms)
    near_sum = near_held + core(near_sent)
    back3 = swap(narrow(far_sum[3]), "gx", 2)
    back1 = swap(narrow(far_sum[1]), "gx", 2)
    back3 = swap(narrow(far_sum[2] + back3), "gx", 1)
    back1 = swap(narrow(far_sum[0] + back1), "gx", 1)
    back0 = swap(narrow(near_sum[2]), "gx", 2)
    back3 = swap(narrow(near_sum[4] + back3), "gz", 3)
    back1 = swap(narrow(near_sum[3] + back1), "gz", 1)
    back0 = swap(narrow(near_sum[1] + back0), "gx", 1)
    return pred, near_sum[0] + back0 + back1 + back3


def exchange_any(message, bases, common, readouts):
    steps_x, steps_y, steps_z = (steps_of(lax.axis_size(a)) for a in AXES)
    near = jnp.concatenate(spread(message[None], "gz"), 0)
    near = jnp.concatenate(spread(near, "gx"), 0)
    near = spread(near, "gy")
    slots = [(x, y, z) for x, z, y in itertools.product(steps_x, steps_z, steps_y)]
    pred, *parts = call_main(slots, len(near), bases, common, readouts, near)
    back = collect(parts, "gy")
    back = back.reshape(len(steps_x), len(steps_z), *back.shape[1:])
    back = collect([back[0]] + [narrow(back[k]) for k in range(1, len(steps_x))], "gx")
    return pred, collect([back[0]] + [narrow(back[k]) for k in range(1, len(steps_z))], "gz")


def on_device(offsets, features, counts, mask, targets, w_in, radial, readout):
    atoms = features.shape[3]
    width = features.shape[4]
    bases = radial.shape[0]
    offs = offsets.reshape(3, 1, atoms)
    count = counts.reshape(1)
    place = jnp.stack([lax.axis_index("gx"), lax.axis_index("gz")]).astype(jnp.int32)
    message = pl.pallas_call(
        message_kernel,
        out_shape=struct(atoms + TAIL, width),
        in_specs=[VMEM, VMEM, VMEM, SMEM],
        out_specs=VMEM,
        name="message",
    )(features[0, 0, 0], w_in, offs, count)
    common = [offs, count, place]
    readouts = [mask.reshape(1, atoms), targets.reshape(3, 1, atoms), radial, readout[None, :]]
    small = tuple(lax.axis_size(a) for a in AXES) == (4, 2, 4)
    pred, back = (exchange_small if small else exchange_any)(message, bases, common, readouts)
    grad = lax.dot_general(
        narrow(back), w_in, (((0,), (1,)), ((), ())), preferred_element_type=jnp.float32
    )
    return (pred.reshape(1, 1, 1, 3, atoms), grad.reshape(1, 1, 1, atoms, width))


def solution(mesh):
    in_specs = (
        P("gx", "gy", "gz", None, None),
        P("gx", "gy", "gz", None, None),
        P("gx", "gy", "gz"),
        P("gx", "gy", "gz", None),
        P("gx", "gy", "gz", None, None),
        P(),
        P(),
        P(),
    )
    out_specs = (P("gx", "gy", "gz", None, None), P("gx", "gy", "gz", None, None))
    return jax.shard_map(
        on_device, mesh=mesh, in_specs=in_specs, out_specs=out_specs, check_vma=False
    )
```

time: 59.2 us -> 52.7 us (0.89)
  waiting for transfers between devices: 30.8 us -> 18.7 us
  starting transfers between devices: 12 us -> 20.4 us
  local copies, waits for them, and re-layouts: 3.56 us -> 1.71 us
    ppermute x10 -> x20, waiting for transfers between devices: 30.8 us -> 18.7 us  [the longest x16 18.7 us: swap(): return lax.ppermute(block, AXES, pairs)]
    ppermute x10 -> x20, starting transfers between devices: 12 us -> 20.4 us  [the longest x16 19.2 us: swap(): return lax.ppermute(block, AXES, pairs)]
    unnamed x25 -> x16, local copies, waits for them, and re-layouts: 3.5 us -> 1.68 us
    pallas_call x2 -> x4, Pallas kernels: 9.55 us -> 8.96 us  [the longest x1 3.82 us: call_main(): pl.pallas_call(functools.partial(main_kernel, slots, ways, bases, bool(ea...]
  transfers between devices with their start and end apart: 10 -> 20, of which waited for: 9 -> 14; matrix products, arithmetic and copies ran while one was open for 3% -> 2% of each run, Pallas kernels for 0% -> 7%
where the time goes in v2:
time: 52.7 us; the launch traced here: 52.5 us
  starting transfers between devices  20.4 us (39%)
  waiting for transfers between devices  18.7 us (35%)
  Pallas kernels  8.96 us (17%)
  local copies, waits for them, and re-layouts  1.71 us (3%)
  between operations  1.49 us (3%)
  matrix products  0.87 us (2%)
    ppermute x16, starting transfers between devices, swap(): return lax.ppermute(block, AXES, pairs)  19.2 us
    ppermute x16, waiting for transfers between devices, swap(): return lax.ppermute(block, AXES, pairs)  18.7 us
    pallas_call x1, Pallas kernels, call_main(): pl.pallas_call(functools.partial(main_kernel, slots, ways, bases, bool(ea...  3.82 us
    pallas_call x1, Pallas kernels, call_early(): pl.pallas_call(functools.partial(early_kernel, slots, ways, bases), out_s...  2.38 us
    pallas_call x1, Pallas kernels, on_device(): pl.pallas_call(message_kernel, out_shape=struct(atoms + TAIL, width), in_...  1.71 us
    unnamed x16, local copies, waits for them, and re-layouts  1.68 us
    ppermute x4, starting transfers between devices, core(): return lax.ppermute(block, 'gy', [(0, 1), (1, 0)])  1.28 us
    pallas_call x1, Pallas kernels, call_late(): pl.pallas_call(late_kernel, out_shape=out_shape, in_specs=[VMEM] * 2, out...  1.06 us
  transfers between devices with their start and end apart: 20, of which 14 were waited for; matrix products, arithmetic and copies ran while one was open for 2% of the time, Pallas kernels for 7%

profile of v2, /device:TPU:0, one launch (start us, length us, event | category | flops | bytes accessed | tf_op | source)
XLA Modules:
  0.0 52.5 jit_solution(3045252364585308488)
XLA Ops:
  1.3 1.7 %message.1 = bf16[144,256]{1,0:T(8,128)(2,1)} custom-call(bf16[128,256]{1,0:T(8,128)(2,1)} %bitcast.88, bf16[256,256]{1,0:T(8,128)(2,1)} %w_ref.1, f32[3,1,128]{2,1,0:T(1,128)} %bitcast.78, s32[1]{0:T(128)} %bitcast.75.counts_ref), custom_call_target="tpu_custom_call" | custom-call | tf_op jit(solution)/shard_map/message/pallas_call | solution.py:344
  3.1 2.4 %collective-permute-start.7 = (bf16[144,256]{1,0:T(8,128)(2,1)}, bf16[144,256]{1,0:T(8,128)(2,1)S(1)}, u32[]{:S(2)}, u32[]{:S(2)}) collective-permute-start(bf16[144,256]{1,0:T(8,128)(2,1)} %message.1), channel_id=1, source_target_pairs={{0,12},{1,13},{2,14},{3,15},{4,8},{5,9},{6,10},{7,11},{8,4},{9,5},... | collective-permute-start | bytes 221192 | tf_op jit(solution)/shard_map/ppermute | solution.py:276
  5.4 3.9 %collective-permute-start.3 = (bf16[144,256]{1,0:T(8,128)(2,1)}, bf16[144,256]{1,0:T(8,128)(2,1)S(1)}, u32[]{:S(2)}, u32[]{:S(2)}) collective-permute-start(bf16[144,256]{1,0:T(8,128)(2,1)} %message.1), channel_id=1, source_target_pairs={{0,7},{1,6},{2,5},{3,4},{4,3},{5,2},{6,1},{7,0},{8,15},{9,14},{10,... | collective-permute-start | bytes 221192 | tf_op jit(solution)/shard_map/ppermute | solution.py:276
  9.3 1.0 %bitcast_dynamic-update-slice_fusion.4 = bf16[5,144,256]{2,1,0:T(8,128)(2,1)S(1)} fusion(bf16[144,256]{1,0:T(8,128)(2,1)} %message.1), kind=kLoop, calls=%fused_computation.29 | loop fusion | bytes 147456
  10.3 1.0 %collective-permute-start.8 = (bf16[144,256]{1,0:T(8,128)(2,1)S(1)}, bf16[144,256]{1,0:T(8,128)(2,1)S(1)}, u32[]{:S(2)}, u32[]{:S(2)}) collective-permute-start(bf16[144,256]{1,0:T(8,128)(2,1)S(1)} %collective-permute-done.7), channel_id=1, source_target_pairs={{0,20},{1,21},{2,22},{3,23},{4,16},{5,17},{6,18},{7,19},{8,28},{9,... | collective-permute-start | bytes 221192 | tf_op jit(solution)/shard_map/ppermute | solution.py:276
  11.3 0.9 %collective-permute-done.3 = bf16[144,256]{1,0:T(8,128)(2,1)S(1)} collective-permute-done((bf16[144,256]{1,0:T(8,128)(2,1)}, bf16[144,256]{1,0:T(8,128)(2,1)S(1)}, u32[]{:S(2)}, u32[]{:S(2)}) %collective-permute-start.3) | collective-permute-done | bytes 73760 | tf_op jit(solution)/shard_map/ppermute | solution.py:276
  12.2 0.4 collective-permute-start.4
  12.6 1.6 %collective-permute-done = bf16[144,256]{1,0:T(8,128)(2,1)S(1)} collective-permute-done((bf16[144,256]{1,0:T(8,128)(2,1)}, bf16[144,256]{1,0:T(8,128)(2,1)S(1)}, u32[]{:S(2)}, u32[]{:S(2)}) %collective-permute-start) | collective-permute-done | bytes 73760 | tf_op jit(solution)/shard_map/ppermute | solution.py:276
  14.4 1.9 %collective-permute-done.4 = bf16[144,256]{1,0:T(8,128)(2,1)S(1)} collective-permute-done((bf16[144,256]{1,0:T(8,128)(2,1)S(1)}, bf16[144,256]{1,0:T(8,128)(2,1)S(1)}, u32[]{:S(2)}, u32[]{:S(2)}) %collective-permute-start.4) | collective-permute-done | bytes 73760 | tf_op jit(solution)/shard_map/ppermute | solution.py:276
  16.2 1.5 %collective-permute-start.5 = (bf16[144,256]{1,0:T(8,128)(2,1)S(1)}, bf16[144,256]{1,0:T(8,128)(2,1)S(1)}, u32[]{:S(2)}, u32[]{:S(2)}) collective-permute-start(bf16[144,256]{1,0:T(8,128)(2,1)S(1)} %collective-permute-done.4), channel_id=1, source_target_pairs={{0,20},{1,21},{2,22},{3,23},{4,16},{5,17},{6,18},{7,19},{8,28},{9,... | collective-permute-start | bytes 221192 | tf_op jit(solution)/shard_map/ppermute | solution.py:276
  17.7 0.8 %collective-permute-done.1 = bf16[144,256]{1,0:T(8,128)(2,1)S(1)} collective-permute-done((bf16[144,256]{1,0:T(8,128)(2,1)S(1)}, bf16[144,256]{1,0:T(8,128)(2,1)S(1)}, u32[]{:S(2)}, u32[]{:S(2)}) %collective-permute-start.1) | collective-permute-done | bytes 73760 | tf_op jit(solution)/shard_map/ppermute | solution.py:276
  18.5 1.3 %collective-permute-start.2 = (bf16[144,256]{1,0:T(8,128)(2,1)S(1)}, bf16[144,256]{1,0:T(8,128)(2,1)S(1)}, u32[]{:S(2)}, u32[]{:S(2)}) collective-permute-start(bf16[144,256]{1,0:T(8,128)(2,1)S(1)} %collective-permute-done.1), channel_id=1, source_target_pairs={{0,20},{1,21},{2,22},{3,23},{4,16},{5,17},{6,18},{7,19},{8,28},{9,... | collective-permute-start | bytes 221192 | tf_op jit(solution)/shard_map/ppermute | solution.py:276
  19.8 0.4 collective-permute-start.9
  20.3 2.4 %collective-permute-done.2 = bf16[144,256]{1,0:T(8,128)(2,1)S(1)} collective-permute-done((bf16[144,256]{1,0:T(8,128)(2,1)S(1)}, bf16[144,256]{1,0:T(8,128)(2,1)S(1)}, u32[]{:S(2)}, u32[]{:S(2)}) %collective-permute-start.2) | collective-permute-done | bytes 73760 | tf_op jit(solution)/shard_map/ppermute | solution.py:276
  23.1 0.7 %copy-done.1 = f32[1,1,1,3,128]{4,2,3,1,0:T(1,128)S(1)} copy-done((f32[1,1,1,3,128]{4,2,3,1,0:T(1,128)S(1)}, f32[1,1,1,3,128]{4,2,3,1,0:T(1,128)}, u32[]{:S(2)}) %copy-start.1) | copy-done | bytes 1560
  23.8 2.4 %early.1 = (bf16[1152,1280]{1,0:T(8,128)(2,1)S(1)}, f32[1152,256]{1,0:T(8,128)S(1)}) custom-call(f32[3,1,128]{2,1,0:T(1,128)S(1)} %bitcast.79, s32[1]{0:T(128)} %bitcast.76.counts_ref, s32[2]{0:T(128)S(1)} %pad_add_fusion.place_ref, bf16[5,144,256]{2,1,0:T(8,128)(2,1)S(1)} %bitcast_dynamic-update-slice_fusion.refs_0_, ...), custom_call_target="tpu_custom_call" | custom-call | flops 754974720 | bytes 2949120 | tf_op jit(solution)/shard_map/early/pallas_call | solution.py:218
  26.2 3.8 %main.1 = (f32[3,1,128]{2,1,0:T(1,128)}, bf16[1152,256]{1,0:T(8,128)(2,1)S(1)}, f32[4,256,128]{2,1,0:T(8,128)S(1)}, bf16[4,256,128]{2,1,0:T(8,128)(2,1)S(1)}) custom-call(f32[3,1,128]{2,1,0:T(1,128)S(1)} %bitcast.80, s32[1]{0:T(128)} %bitcast.77.counts_ref, s32[2]{0:T(128)S(1)} %pad_add_fusion.place_ref, s32[1,128]{1,0:T(1,128)S(1)} %bitcast.83, ...), custom_call_target="tpu_custom_call" | custom-call | tf_op jit(solution)/shard_map/main/pallas_call | solution.py:240
  30.0 0.4 collective-permute-start.13
  30.5 1.1 %late.1 = (f32[5,256,128]{2,1,0:T(8,128)S(1)}, bf16[5,256,128]{2,1,0:T(8,128)(2,1)S(1)}) custom-call(bf16[1152,256]{1,0:T(8,128)(2,1)S(1)} %get-tuple-element.12.right_ref, bf16[1152,1280]{1,0:T(8,128)(2,1)S(1)} %get-tuple-element.13.kern_ref), custom_call_target="tpu_custom_call" | custom-call | flops 754974720 | bytes 2949120 | tf_op jit(solution)/shard_map/late/pallas_call | solution.py:255
  31.8 1.6 %collective-permute-start.14 = (bf16[256,128]{1,0:T(8,128)(2,1)S(1)}, bf16[256,128]{1,0:T(8,128)(2,1)S(1)}, u32[]{:S(2)}, u32[]{:S(2)}) collective-permute-start(bf16[256,128]{1,0:T(8,128)(2,1)S(1)} %get-tuple-element.27), channel_id=1, source_target_pairs={{0,20},{1,21},{2,22},{3,23},{4,16},{5,17},{6,18},{7,19},{8,28},{9,... | collective-permute-start | bytes 196616 | tf_op jit(solution)/shard_map/ppermute | solution.py:276
  33.7 2.2 %collective-permute-done.14 = bf16[256,128]{1,0:T(8,128)(2,1)S(1)} collective-permute-done((bf16[256,128]{1,0:T(8,128)(2,1)S(1)}, bf16[256,128]{1,0:T(8,128)(2,1)S(1)}, u32[]{:S(2)}, u32[]{:S(2)}) %collective-permute-start.14) | collective-permute-done | bytes 65568 | tf_op jit(solution)/shard_map/ppermute | solution.py:276
  35.8 1.6 %collective-permute-done.17 = bf16[256,128]{1,0:T(8,128)(2,1)S(1)} collective-permute-done((bf16[256,128]{1,0:T(8,128)(2,1)S(1)}, bf16[256,128]{1,0:T(8,128)(2,1)S(1)}, u32[]{:S(2)}, u32[]{:S(2)}) %collective-permute-start.17) | collective-permute-done | bytes 65568 | tf_op jit(solution)/shard_map/ppermute | solution.py:276
  37.8 1.5 %collective-permute-start.18 = (bf16[256,128]{1,0:T(8,128)(2,1)S(1)}, bf16[256,128]{1,0:T(8,128)(2,1)S(1)}, u32[]{:S(2)}, u32[]{:S(2)}) collective-permute-start(bf16[256,128]{1,0:T(8,128)(2,1)S(1)} %get-tuple-element.26), channel_id=1, source_target_pairs={{0,12},{1,13},{2,14},{3,15},{4,8},{5,9},{6,10},{7,11},{8,4},{9,5},... | collective-permute-start | bytes 196616 | tf_op jit(solution)/shard_map/ppermute | solution.py:276
  39.4 1.3 %collective-permute-start.11 = (bf16[256,128]{1,0:T(8,128)(2,1)S(1)}, bf16[256,128]{1,0:T(8,128)(2,1)S(1)}, u32[]{:S(2)}, u32[]{:S(2)}) collective-permute-start(bf16[256,128]{1,0:T(8,128)(2,1)S(1)} %fusion.15), channel_id=1, source_target_pairs={{0,20},{1,21},{2,22},{3,23},{4,16},{5,17},{6,18},{7,19},{8,28},{9,... | collective-permute-start | bytes 196616 | tf_op jit(solution)/shard_map/ppermute | solution.py:276
  40.7 1.0 %collective-permute-done.15 = bf16[256,128]{1,0:T(8,128)(2,1)S(1)} collective-permute-done((bf16[256,128]{1,0:T(8,128)(2,1)S(1)}, bf16[256,128]{1,0:T(8,128)(2,1)S(1)}, u32[]{:S(2)}, u32[]{:S(2)}) %collective-permute-start.15) | collective-permute-done | bytes 65568 | tf_op jit(solution)/shard_map/ppermute | solution.py:276
  41.6 1.4 %collective-permute-done.18 = bf16[256,128]{1,0:T(8,128)(2,1)S(1)} collective-permute-done((bf16[256,128]{1,0:T(8,128)(2,1)S(1)}, bf16[256,128]{1,0:T(8,128)(2,1)S(1)}, u32[]{:S(2)}, u32[]{:S(2)}) %collective-permute-start.18) | collective-permute-done | bytes 65568 | tf_op jit(solution)/shard_map/ppermute | solution.py:276
  43.0 0.5 collective-permute-done.11
  43.9 3.4 %collective-permute-start.19 = (bf16[256,128]{1,0:T(8,128)(2,1)S(1)}, bf16[256,128]{1,0:T(8,128)(2,1)S(1)}, u32[]{:S(2)}, u32[]{:S(2)}) collective-permute-start(bf16[256,128]{1,0:T(8,128)(2,1)S(1)} %get-tuple-element.23), channel_id=1, source_target_pairs={{0,7},{1,6},{2,5},{3,4},{4,3},{5,2},{6,1},{7,0},{8,15},{9,14},{10,... | collective-permute-start | bytes 196616 | tf_op jit(solution)/shard_map/ppermute | solution.py:276
  47.3 0.5 collective-permute-done.12
  47.8 1.9 %collective-permute-done.19 = bf16[256,128]{1,0:T(8,128)(2,1)S(1)} collective-permute-done((bf16[256,128]{1,0:T(8,128)(2,1)S(1)}, bf16[256,128]{1,0:T(8,128)(2,1)S(1)}, u32[]{:S(2)}, u32[]{:S(2)}) %collective-permute-start.19) | collective-permute-done | bytes 65568 | tf_op jit(solution)/shard_map/ppermute | solution.py:276
  49.7 1.9 %collective-permute-done.16 = bf16[256,128]{1,0:T(8,128)(2,1)S(1)} collective-permute-done((bf16[256,128]{1,0:T(8,128)(2,1)S(1)}, bf16[256,128]{1,0:T(8,128)(2,1)S(1)}, u32[]{:S(2)}, u32[]{:S(2)}) %collective-permute-start.16) | collective-permute-done | bytes 65568 | tf_op jit(solution)/shard_map/ppermute | solution.py:276
  51.6 0.9 %convolution_bitcast_fusion = f32[1,1,1,128,256]{4,3,2,1,0:T(8,128)} fusion(bf16[256,256]{1,0:T(8,128)(2,1)S(1)} %copy-done.5, f32[5,256,128]{2,1,0:T(8,128)S(1)} %convert_add_fusion, bf16[256,128]{1,0:T(8,128)(2,1)S(1)} %collective-permute-done.19, bf16[256,128]{1,0:T(8,128)(2,1)S(1)} %collective-permute-done.16, bf16[256,128]{1,0:T(8,128)(2,1)S(1)} %collective-permute-done.12), kind=kOutput, calls=%fused_computation | convolution fusion | flops 17006592 | bytes 589824 | tf_op jit(solution)/shard_map/dot_general | solution.py:355
  (38 shorter events, 1.9 us)
Async XLA Ops:
  0.6 25.5 %copy-start.3 = (f32[256]{0:T(256)S(1)}, f32[256]{0:T(256)}, u32[]{:S(2)}) copy-start(f32[256]{0:T(256)} %param.15) | copy-start | bytes 3076
  0.6 25.5 %copy-start = (f32[6,256]{1,0:T(8,128)S(1)}, f32[6,256]{1,0:T(8,128)}, u32[]{:S(2)}) copy-start(f32[6,256]{1,0:T(8,128)} %radial_ref.1) | copy-start | bytes 18436
  0.7 25.5 %copy-start.2 = (f32[1,1,1,3,128]{4,2,3,1,0:T(1,128)S(1)}, f32[1,1,1,3,128]{4,2,3,1,0:T(1,128)}, u32[]{:S(2)}) copy-start(f32[1,1,1,3,128]{4,2,3,1,0:T(1,128)} %param.12) | copy-start | bytes 4612
  0.7 25.5 %copy-start.4 = (s32[1,1,1,128]{3,2,1,0:T(1,128)S(1)}, s32[1,1,1,128]{3,2,1,0:T(1,128)}, u32[]{:S(2)}) copy-start(s32[1,1,1,128]{3,2,1,0:T(1,128)} %param.11) | copy-start | bytes 1540
  3.1 7.2 %collective-permute-start.7 = (bf16[144,256]{1,0:T(8,128)(2,1)}, bf16[144,256]{1,0:T(8,128)(2,1)S(1)}, u32[]{:S(2)}, u32[]{:S(2)}) collective-permute-start(bf16[144,256]{1,0:T(8,128)(2,1)} %message.1), channel_id=1, source_target_pairs={{0,12},{1,13},{2,14},{3,15},{4,8},{5,9},{6,10},{7,11},{8,4},{9,5},... | collective-permute-start | bytes 221192 | tf_op jit(solution)/shard_map/ppermute | solution.py:276
  5.4 6.8 %collective-permute-start.3 = (bf16[144,256]{1,0:T(8,128)(2,1)}, bf16[144,256]{1,0:T(8,128)(2,1)S(1)}, u32[]{:S(2)}, u32[]{:S(2)}) collective-permute-start(bf16[144,256]{1,0:T(8,128)(2,1)} %message.1), channel_id=1, source_target_pairs={{0,7},{1,6},{2,5},{3,4},{4,3},{5,2},{6,1},{7,0},{8,15},{9,14},{10,... | collective-permute-start | bytes 221192 | tf_op jit(solution)/shard_map/ppermute | solution.py:276
  9.3 4.9 %collective-permute-start = (bf16[144,256]{1,0:T(8,128)(2,1)}, bf16[144,256]{1,0:T(8,128)(2,1)S(1)}, u32[]{:S(2)}, u32[]{:S(2)}) collective-permute-start(bf16[144,256]{1,0:T(8,128)(2,1)} %message.1), channel_id=1, source_target_pairs={{0,5},{1,4},{2,7},{3,6},{4,1},{5,0},{6,3},{7,2},{8,13},{9,12},{10,... | collective-permute-start | bytes 221192 | tf_op jit(solution)/shard_map/ppermute | solution.py:276
  10.3 9.5 %collective-permute-start.8 = (bf16[144,256]{1,0:T(8,128)(2,1)S(1)}, bf16[144,256]{1,0:T(8,128)(2,1)S(1)}, u32[]{:S(2)}, u32[]{:S(2)}) collective-permute-start(bf16[144,256]{1,0:T(8,128)(2,1)S(1)} %collective-permute-done.7), channel_id=1, source_target_pairs={{0,20},{1,21},{2,22},{3,23},{4,16},{5,17},{6,18},{7,19},{8,28},{9,... | collective-permute-start | bytes 221192 | tf_op jit(solution)/shard_map/ppermute | solution.py:276
  12.2 4.0 %collective-permute-start.4 = (bf16[144,256]{1,0:T(8,128)(2,1)S(1)}, bf16[144,256]{1,0:T(8,128)(2,1)S(1)}, u32[]{:S(2)}, u32[]{:S(2)}) collective-permute-start(bf16[144,256]{1,0:T(8,128)(2,1)S(1)} %collective-permute-done.3), channel_id=1, source_target_pairs={{0,12},{1,13},{2,14},{3,15},{4,8},{5,9},{6,10},{7,11},{8,4},{9,5},... | collective-permute-start | bytes 221192 | tf_op jit(solution)/shard_map/ppermute | solution.py:276
  14.2 4.3 %collective-permute-start.1 = (bf16[144,256]{1,0:T(8,128)(2,1)S(1)}, bf16[144,256]{1,0:T(8,128)(2,1)S(1)}, u32[]{:S(2)}, u32[]{:S(2)}) collective-permute-start(bf16[144,256]{1,0:T(8,128)(2,1)S(1)} %collective-permute-done), channel_id=1, source_target_pairs={{0,12},{1,13},{2,14},{3,15},{4,8},{5,9},{6,10},{7,11},{8,4},{9,5},... | collective-permute-start | bytes 221192 | tf_op jit(solution)/shard_map/ppermute | solution.py:276
  16.2 4.1 %collective-permute-start.5 = (bf16[144,256]{1,0:T(8,128)(2,1)S(1)}, bf16[144,256]{1,0:T(8,128)(2,1)S(1)}, u32[]{:S(2)}, u32[]{:S(2)}) collective-permute-start(bf16[144,256]{1,0:T(8,128)(2,1)S(1)} %collective-permute-done.4), channel_id=1, source_target_pairs={{0,20},{1,21},{2,22},{3,23},{4,16},{5,17},{6,18},{7,19},{8,28},{9,... | collective-permute-start | bytes 221192 | tf_op jit(solution)/shard_map/ppermute | solution.py:276
  18.5 4.3 %collective-permute-start.2 = (bf16[144,256]{1,0:T(8,128)(2,1)S(1)}, bf16[144,256]{1,0:T(8,128)(2,1)S(1)}, u32[]{:S(2)}, u32[]{:S(2)}) collective-permute-start(bf16[144,256]{1,0:T(8,128)(2,1)S(1)} %collective-permute-done.1), channel_id=1, source_target_pairs={{0,20},{1,21},{2,22},{3,23},{4,16},{5,17},{6,18},{7,19},{8,28},{9,... | collective-permute-start | bytes 221192 | tf_op jit(solution)/shard_map/ppermute | solution.py:276
  19.8 3.3 %collective-permute-start.9 = (bf16[5,144,256]{2,1,0:T(8,128)(2,1)S(1)}, bf16[5,144,256]{2,1,0:T(8,128)(2,1)S(1)}, u32[]{:S(2)}, u32[]{:S(2)}) collective-permute-start(bf16[5,144,256]{2,1,0:T(8,128)(2,1)S(1)} %bitcast_dynamic-update-slice_fusion.refs_0_), channel_id=1, source_target_pairs={{0,4},{4,0},{1,5},{5,1},{2,6},{6,2},{3,7},{7,3},{8,12},{12,8},{9,1... | collective-permute-start | bytes 1105928 | tf_op jit(solution)/shard_map/ppermute | solution.py:280
  22.8 3.3 %collective-permute-start.6 = (bf16[4,144,256]{2,1,0:T(8,128)(2,1)S(1)}, bf16[4,144,256]{2,1,0:T(8,128)(2,1)S(1)}, u32[]{:S(2)}, u32[]{:S(2)}) collective-permute-start(bf16[4,144,256]{2,1,0:T(8,128)(2,1)S(1)} %pad_maximum_fusion.refs_0_), channel_id=1, source_target_pairs={{0,4},{4,0},{1,5},{5,1},{2,6},{6,2},{3,7},{7,3},{8,12},{12,8},{9,1... | collective-permute-start | bytes 884744 | tf_op jit(solution)/shard_map/ppermute | solution.py:280
  23.1 0.7 %copy-start.1 = (f32[1,1,1,3,128]{4,2,3,1,0:T(1,128)S(1)}, f32[1,1,1,3,128]{4,2,3,1,0:T(1,128)}, u32[]{:S(2)}) copy-start(f32[1,1,1,3,128]{4,2,3,1,0:T(1,128)} %param.8) | copy-start | bytes 4612
  30.0 1.7 %collective-permute-start.13 = (bf16[4,256,128]{2,1,0:T(8,128)(2,1)S(1)}, bf16[4,256,128]{2,1,0:T(8,128)(2,1)S(1)}, u32[]{:S(2)}, u32[]{:S(2)}) collective-permute-start(bf16[4,256,128]{2,1,0:T(8,128)(2,1)S(1)} %get-tuple-element.17), channel_id=1, source_target_pairs={{0,4},{4,0},{1,5},{5,1},{2,6},{6,2},{3,7},{7,3},{8,12},{12,8},{9,1... | collective-permute-start | bytes 786440 | tf_op jit(solution)/shard_map/ppermute | solution.py:280
  31.5 20.1 %copy-start.5 = (bf16[256,256]{1,0:T(8,128)(2,1)S(1)}, bf16[256,256]{1,0:T(8,128)(2,1)}, u32[]{:S(2)}) copy-start(bf16[256,256]{1,0:T(8,128)(2,1)} %w_ref.1) | copy-start | bytes 393220
  31.6 7.8 %collective-permute-start.10 = (bf16[5,256,128]{2,1,0:T(8,128)(2,1)S(1)}, bf16[5,256,128]{2,1,0:T(8,128)(2,1)S(1)}, u32[]{:S(2)}, u32[]{:S(2)}) collective-permute-start(bf16[5,256,128]{2,1,0:T(8,128)(2,1)S(1)} %get-tuple-element.15), channel_id=1, source_target_pairs={{0,4},{4,0},{1,5},{5,1},{2,6},{6,2},{3,7},{7,3},{8,12},{12,8},{9,1... | collective-permute-start | bytes 983048 | tf_op jit(solution)/shard_map/ppermute | solution.py:280
  31.8 4.0 %collective-permute-start.14 = (bf16[256,128]{1,0:T(8,128)(2,1)S(1)}, bf16[256,128]{1,0:T(8,128)(2,1)S(1)}, u32[]{:S(2)}, u32[]{:S(2)}) collective-permute-start(bf16[256,128]{1,0:T(8,128)(2,1)S(1)} %get-tuple-element.27), channel_id=1, source_target_pairs={{0,20},{1,21},{2,22},{3,23},{4,16},{5,17},{6,18},{7,19},{8,28},{9,... | collective-permute-start | bytes 196616 | tf_op jit(solution)/shard_map/ppermute | solution.py:276
  33.4 4.1 %collective-permute-start.17 = (bf16[256,128]{1,0:T(8,128)(2,1)S(1)}, bf16[256,128]{1,0:T(8,128)(2,1)S(1)}, u32[]{:S(2)}, u32[]{:S(2)}) collective-permute-start(bf16[256,128]{1,0:T(8,128)(2,1)S(1)} %get-tuple-element.28), channel_id=1, source_target_pairs={{0,20},{1,21},{2,22},{3,23},{4,16},{5,17},{6,18},{7,19},{8,28},{9,... | collective-permute-start | bytes 196616 | tf_op jit(solution)/shard_map/ppermute | solution.py:276
  37.5 4.1 %collective-permute-start.15 = (bf16[256,128]{1,0:T(8,128)(2,1)S(1)}, bf16[256,128]{1,0:T(8,128)(2,1)S(1)}, u32[]{:S(2)}, u32[]{:S(2)}) collective-permute-start(bf16[256,128]{1,0:T(8,128)(2,1)S(1)} %get-tuple-element.25), channel_id=1, source_target_pairs={{0,12},{1,13},{2,14},{3,15},{4,8},{5,9},{6,10},{7,11},{8,4},{9,5},... | collective-permute-start | bytes 196616 | tf_op jit(solution)/shard_map/ppermute | solution.py:276
  37.8 5.2 %collective-permute-start.18 = (bf16[256,128]{1,0:T(8,128)(2,1)S(1)}, bf16[256,128]{1,0:T(8,128)(2,1)S(1)}, u32[]{:S(2)}, u32[]{:S(2)}) collective-permute-start(bf16[256,128]{1,0:T(8,128)(2,1)S(1)} %get-tuple-element.26), channel_id=1, source_target_pairs={{0,12},{1,13},{2,14},{3,15},{4,8},{5,9},{6,10},{7,11},{8,4},{9,5},... | collective-permute-start | bytes 196616 | tf_op jit(solution)/shard_map/ppermute | solution.py:276
  39.4 4.1 %collective-permute-start.11 = (bf16[256,128]{1,0:T(8,128)(2,1)S(1)}, bf16[256,128]{1,0:T(8,128)(2,1)S(1)}, u32[]{:S(2)}, u32[]{:S(2)}) collective-permute-start(bf16[256,128]{1,0:T(8,128)(2,1)S(1)} %fusion.15), channel_id=1, source_target_pairs={{0,20},{1,21},{2,22},{3,23},{4,16},{5,17},{6,18},{7,19},{8,28},{9,... | collective-permute-start | bytes 196616 | tf_op jit(solution)/shard_map/ppermute | solution.py:276
  43.6 4.2 %collective-permute-start.12 = (bf16[256,128]{1,0:T(8,128)(2,1)S(1)}, bf16[256,128]{1,0:T(8,128)(2,1)S(1)}, u32[]{:S(2)}, u32[]{:S(2)}) collective-permute-start(bf16[256,128]{1,0:T(8,128)(2,1)S(1)} %get-tuple-element.22), channel_id=1, source_target_pairs={{0,12},{1,13},{2,14},{3,15},{4,8},{5,9},{6,10},{7,11},{8,4},{9,5},... | collective-permute-start | bytes 196616 | tf_op jit(solution)/shard_map/ppermute | solution.py:276
  43.9 5.8 %collective-permute-start.19 = (bf16[256,128]{1,0:T(8,128)(2,1)S(1)}, bf16[256,128]{1,0:T(8,128)(2,1)S(1)}, u32[]{:S(2)}, u32[]{:S(2)}) collective-permute-start(bf16[256,128]{1,0:T(8,128)(2,1)S(1)} %get-tuple-element.23), channel_id=1, source_target_pairs={{0,7},{1,6},{2,5},{3,4},{4,3},{5,2},{6,1},{7,0},{8,15},{9,14},{10,... | collective-permute-start | bytes 196616 | tf_op jit(solution)/shard_map/ppermute | solution.py:276
  47.3 4.3 %collective-permute-start.16 = (bf16[256,128]{1,0:T(8,128)(2,1)S(1)}, bf16[256,128]{1,0:T(8,128)(2,1)S(1)}, u32[]{:S(2)}, u32[]{:S(2)}) collective-permute-start(bf16[256,128]{1,0:T(8,128)(2,1)S(1)} %get-tuple-element.24), channel_id=1, source_target_pairs={{0,5},{1,4},{2,7},{3,6},{4,1},{5,0},{6,3},{7,2},{8,13},{9,12},{10,... | collective-permute-start | bytes 196616 | tf_op jit(solution)/shard_map/ppermute | solution.py:276

commit v3 on v2

--- a/solution.py
+++ b/solution.py
@@ -41,7 +41,7 @@
 
 
 def occupied(counts_ref, atoms):
-    return lax.broadcasted_iota(jnp.int32, (1, atoms), 1) < counts_ref[0]
+    return lax.broadcasted_iota(jnp.int32, (1, atoms), 1) < counts_ref[...]
 
 
 def message_kernel(feat_ref, w_ref, offs_ref, counts_ref, out_ref):
@@ -140,21 +140,22 @@
             ref[k] = back[:, (way + 1) * atoms : (way + 2) * atoms].astype(jnp.bfloat16)
 
 
-def pick(refs, count, ways):
-    return [refs[way].at[k] for k in range(count) for way in range(ways)]
+def pick(refs, ways):
+    groups = [refs[g : g + ways] for g in range(0, len(refs), ways)]
+    return [ref.at[k] for group in groups for k in range(group[0].shape[0]) for ref in group]
 
 
 def early_kernel(slots, ways, bases, offs_ref, counts_ref, place_ref, *refs):
-    near, (kern_ref, msg_ref, proj_ref) = refs[:ways], refs[ways:]
-    blocks = pick(near, len(slots) // ways, ways)
+    near, (kern_ref, msg_ref, proj_ref) = refs[:-3], refs[-3:]
+    blocks = pick(near, ways)
     build(slots, bases, offs_ref, counts_ref, place_ref, blocks, kern_ref, proj_ref)
     rows = kern_ref.shape[0] // 3
     for m, part in enumerate(gather(kern_ref, proj_ref)):
         msg_ref[m * rows : (m + 1) * rows, :] = part
 
 
-def main_kernel(slots, ways, bases, early, offs_ref, counts_ref, place_ref, mask_ref, targ_ref, radial_ref, readout_ref, *refs):
-    near, refs = refs[:ways], refs[ways:]
+def main_kernel(slots, ways, bases, arrays, early, offs_ref, counts_ref, place_ref, mask_ref, targ_ref, radial_ref, readout_ref, *refs):
+    near, refs = refs[:arrays], refs[arrays:]
     if early:
         before_ref, pred_ref, right_ref, held_ref = refs[:4]
         refs = refs[4:]
@@ -164,7 +165,7 @@
     others, (kern_ref, proj_ref) = refs[: ways - 1], refs[ways - 1 :]
     atoms = offs_ref.shape[2]
     width = radial_ref.shape[1]
-    blocks = pick(near, len(slots) // ways, ways)
+    blocks = pick(near, ways)
     build(slots, bases, offs_ref, counts_ref, place_ref, blocks, kern_ref, proj_ref)
     msg = jnp.concatenate(gather(kern_ref, proj_ref), 0)
     if early:
@@ -218,12 +219,12 @@
     return pl.pallas_call(
         functools.partial(early_kernel, slots, ways, bases),
         out_shape=[struct(rows, columns), struct(rows, width, dtype=jnp.float32)],
-        in_specs=[VMEM, SMEM, SMEM] + [VMEM] * ways,
+        in_specs=[VMEM, VMEM, SMEM] + [VMEM] * len(near),
         out_specs=[VMEM] * 2,
         scratch_shapes=[pltpu.VMEM((columns, width), jnp.bfloat16)],
         compiler_params=LIMIT,
         cost_estimate=pl.CostEstimate(
-            flops=2 * rows * columns * width, bytes_accessed=2 * rows * columns, transcendentals=2 * atoms * columns
+            flops=10 * rows * columns * width, bytes_accessed=8 * rows * columns, transcendentals=2 * atoms * columns
         ),
         name="early",
     )(*common, *near)
@@ -238,9 +239,9 @@
         out_shape.append(struct(rows, width))
     out_shape += products(len(slots) // ways, ways, width, atoms)
     return pl.pallas_call(
-        functools.partial(main_kernel, slots, ways, bases, bool(early)),
+        functools.partial(main_kernel, slots, ways, bases, len(near), bool(early)),
         out_shape=out_shape,
-        in_specs=[VMEM, SMEM, SMEM] + [VMEM] * (len(readouts) + ways + len(early)),
+        in_specs=[VMEM, VMEM, SMEM] + [VMEM] * (len(readouts) + len(near) + len(early)),
         out_specs=[VMEM] * len(out_shape),
         scratch_shapes=[pltpu.VMEM((rows, columns), jnp.bfloat16), pltpu.VMEM((columns, width), jnp.bfloat16)],
         compiler_params=LIMIT,
@@ -284,6 +285,10 @@
     return block.astype(jnp.bfloat16)
 
 
+def after(block, other):
+    return lax.optimization_barrier((block, other))[0]
+
+
 def exchange_small(message, bases, common, readouts):
     atoms = message.shape[0] - TAIL
     x1 = swap(message, "gx", 1)
@@ -294,10 +299,8 @@
     x3z1 = swap(x1z1, "gx", 2)
     x1z3 = swap(z3, "gx", 1)
     x3z3 = swap(x1z3, "gx", 2)
-    near = jnp.stack([message, x1, x3, z1, z3])
-    near_other = core(near)
-    far = jnp.stack([x1z1, x3z1, x1z3, x3z3])
-    far_other = core(far)
+    near = jnp.stack([x1, x3, z1, z3])
+    near = [message[None], core(message)[None], near, core(near)]
 
     def both(x, z, hops):
         held, other = (0, None) if hops % 2 == 0 else (None, 0)
@@ -305,20 +308,27 @@
 
     near_slots = both(0, 0, 0) + both("1", 0, 1) + both("-1", 0, 2) + both(0, "1", 1) + both(0, "-1", 1)
     far_slots = both("1", "1", 2) + both("-1", "1", 3) + both("1", "-1", 2) + both("-1", "-1", 3)
-    kern, before = call_early(near_slots, 2, bases, common, [near, near_other])
-    pred, right, far_held, far_sent = call_main(far_slots, 2, bases, common, readouts, [far, far_other], before)
+    kern, before = call_early(near_slots, 2, bases, common, near)
+    far1 = jnp.stack([x1z1, x3z1])
+    far = [far1, core(far1)]
+    x1z3, x3z3, _, _ = lax.optimization_barrier((x1z3, x3z3, far[1], before))
+    far3 = jnp.stack([x1z3, x3z3])
+    far += [far3, core(far3)]
+    pred, right, far_held, far_sent = call_main(far_slots, 2, bases, common, readouts, far, before)
     far_sum = far_held + core(far_sent)
     near_held, near_sent = call_late(right, kern, 2, atoms)
     near_sum = near_held + core(near_sent)
     back3 = swap(narrow(far_sum[3]), "gx", 2)
-    back1 = swap(narrow(far_sum[1]), "gx", 2)
-    back3 = swap(narrow(far_sum[2] + back3), "gx", 1)
-    back1 = swap(narrow(far_sum[0] + back1), "gx", 1)
-    back0 = swap(narrow(near_sum[2]), "gx", 2)
-    back3 = swap(narrow(near_sum[4] + back3), "gz", 3)
-    back1 = swap(narrow(near_sum[3] + back1), "gz", 1)
-    back0 = swap(narrow(near_sum[1] + back0), "gx", 1)
-    return pred, near_sum[0] + back0 + back1 + back3
+    back1 = swap(narrow(jnp.stack([far_sum[1], near_sum[2]])), "gx", 2)
+    next3 = narrow(far_sum[2] + back3)
+    next1 = narrow(jnp.stack([far_sum[0], near_sum[1]]) + after(back1, next3))
+    back3 = swap(next3, "gx", 1)
+    back1 = swap(next1, "gx", 1)
+    next3 = narrow(near_sum[4] + back3)
+    back1 = after(back1, next3)
+    next1 = narrow(near_sum[3] + back1[0])
+    back3 = swap(next3, "gz", 3)
+    return pred, near_sum[0] + back1[1] + swap(next1, "gz", 1) + back3
 
 
 def exchange_any(message, bases, common, readouts):
@@ -339,12 +349,12 @@
     width = features.shape[4]
     bases = radial.shape[0]
     offs = offsets.reshape(3, 1, atoms)
-    count = counts.reshape(1)
+    count = counts.reshape(1, 1)
     place = jnp.stack([lax.axis_index("gx"), lax.axis_index("gz")]).astype(jnp.int32)
     message = pl.pallas_call(
         message_kernel,
         out_shape=struct(atoms + TAIL, width),
-        in_specs=[VMEM, VMEM, VMEM, SMEM],
+        in_specs=[VMEM] * 4,
         out_specs=VMEM,
         name="message",
     )(features[0, 0, 0], w_in, offs, count)

time: 52.7 us -> 49 us (0.930)
  waiting for transfers between devices: 18.7 us -> 12.1 us
  starting transfers between devices: 20.4 us -> 23.4 us
    ppermute x16 -> x14, waiting for transfers between devices: 18.7 us -> 10.5 us  [swap(): return lax.ppermute(block, AXES, pairs)]
    ppermute x16 -> x14, starting transfers between devices: 19.2 us -> 21.5 us  [swap(): return lax.ppermute(block, AXES, pairs)]
    ppermute x4 -> x6, waiting for transfers between devices: 0.01 us -> 1.57 us  [core(): return lax.ppermute(block, 'gy', [(0, 1), (1, 0)])]
    ppermute x4 -> x6, starting transfers between devices: 1.28 us -> 1.86 us  [core(): return lax.ppermute(block, 'gy', [(0, 1), (1, 0)])]
  transfers between devices with their start and end apart: 20 -> 20, of which waited for: 14 -> 9; matrix products, arithmetic and copies ran while one was open for 2% -> 1% of each run, Pallas kernels for 7% -> 7%
where the time goes in v3:
time: 49 us; the launch traced here: 48.8 us
  starting transfers between devices  23.4 us (48%)
  waiting for transfers between devices  12.1 us (25%)
  Pallas kernels  8.98 us (18%)
  local copies, waits for them, and re-layouts  1.63 us (3%)
  between operations  1.45 us (3%)
  matrix products  0.87 us (2%)
    ppermute x14, starting transfers between devices, swap(): return lax.ppermute(block, AXES, pairs)  21.5 us
    ppermute x14, waiting for transfers between devices, swap(): return lax.ppermute(block, AXES, pairs)  10.5 us
    pallas_call x1, Pallas kernels, call_main(): pl.pallas_call(functools.partial(main_kernel, slots, ways, bases, len(nea...  3.85 us
    pallas_call x1, Pallas kernels, call_early(): pl.pallas_call(functools.partial(early_kernel, slots, ways, bases), out_s...  2.38 us
    ppermute x6, starting transfers between devices, core(): return lax.ppermute(block, 'gy', [(0, 1), (1, 0)])  1.86 us
    pallas_call x1, Pallas kernels, on_device(): pl.pallas_call(message_kernel, out_shape=struct(atoms + TAIL, width), in_...  1.71 us
    unnamed x16, local copies, waits for them, and re-layouts  1.59 us
    ppermute x6, waiting for transfers between devices, core(): return lax.ppermute(block, 'gy', [(0, 1), (1, 0)])  1.57 us
  transfers between devices with their start and end apart: 20, of which 9 were waited for; matrix products, arithmetic and copies ran while one was open for 1% of the time, Pallas kernels for 7%

profile of v3, /device:TPU:0, one launch (start us, length us, event | category | flops | bytes accessed | tf_op | source)
XLA Modules:
  0.0 48.8 jit_solution(3378539800277820525)
XLA Ops:
  1.3 1.7 %message.1 = bf16[144,256]{1,0:T(8,128)(2,1)} custom-call(bf16[128,256]{1,0:T(8,128)(2,1)} %bitcast.68, bf16[256,256]{1,0:T(8,128)(2,1)} %w_ref.1, f32[3,1,128]{2,1,0:T(1,128)} %bitcast.53, s32[1,1]{1,0:T(1,128)} %bitcast.49.counts_ref), custom_call_target="tpu_custom_call" | custom-call | tf_op jit(solution)/shard_map/message/pallas_call | solution.py:354
  3.0 2.4 %collective-permute-start.8 = (bf16[144,256]{1,0:T(8,128)(2,1)}, bf16[144,256]{1,0:T(8,128)(2,1)S(1)}, u32[]{:S(2)}, u32[]{:S(2)}) collective-permute-start(bf16[144,256]{1,0:T(8,128)(2,1)} %message.1), channel_id=1, source_target_pairs={{0,12},{1,13},{2,14},{3,15},{4,8},{5,9},{6,10},{7,11},{8,4},{9,5},... | collective-permute-start | bytes 221192 | tf_op jit(solution)/shard_map/ppermute | solution.py:277
  5.4 1.9 %collective-permute-start = (bf16[144,256]{1,0:T(8,128)(2,1)}, bf16[144,256]{1,0:T(8,128)(2,1)S(1)}, u32[]{:S(2)}, u32[]{:S(2)}) collective-permute-start(bf16[144,256]{1,0:T(8,128)(2,1)} %message.1), channel_id=1, source_target_pairs={{0,5},{1,4},{2,7},{3,6},{4,1},{5,0},{6,3},{7,2},{8,13},{9,12},{10,... | collective-permute-start | bytes 221192 | tf_op jit(solution)/shard_map/ppermute | solution.py:277
  7.2 2.0 %collective-permute-start.4 = (bf16[144,256]{1,0:T(8,128)(2,1)}, bf16[144,256]{1,0:T(8,128)(2,1)S(1)}, u32[]{:S(2)}, u32[]{:S(2)}) collective-permute-start(bf16[144,256]{1,0:T(8,128)(2,1)} %message.1), channel_id=1, source_target_pairs={{0,7},{1,6},{2,5},{3,4},{4,3},{5,2},{6,1},{7,0},{8,15},{9,14},{10,... | collective-permute-start | bytes 221192 | tf_op jit(solution)/shard_map/ppermute | solution.py:277
  9.3 1.7 %collective-permute-start.9 = (bf16[144,256]{1,0:T(8,128)(2,1)S(1)}, bf16[144,256]{1,0:T(8,128)(2,1)S(1)}, u32[]{:S(2)}, u32[]{:S(2)}) collective-permute-start(bf16[144,256]{1,0:T(8,128)(2,1)S(1)} %collective-permute-done.8), channel_id=1, source_target_pairs={{0,20},{1,21},{2,22},{3,23},{4,16},{5,17},{6,18},{7,19},{8,28},{9,... | collective-permute-start | bytes 221192 | tf_op jit(solution)/shard_map/ppermute | solution.py:277
  10.9 1.0 %collective-permute-start.1 = (bf16[144,256]{1,0:T(8,128)(2,1)S(1)}, bf16[144,256]{1,0:T(8,128)(2,1)S(1)}, u32[]{:S(2)}, u32[]{:S(2)}) collective-permute-start(bf16[144,256]{1,0:T(8,128)(2,1)S(1)} %collective-permute-done), channel_id=1, source_target_pairs={{0,12},{1,13},{2,14},{3,15},{4,8},{5,9},{6,10},{7,11},{8,4},{9,5},... | collective-permute-start | bytes 221192 | tf_op jit(solution)/shard_map/ppermute | solution.py:277
  12.0 1.9 %collective-permute-done.4 = bf16[144,256]{1,0:T(8,128)(2,1)S(1)} collective-permute-done((bf16[144,256]{1,0:T(8,128)(2,1)}, bf16[144,256]{1,0:T(8,128)(2,1)S(1)}, u32[]{:S(2)}, u32[]{:S(2)}) %collective-permute-start.4) | collective-permute-done | bytes 73760 | tf_op jit(solution)/shard_map/ppermute | solution.py:277
  14.0 0.4 collective-permute-start.7
  14.4 1.2 %collective-permute-start.5 = (bf16[144,256]{1,0:T(8,128)(2,1)S(1)}, bf16[144,256]{1,0:T(8,128)(2,1)S(1)}, u32[]{:S(2)}, u32[]{:S(2)}) collective-permute-start(bf16[144,256]{1,0:T(8,128)(2,1)S(1)} %collective-permute-done.4), channel_id=1, source_target_pairs={{0,12},{1,13},{2,14},{3,15},{4,8},{5,9},{6,10},{7,11},{8,4},{9,5},... | collective-permute-start | bytes 221192 | tf_op jit(solution)/shard_map/ppermute | solution.py:277
  15.6 1.2 %collective-permute-start.2 = (bf16[144,256]{1,0:T(8,128)(2,1)S(1)}, bf16[144,256]{1,0:T(8,128)(2,1)S(1)}, u32[]{:S(2)}, u32[]{:S(2)}) collective-permute-start(bf16[144,256]{1,0:T(8,128)(2,1)S(1)} %collective-permute-done.1), channel_id=1, source_target_pairs={{0,20},{1,21},{2,22},{3,23},{4,16},{5,17},{6,18},{7,19},{8,28},{9,... | collective-permute-start | bytes 221192 | tf_op jit(solution)/shard_map/ppermute | solution.py:277
  16.9 1.8 %collective-permute-done.5 = bf16[144,256]{1,0:T(8,128)(2,1)S(1)} collective-permute-done((bf16[144,256]{1,0:T(8,128)(2,1)S(1)}, bf16[144,256]{1,0:T(8,128)(2,1)S(1)}, u32[]{:S(2)}, u32[]{:S(2)}) %collective-permute-start.5) | collective-permute-done | bytes 73760 | tf_op jit(solution)/shard_map/ppermute | solution.py:277
  18.8 1.5 %collective-permute-start.6 = (bf16[144,256]{1,0:T(8,128)(2,1)S(1)}, bf16[144,256]{1,0:T(8,128)(2,1)S(1)}, u32[]{:S(2)}, u32[]{:S(2)}) collective-permute-start(bf16[144,256]{1,0:T(8,128)(2,1)S(1)} %collective-permute-done.5), channel_id=1, source_target_pairs={{0,20},{1,21},{2,22},{3,23},{4,16},{5,17},{6,18},{7,19},{8,28},{9,... | collective-permute-start | bytes 221192 | tf_op jit(solution)/shard_map/ppermute | solution.py:277
  20.4 0.9 %copy-done = bf16[144,256]{1,0:T(8,128)(2,1)S(1)} copy-done((bf16[144,256]{1,0:T(8,128)(2,1)S(1)}, bf16[144,256]{1,0:T(8,128)(2,1)}, u32[]{:S(2)}) %copy-start) | copy-done | bytes 73752
  21.3 0.7 %copy-done.2 = f32[1,1,1,3,128]{4,2,3,1,0:T(1,128)S(1)} copy-done((f32[1,1,1,3,128]{4,2,3,1,0:T(1,128)S(1)}, f32[1,1,1,3,128]{4,2,3,1,0:T(1,128)}, u32[]{:S(2)}) %copy-start.2) | copy-done | bytes 1560
  22.0 2.4 %early.1 = (bf16[1152,1280]{1,0:T(8,128)(2,1)S(1)}, f32[1152,256]{1,0:T(8,128)S(1)}) custom-call(f32[3,1,128]{2,1,0:T(1,128)S(1)} %bitcast.54, s32[1,1]{1,0:T(1,128)} %bitcast.50.counts_ref, s32[2]{0:T(128)S(1)} %pad_add_fusion.place_ref, bf16[1,144,256]{2,1,0:T(8,128)(2,1)S(1)} %bitcast.52, bf16[1,144,256]{2,1,0:T(8,128)(2,1)S(1)} %bitcast.59, ...), custom_call_target="tpu_custom_call" | custom-call | flops 3774873600 | bytes 11796480 | tf_op jit(solution)/shard_map/early/pallas_call | solution.py:219
  24.5 0.5 %collective-permute-start.11 = (bf16[2,144,256]{2,1,0:T(8,128)(2,1)S(1)}, bf16[2,144,256]{2,1,0:T(8,128)(2,1)S(1)}, u32[]{:S(2)}, u32[]{:S(2)}) collective-permute-start(bf16[2,144,256]{2,1,0:T(8,128)(2,1)S(1)} %pad_maximum_fusion.2.refs_2_), channel_id=1, source_target_pairs={{0,4},{4,0},{1,5},{5,1},{2,6},{6,2},{3,7},{7,3},{8,12},{12,8},{9,1... | collective-permute-start | bytes 442376 | tf_op jit(solution)/shard_map/ppermute | solution.py:281
  25.0 1.0 %collective-permute-done.11.refs_3_ = bf16[2,144,256]{2,1,0:T(8,128)(2,1)S(1)} collective-permute-done((bf16[2,144,256]{2,1,0:T(8,128)(2,1)S(1)}, bf16[2,144,256]{2,1,0:T(8,128)(2,1)S(1)}, u32[]{:S(2)}, u32[]{:S(2)}) %collective-permute-start.11) | collective-permute-done | bytes 147488 | tf_op jit(solution)/shard_map/ppermute | solution.py:281
  26.0 3.8 %main.1 = (f32[3,1,128]{2,1,0:T(1,128)}, bf16[1152,256]{1,0:T(8,128)(2,1)S(1)}, f32[4,256,128]{2,1,0:T(8,128)S(1)}, bf16[4,256,128]{2,1,0:T(8,128)(2,1)S(1)}) custom-call(f32[3,1,128]{2,1,0:T(1,128)S(1)} %bitcast.55, s32[1,1]{1,0:T(1,128)} %bitcast.51.counts_ref, s32[2]{0:T(128)S(1)} %pad_add_fusion.place_ref, s32[1,128]{1,0:T(1,128)S(1)} %bitcast.58, ...), custom_call_target="tpu_custom_call" | custom-call | tf_op jit(solution)/shard_map/main/pallas_call | solution.py:241
  30.3 1.0 %late.1 = (f32[5,256,128]{2,1,0:T(8,128)S(1)}, bf16[5,256,128]{2,1,0:T(8,128)(2,1)S(1)}) custom-call(bf16[1152,256]{1,0:T(8,128)(2,1)S(1)} %get-tuple-element.18.right_ref, bf16[1152,1280]{1,0:T(8,128)(2,1)S(1)} %get-tuple-element.19.kern_ref), custom_call_target="tpu_custom_call" | custom-call | flops 754974720 | bytes 2949120 | tf_op jit(solution)/shard_map/late/pallas_call | solution.py:256
  31.7 0.8 %collective-permute-start.15 = (bf16[256,128]{1,0:T(8,128)(2,1)S(1)}, bf16[256,128]{1,0:T(8,128)(2,1)S(1)}, u32[]{:S(2)}, u32[]{:S(2)}) collective-permute-start(bf16[256,128]{1,0:T(8,128)(2,1)S(1)} %get-tuple-element.31), channel_id=1, source_target_pairs={{0,20},{1,21},{2,22},{3,23},{4,16},{5,17},{6,18},{7,19},{8,28},{9,... | collective-permute-start | bytes 196616 | tf_op jit(solution)/shard_map/ppermute | solution.py:277
  32.5 0.6 %collective-permute-done.12 = bf16[5,256,128]{2,1,0:T(8,128)(2,1)S(1)} collective-permute-done((bf16[5,256,128]{2,1,0:T(8,128)(2,1)S(1)}, bf16[5,256,128]{2,1,0:T(8,128)(2,1)S(1)}, u32[]{:S(2)}, u32[]{:S(2)}) %collective-permute-start.12) | collective-permute-done | bytes 327712 | tf_op jit(solution)/shard_map/ppermute | solution.py:281
  33.1 0.7 %collective-permute-start.14 = (bf16[2,256,128]{2,1,0:T(8,128)(2,1)S(1)}, bf16[2,256,128]{2,1,0:T(8,128)(2,1)S(1)}, u32[]{:S(2)}, u32[]{:S(2)}) collective-permute-start(bf16[2,256,128]{2,1,0:T(8,128)(2,1)S(1)} %pad_maximum_fusion.3), channel_id=1, source_target_pairs={{0,20},{1,21},{2,22},{3,23},{4,16},{5,17},{6,18},{7,19},{8,28},{9,... | collective-permute-start | bytes 393224 | tf_op jit(solution)/shard_map/ppermute | solution.py:277
  33.9 1.8 %collective-permute-done.15 = bf16[256,128]{1,0:T(8,128)(2,1)S(1)} collective-permute-done((bf16[256,128]{1,0:T(8,128)(2,1)S(1)}, bf16[256,128]{1,0:T(8,128)(2,1)S(1)}, u32[]{:S(2)}, u32[]{:S(2)}) %collective-permute-start.15) | collective-permute-done | bytes 65568 | tf_op jit(solution)/shard_map/ppermute | solution.py:277
  35.7 1.1 %collective-permute-start.17 = (bf16[256,128]{1,0:T(8,128)(2,1)S(1)}, bf16[256,128]{1,0:T(8,128)(2,1)S(1)}, u32[]{:S(2)}, u32[]{:S(2)}) collective-permute-start(bf16[256,128]{1,0:T(8,128)(2,1)S(1)} %fusion.5), channel_id=1, source_target_pairs={{0,12},{1,13},{2,14},{3,15},{4,8},{5,9},{6,10},{7,11},{8,4},{9,5},... | collective-permute-start | bytes 196616 | tf_op jit(solution)/shard_map/ppermute | solution.py:277
  36.8 1.9 %collective-permute-done.14 = bf16[2,256,128]{2,1,0:T(8,128)(2,1)S(1)} collective-permute-done((bf16[2,256,128]{2,1,0:T(8,128)(2,1)S(1)}, bf16[2,256,128]{2,1,0:T(8,128)(2,1)S(1)}, u32[]{:S(2)}, u32[]{:S(2)}) %collective-permute-start.14) | collective-permute-done | bytes 131104 | tf_op jit(solution)/shard_map/ppermute | solution.py:277
  38.7 1.3 %collective-permute-start.16 = (bf16[2,256,128]{2,1,0:T(8,128)(2,1)S(1)}, bf16[2,256,128]{2,1,0:T(8,128)(2,1)S(1)}, u32[]{:S(2)}, u32[]{:S(2)}) collective-permute-start(bf16[2,256,128]{2,1,0:T(8,128)(2,1)S(1)} %fusion), channel_id=1, source_target_pairs={{0,12},{1,13},{2,14},{3,15},{4,8},{5,9},{6,10},{7,11},{8,4},{9,5},... | collective-permute-start | bytes 393224 | tf_op jit(solution)/shard_map/ppermute | solution.py:277
  40.0 3.1 %collective-permute-start.19 = (bf16[256,128]{1,0:T(8,128)(2,1)S(1)}, bf16[256,128]{1,0:T(8,128)(2,1)S(1)}, u32[]{:S(2)}, u32[]{:S(2)}) collective-permute-start(bf16[256,128]{1,0:T(8,128)(2,1)S(1)} %fusion.3), channel_id=1, source_target_pairs={{0,7},{1,6},{2,5},{3,4},{4,3},{5,2},{6,1},{7,0},{8,15},{9,14},{10,... | collective-permute-start | bytes 196616 | tf_op jit(solution)/shard_map/ppermute | solution.py:277
  43.2 0.8 %collective-permute-done.16 = bf16[2,256,128]{2,1,0:T(8,128)(2,1)S(1)} collective-permute-done((bf16[2,256,128]{2,1,0:T(8,128)(2,1)S(1)}, bf16[2,256,128]{2,1,0:T(8,128)(2,1)S(1)}, u32[]{:S(2)}, u32[]{:S(2)}) %collective-permute-start.16) | collective-permute-done | bytes 131104 | tf_op jit(solution)/shard_map/ppermute | solution.py:277
  44.0 1.6 %collective-permute-start.18 = (bf16[256,128]{1,0:T(8,128)(2,1)S(1)}, bf16[256,128]{1,0:T(8,128)(2,1)S(1)}, u32[]{:S(2)}, u32[]{:S(2)}) collective-permute-start(bf16[256,128]{1,0:T(8,128)(2,1)S(1)} %fusion.11), channel_id=1, source_target_pairs={{0,5},{1,4},{2,7},{3,6},{4,1},{5,0},{6,3},{7,2},{8,13},{9,12},{10,... | collective-permute-start | bytes 196616 | tf_op jit(solution)/shard_map/ppermute | solution.py:277
  45.6 0.5 collective-permute-done.19
  46.1 1.8 %collective-permute-done.18 = bf16[256,128]{1,0:T(8,128)(2,1)S(1)} collective-permute-done((bf16[256,128]{1,0:T(8,128)(2,1)S(1)}, bf16[256,128]{1,0:T(8,128)(2,1)S(1)}, u32[]{:S(2)}, u32[]{:S(2)}) %collective-permute-start.18) | collective-permute-done | bytes 65568 | tf_op jit(solution)/shard_map/ppermute | solution.py:277
  47.9 0.9 %convolution_bitcast_fusion = f32[1,1,1,128,256]{4,3,2,1,0:T(8,128)} fusion(bf16[256,256]{1,0:T(8,128)(2,1)S(1)} %copy-done.7, f32[5,256,128]{2,1,0:T(8,128)S(1)} %convert_add_fusion, bf16[256,128]{1,0:T(8,128)(2,1)S(1)} %collective-permute-done.19, bf16[256,128]{1,0:T(8,128)(2,1)S(1)} %collective-permute-done.18, ...), kind=kOutput, calls=%fused_computation | convolution fusion | flops 17006592 | bytes 589824 | tf_op jit(solution)/shard_map/dot_general | solution.py:365
  (44 shorter events, 1.4 us)
Async XLA Ops:
  3.0 6.3 %collective-permute-start.8 = (bf16[144,256]{1,0:T(8,128)(2,1)}, bf16[144,256]{1,0:T(8,128)(2,1)S(1)}, u32[]{:S(2)}, u32[]{:S(2)}) collective-permute-start(bf16[144,256]{1,0:T(8,128)(2,1)} %message.1), channel_id=1, source_target_pairs={{0,12},{1,13},{2,14},{3,15},{4,8},{5,9},{6,10},{7,11},{8,4},{9,5},... | collective-permute-start | bytes 221192 | tf_op jit(solution)/shard_map/ppermute | solution.py:277
  5.4 5.6 %collective-permute-start = (bf16[144,256]{1,0:T(8,128)(2,1)}, bf16[144,256]{1,0:T(8,128)(2,1)S(1)}, u32[]{:S(2)}, u32[]{:S(2)}) collective-permute-start(bf16[144,256]{1,0:T(8,128)(2,1)} %message.1), channel_id=1, source_target_pairs={{0,5},{1,4},{2,7},{3,6},{4,1},{5,0},{6,3},{7,2},{8,13},{9,12},{10,... | collective-permute-start | bytes 221192 | tf_op jit(solution)/shard_map/ppermute | solution.py:277
  7.2 6.6 %collective-permute-start.4 = (bf16[144,256]{1,0:T(8,128)(2,1)}, bf16[144,256]{1,0:T(8,128)(2,1)S(1)}, u32[]{:S(2)}, u32[]{:S(2)}) collective-permute-start(bf16[144,256]{1,0:T(8,128)(2,1)} %message.1), channel_id=1, source_target_pairs={{0,7},{1,6},{2,5},{3,4},{4,3},{5,2},{6,1},{7,0},{8,15},{9,14},{10,... | collective-permute-start | bytes 221192 | tf_op jit(solution)/shard_map/ppermute | solution.py:277
  9.3 4.6 %collective-permute-start.9 = (bf16[144,256]{1,0:T(8,128)(2,1)S(1)}, bf16[144,256]{1,0:T(8,128)(2,1)S(1)}, u32[]{:S(2)}, u32[]{:S(2)}) collective-permute-start(bf16[144,256]{1,0:T(8,128)(2,1)S(1)} %collective-permute-done.8), channel_id=1, source_target_pairs={{0,20},{1,21},{2,22},{3,23},{4,16},{5,17},{6,18},{7,19},{8,28},{9,... | collective-permute-start | bytes 221192 | tf_op jit(solution)/shard_map/ppermute | solution.py:277
  10.9 4.7 %collective-permute-start.1 = (bf16[144,256]{1,0:T(8,128)(2,1)S(1)}, bf16[144,256]{1,0:T(8,128)(2,1)S(1)}, u32[]{:S(2)}, u32[]{:S(2)}) collective-permute-start(bf16[144,256]{1,0:T(8,128)(2,1)S(1)} %collective-permute-done), channel_id=1, source_target_pairs={{0,12},{1,13},{2,14},{3,15},{4,8},{5,9},{6,10},{7,11},{8,4},{9,5},... | collective-permute-start | bytes 221192 | tf_op jit(solution)/shard_map/ppermute | solution.py:277
  13.9 6.6 %collective-permute-start.10 = (bf16[4,144,256]{2,1,0:T(8,128)(2,1)S(1)}, bf16[4,144,256]{2,1,0:T(8,128)(2,1)S(1)}, u32[]{:S(2)}, u32[]{:S(2)}) collective-permute-start(bf16[4,144,256]{2,1,0:T(8,128)(2,1)S(1)} %pad_maximum_fusion.refs_2_), channel_id=1, source_target_pairs={{0,4},{4,0},{1,5},{5,1},{2,6},{6,2},{3,7},{7,3},{8,12},{12,8},{9,1... | collective-permute-start | bytes 884744 | tf_op jit(solution)/shard_map/ppermute | solution.py:281
  14.0 6.4 %collective-permute-start.7 = (bf16[144,256]{1,0:T(8,128)(2,1)}, bf16[144,256]{1,0:T(8,128)(2,1)S(1)}, u32[]{:S(2)}, u32[]{:S(2)}) collective-permute-start(bf16[144,256]{1,0:T(8,128)(2,1)} %message.1), channel_id=1, source_target_pairs={{0,4},{4,0},{1,5},{5,1},{2,6},{6,2},{3,7},{7,3},{8,12},{12,8},{9,1... | collective-permute-start | bytes 221192 | tf_op jit(solution)/shard_map/ppermute | solution.py:281
  14.4 4.3 %collective-permute-start.5 = (bf16[144,256]{1,0:T(8,128)(2,1)S(1)}, bf16[144,256]{1,0:T(8,128)(2,1)S(1)}, u32[]{:S(2)}, u32[]{:S(2)}) collective-permute-start(bf16[144,256]{1,0:T(8,128)(2,1)S(1)} %collective-permute-done.4), channel_id=1, source_target_pairs={{0,12},{1,13},{2,14},{3,15},{4,8},{5,9},{6,10},{7,11},{8,4},{9,5},... | collective-permute-start | bytes 221192 | tf_op jit(solution)/shard_map/ppermute | solution.py:277
  15.6 4.7 %collective-permute-start.2 = (bf16[144,256]{1,0:T(8,128)(2,1)S(1)}, bf16[144,256]{1,0:T(8,128)(2,1)S(1)}, u32[]{:S(2)}, u32[]{:S(2)}) collective-permute-start(bf16[144,256]{1,0:T(8,128)(2,1)S(1)} %collective-permute-done.1), channel_id=1, source_target_pairs={{0,20},{1,21},{2,22},{3,23},{4,16},{5,17},{6,18},{7,19},{8,28},{9,... | collective-permute-start | bytes 221192 | tf_op jit(solution)/shard_map/ppermute | solution.py:277
  18.8 5.7 %collective-permute-start.6 = (bf16[144,256]{1,0:T(8,128)(2,1)S(1)}, bf16[144,256]{1,0:T(8,128)(2,1)S(1)}, u32[]{:S(2)}, u32[]{:S(2)}) collective-permute-start(bf16[144,256]{1,0:T(8,128)(2,1)S(1)} %collective-permute-done.5), channel_id=1, source_target_pairs={{0,20},{1,21},{2,22},{3,23},{4,16},{5,17},{6,18},{7,19},{8,28},{9,... | collective-permute-start | bytes 221192 | tf_op jit(solution)/shard_map/ppermute | solution.py:277
  20.3 4.1 %collective-permute-start.3 = (bf16[2,144,256]{2,1,0:T(8,128)(2,1)S(1)}, bf16[2,144,256]{2,1,0:T(8,128)(2,1)S(1)}, u32[]{:S(2)}, u32[]{:S(2)}) collective-permute-start(bf16[2,144,256]{2,1,0:T(8,128)(2,1)S(1)} %pad_maximum_fusion.1.refs_0_), channel_id=1, source_target_pairs={{0,4},{4,0},{1,5},{5,1},{2,6},{6,2},{3,7},{7,3},{8,12},{12,8},{9,1... | collective-permute-start | bytes 442376 | tf_op jit(solution)/shard_map/ppermute | solution.py:281
  20.4 0.9 %copy-start = (bf16[144,256]{1,0:T(8,128)(2,1)S(1)}, bf16[144,256]{1,0:T(8,128)(2,1)}, u32[]{:S(2)}) copy-start(bf16[144,256]{1,0:T(8,128)(2,1)} %message.1) | copy-start | bytes 221188
  21.3 0.7 %copy-start.2 = (f32[1,1,1,3,128]{4,2,3,1,0:T(1,128)S(1)}, f32[1,1,1,3,128]{4,2,3,1,0:T(1,128)}, u32[]{:S(2)}) copy-start(f32[1,1,1,3,128]{4,2,3,1,0:T(1,128)} %param.8) | copy-start | bytes 4612
  22.0 4.0 %copy-start.1 = (f32[6,256]{1,0:T(8,128)S(1)}, f32[6,256]{1,0:T(8,128)}, u32[]{:S(2)}) copy-start(f32[6,256]{1,0:T(8,128)} %radial_ref.1) | copy-start | bytes 18436
  22.0 4.0 %copy-start.3 = (f32[1,1,1,3,128]{4,2,3,1,0:T(1,128)S(1)}, f32[1,1,1,3,128]{4,2,3,1,0:T(1,128)}, u32[]{:S(2)}) copy-start(f32[1,1,1,3,128]{4,2,3,1,0:T(1,128)} %param.8) | copy-start | bytes 4612
  22.0 4.0 %copy-start.4 = (f32[1,1,1,3,128]{4,2,3,1,0:T(1,128)S(1)}, f32[1,1,1,3,128]{4,2,3,1,0:T(1,128)}, u32[]{:S(2)}) copy-start(f32[1,1,1,3,128]{4,2,3,1,0:T(1,128)} %param.12) | copy-start | bytes 4612
  22.0 4.0 %copy-start.5 = (f32[256]{0:T(256)S(1)}, f32[256]{0:T(256)}, u32[]{:S(2)}) copy-start(f32[256]{0:T(256)} %param.15) | copy-start | bytes 3076
  22.0 4.0 %copy-start.6 = (s32[1,1,1,128]{3,2,1,0:T(1,128)S(1)}, s32[1,1,1,128]{3,2,1,0:T(1,128)}, u32[]{:S(2)}) copy-start(s32[1,1,1,128]{3,2,1,0:T(1,128)} %param.11) | copy-start | bytes 1540
  24.5 1.5 %collective-permute-start.11 = (bf16[2,144,256]{2,1,0:T(8,128)(2,1)S(1)}, bf16[2,144,256]{2,1,0:T(8,128)(2,1)S(1)}, u32[]{:S(2)}, u32[]{:S(2)}) collective-permute-start(bf16[2,144,256]{2,1,0:T(8,128)(2,1)S(1)} %pad_maximum_fusion.2.refs_2_), channel_id=1, source_target_pairs={{0,4},{4,0},{1,5},{5,1},{2,6},{6,2},{3,7},{7,3},{8,12},{12,8},{9,1... | collective-permute-start | bytes 442376 | tf_op jit(solution)/shard_map/ppermute | solution.py:281
  29.8 1.7 %collective-permute-start.13 = (bf16[4,256,128]{2,1,0:T(8,128)(2,1)S(1)}, bf16[4,256,128]{2,1,0:T(8,128)(2,1)S(1)}, u32[]{:S(2)}, u32[]{:S(2)}) collective-permute-start(bf16[4,256,128]{2,1,0:T(8,128)(2,1)S(1)} %get-tuple-element.23), channel_id=1, source_target_pairs={{0,4},{4,0},{1,5},{5,1},{2,6},{6,2},{3,7},{7,3},{8,12},{12,8},{9,1... | collective-permute-start | bytes 786440 | tf_op jit(solution)/shard_map/ppermute | solution.py:281
  31.3 16.6 %copy-start.7 = (bf16[256,256]{1,0:T(8,128)(2,1)S(1)}, bf16[256,256]{1,0:T(8,128)(2,1)}, u32[]{:S(2)}) copy-start(bf16[256,256]{1,0:T(8,128)(2,1)} %w_ref.1) | copy-start | bytes 393220
  31.3 1.7 %collective-permute-start.12 = (bf16[5,256,128]{2,1,0:T(8,128)(2,1)S(1)}, bf16[5,256,128]{2,1,0:T(8,128)(2,1)S(1)}, u32[]{:S(2)}, u32[]{:S(2)}) collective-permute-start(bf16[5,256,128]{2,1,0:T(8,128)(2,1)S(1)} %get-tuple-element.21), channel_id=1, source_target_pairs={{0,4},{4,0},{1,5},{5,1},{2,6},{6,2},{3,7},{7,3},{8,12},{12,8},{9,1... | collective-permute-start | bytes 983048 | tf_op jit(solution)/shard_map/ppermute | solution.py:281
  31.7 4.0 %collective-permute-start.15 = (bf16[256,128]{1,0:T(8,128)(2,1)S(1)}, bf16[256,128]{1,0:T(8,128)(2,1)S(1)}, u32[]{:S(2)}, u32[]{:S(2)}) collective-permute-start(bf16[256,128]{1,0:T(8,128)(2,1)S(1)} %get-tuple-element.31), channel_id=1, source_target_pairs={{0,20},{1,21},{2,22},{3,23},{4,16},{5,17},{6,18},{7,19},{8,28},{9,... | collective-permute-start | bytes 196616 | tf_op jit(solution)/shard_map/ppermute | solution.py:277
  33.1 5.5 %collective-permute-start.14 = (bf16[2,256,128]{2,1,0:T(8,128)(2,1)S(1)}, bf16[2,256,128]{2,1,0:T(8,128)(2,1)S(1)}, u32[]{:S(2)}, u32[]{:S(2)}) collective-permute-start(bf16[2,256,128]{2,1,0:T(8,128)(2,1)S(1)} %pad_maximum_fusion.3), channel_id=1, source_target_pairs={{0,20},{1,21},{2,22},{3,23},{4,16},{5,17},{6,18},{7,19},{8,28},{9,... | collective-permute-start | bytes 393224 | tf_op jit(solution)/shard_map/ppermute | solution.py:277
  35.7 4.3 %collective-permute-start.17 = (bf16[256,128]{1,0:T(8,128)(2,1)S(1)}, bf16[256,128]{1,0:T(8,128)(2,1)S(1)}, u32[]{:S(2)}, u32[]{:S(2)}) collective-permute-start(bf16[256,128]{1,0:T(8,128)(2,1)S(1)} %fusion.5), channel_id=1, source_target_pairs={{0,12},{1,13},{2,14},{3,15},{4,8},{5,9},{6,10},{7,11},{8,4},{9,5},... | collective-permute-start | bytes 196616 | tf_op jit(solution)/shard_map/ppermute | solution.py:277
  38.7 5.3 %collective-permute-start.16 = (bf16[2,256,128]{2,1,0:T(8,128)(2,1)S(1)}, bf16[2,256,128]{2,1,0:T(8,128)(2,1)S(1)}, u32[]{:S(2)}, u32[]{:S(2)}) collective-permute-start(bf16[2,256,128]{2,1,0:T(8,128)(2,1)S(1)} %fusion), channel_id=1, source_target_pairs={{0,12},{1,13},{2,14},{3,15},{4,8},{5,9},{6,10},{7,11},{8,4},{9,5},... | collective-permute-start | bytes 393224 | tf_op jit(solution)/shard_map/ppermute | solution.py:277
  40.0 6.1 %collective-permute-start.19 = (bf16[256,128]{1,0:T(8,128)(2,1)S(1)}, bf16[256,128]{1,0:T(8,128)(2,1)S(1)}, u32[]{:S(2)}, u32[]{:S(2)}) collective-permute-start(bf16[256,128]{1,0:T(8,128)(2,1)S(1)} %fusion.3), channel_id=1, source_target_pairs={{0,7},{1,6},{2,5},{3,4},{4,3},{5,2},{6,1},{7,0},{8,15},{9,14},{10,... | collective-permute-start | bytes 196616 | tf_op jit(solution)/shard_map/ppermute | solution.py:277
  44.0 3.9 %collective-permute-start.18 = (bf16[256,128]{1,0:T(8,128)(2,1)S(1)}, bf16[256,128]{1,0:T(8,128)(2,1)S(1)}, u32[]{:S(2)}, u32[]{:S(2)}) collective-permute-start(bf16[256,128]{1,0:T(8,128)(2,1)S(1)} %fusion.11), channel_id=1, source_target_pairs={{0,5},{1,4},{2,7},{3,6},{4,1},{5,0},{6,3},{7,2},{8,13},{9,12},{10,... | collective-permute-start | bytes 196616 | tf_op jit(solution)/shard_map/ppermute | solution.py:277

commit v4 on v3

--- a/solution.py
+++ b/solution.py
@@ -40,16 +40,15 @@
     return total
 
 
-def occupied(counts_ref, atoms):
-    return lax.broadcasted_iota(jnp.int32, (1, atoms), 1) < counts_ref[...]
-
-
 def message_kernel(feat_ref, w_ref, offs_ref, counts_ref, out_ref):
     atoms, width = feat_ref.shape
-    place = jnp.where(occupied(counts_ref, atoms), offs_ref[:, 0, :], -FAR)
-    out_ref[:atoms, :] = jnp.dot(
+    occupied = lax.broadcasted_iota(jnp.int32, (1, atoms), 1) < counts_ref[...]
+    place = jnp.where(occupied, offs_ref[:, 0, :], -FAR)
+    proj = jnp.dot(
         feat_ref[...], w_ref[...], preferred_element_type=jnp.float32
     ).astype(jnp.bfloat16)
+    for half in range(width // atoms):
+        out_ref[half * atoms : (half + 1) * atoms, :] = proj[:, half * atoms : (half + 1) * atoms]
     high = place.astype(jnp.bfloat16)
     rest = place - high.astype(jnp.float32)
     middle = rest.astype(jnp.bfloat16)
@@ -63,28 +62,31 @@
         ],
         0,
     )
-    out_ref[atoms:, :atoms] = rows.astype(jnp.bfloat16)
-    if width > atoms:
-        out_ref[atoms:, atoms:] = jnp.zeros((TAIL, width - atoms), jnp.bfloat16)
+    out_ref[width:, :] = rows.astype(jnp.bfloat16)
 
 
 def across(row, count):
     return jnp.transpose(jnp.broadcast_to(row, (count, row.shape[1])))
 
 
-def build(slots, bases, offs_ref, counts_ref, place_ref, blocks, kern_ref, proj_ref):
-    atoms = offs_ref.shape[2]
+def spots(block):
+    coded = block[block.shape[0] - TAIL :, :].astype(jnp.float32)
+    return [coded[c : c + 1, :] + coded[3 + c : 4 + c, :] + coded[6 + c : 7 + c, :] for c in range(3)]
+
+
+def build(slots, bases, own, place_ref, blocks, kern_ref, proj_ref):
+    rows, atoms = blocks[0].shape
     rate = 2.0 * GAMMA / (bases - 1)
-    occ = occupied(counts_ref, atoms)
-    own = [across(jnp.where(occ, offs_ref[c], FAR), atoms) for c in range(3)]
+    own = [across(jnp.where(spot < -0.5 * FAR, FAR, spot), atoms) for spot in spots(own)]
     turn = [None if axis is None else 1 - 2 * (place_ref[axis] & 1) for axis in (0, None, 1)]
     for s, steps in enumerate(slots):
         block = blocks[s]
-        proj_ref[s * atoms : (s + 1) * atoms, :] = block[:atoms, :]
-        coded = block[atoms:, :atoms].astype(jnp.float32)
+        for half in range((rows - TAIL) // atoms):
+            proj_ref[s * atoms : (s + 1) * atoms, half * atoms : (half + 1) * atoms] = block[
+                half * atoms : (half + 1) * atoms, :
+            ]
         apart = []
-        for c in range(3):
-            spot = coded[c : c + 1, :] + coded[3 + c : 4 + c, :] + coded[6 + c : 7 + c, :]
+        for c, spot in enumerate(spots(block)):
             step = steps[c]
             if step is None:
                 away = spot - own[c]
@@ -127,17 +129,17 @@
     ]
 
 
-def scatter(right, kern_ref, held_ref, other_refs):
+def scatter(right, kern_ref, lane, held_ref, other_refs, columns):
     atoms = held_ref.shape[2]
     ways = 1 + len(other_refs)
-    for k in range(held_ref.shape[0]):
-        lanes = slice(k * ways * atoms, (k + 1) * ways * atoms)
+    for k, column in enumerate(columns):
+        lanes = slice(lane + k * ways * atoms, lane + (k + 1) * ways * atoms)
         back = lax.dot_general(
             right, kern_ref[:, lanes], (((0,), (0,)), ((), ())), preferred_element_type=jnp.float32
         )
-        held_ref[k] = back[:, :atoms]
+        held_ref[column] = back[:, :atoms]
         for way, ref in enumerate(other_refs):
-            ref[k] = back[:, (way + 1) * atoms : (way + 2) * atoms].astype(jnp.bfloat16)
+            ref[column] = back[:, (way + 1) * atoms : (way + 2) * atoms].astype(jnp.bfloat16)
 
 
 def pick(refs, ways):
@@ -145,28 +147,28 @@
     return [ref.at[k] for group in groups for k in range(group[0].shape[0]) for ref in group]
 
 
-def early_kernel(slots, ways, bases, offs_ref, counts_ref, place_ref, *refs):
+def early_kernel(slots, ways, bases, own_ref, place_ref, *refs):
     near, (kern_ref, msg_ref, proj_ref) = refs[:-3], refs[-3:]
-    blocks = pick(near, ways)
-    build(slots, bases, offs_ref, counts_ref, place_ref, blocks, kern_ref, proj_ref)
+    build(slots, bases, own_ref.at[0], place_ref, pick((own_ref,) + near, ways), kern_ref, proj_ref)
     rows = kern_ref.shape[0] // 3
     for m, part in enumerate(gather(kern_ref, proj_ref)):
         msg_ref[m * rows : (m + 1) * rows, :] = part
 
 
-def main_kernel(slots, ways, bases, arrays, early, offs_ref, counts_ref, place_ref, mask_ref, targ_ref, radial_ref, readout_ref, *refs):
+def main_kernel(slots, ways, bases, arrays, early, own_ref, place_ref, mask_ref, targ_ref, radial_ref, readout_ref, *refs):
     near, refs = refs[:arrays], refs[arrays:]
     if early:
-        before_ref, pred_ref, right_ref, held_ref = refs[:4]
-        refs = refs[4:]
+        before_ref, side_ref, pred_ref, right_ref, held_ref = refs[:5]
+        refs = refs[5:]
     else:
         pred_ref, held_ref = refs[:2]
         refs = refs[2:]
     others, (kern_ref, proj_ref) = refs[: ways - 1], refs[ways - 1 :]
-    atoms = offs_ref.shape[2]
+    own = own_ref.at[0]
+    atoms = own.shape[1]
     width = radial_ref.shape[1]
-    blocks = pick(near, ways)
-    build(slots, bases, offs_ref, counts_ref, place_ref, blocks, kern_ref, proj_ref)
+    blocks = pick(near if early else (own_ref,) + near, ways)
+    build(slots, bases, own, place_ref, blocks, kern_ref, proj_ref)
     msg = jnp.concatenate(gather(kern_ref, proj_ref), 0)
     if early:
         msg = msg + before_ref[...]
@@ -179,7 +181,7 @@
     readout = readout_ref[...]
     gates = readout * gate
     vec = [msg[(bases + c) * atoms : (bases + c + 1) * atoms] for c in range(3)]
-    chosen = jnp.where(occupied(counts_ref, atoms), mask_ref[...].astype(jnp.float32), 0.0)
+    chosen = jnp.where(spots(own)[0] < -0.5 * FAR, 0.0, mask_ref[...].astype(jnp.float32))
     lean = jnp.zeros((atoms, width), jnp.float32)
     sides = []
     for c in range(3):
@@ -193,11 +195,15 @@
     right = jnp.concatenate([(weight[b] * slope).astype(jnp.bfloat16) for b in range(bases)] + sides, 0)
     if early:
         right_ref[...] = right
-    scatter(right, kern_ref, held_ref, others)
+    total, fresh = held_ref.shape[0], len(slots) // ways
+    scatter(right, kern_ref, 0, held_ref, others, range(total - fresh, total))
+    if early:
+        lane = side_ref.shape[1] - (total - fresh) * ways * atoms
+        scatter(right, side_ref, lane, held_ref, others, range(total - fresh))
 
 
 def late_kernel(right_ref, kern_ref, held_ref, *other_refs):
-    scatter(right_ref[...], kern_ref, held_ref, other_refs)
+    scatter(right_ref[...], kern_ref, 0, held_ref, other_refs, range(held_ref.shape[0]))
 
 
 VMEM = pl.BlockSpec(memory_space=pltpu.VMEM)
@@ -213,13 +219,13 @@
     return [struct(count, width, atoms, dtype=jnp.float32)] + [struct(count, width, atoms)] * (ways - 1)
 
 
-def call_early(slots, ways, bases, common, near):
-    atoms, width = near[0].shape[1] - TAIL, near[0].shape[2]
+def call_early(slots, ways, bases, own, place, near):
+    atoms, width = near[0].shape[2], near[0].shape[1] - TAIL
     rows, columns = (bases + 3) * atoms, len(slots) * atoms
     return pl.pallas_call(
         functools.partial(early_kernel, slots, ways, bases),
         out_shape=[struct(rows, columns), struct(rows, width, dtype=jnp.float32)],
-        in_specs=[VMEM, VMEM, SMEM] + [VMEM] * len(near),
+        in_specs=[VMEM, SMEM] + [VMEM] * len(near),
         out_specs=[VMEM] * 2,
         scratch_shapes=[pltpu.VMEM((columns, width), jnp.bfloat16)],
         compiler_params=LIMIT,
@@ -227,32 +233,32 @@
             flops=10 * rows * columns * width, bytes_accessed=8 * rows * columns, transcendentals=2 * atoms * columns
         ),
         name="early",
-    )(*common, *near)
-
-
-def call_main(slots, ways, bases, common, readouts, near, before=None):
-    atoms, width = near[0].shape[1] - TAIL, near[0].shape[2]
+    )(own, place, *near)
+
+
+def call_main(slots, ways, bases, own, place, readouts, near, before=(), side=0):
+    atoms, width = near[0].shape[2], near[0].shape[1] - TAIL
     rows, columns = (bases + 3) * atoms, len(slots) * atoms
-    early = [] if before is None else [before]
+    early = list(before)
     out_shape = [struct(3, 1, atoms, dtype=jnp.float32)]
     if early:
         out_shape.append(struct(rows, width))
-    out_shape += products(len(slots) // ways, ways, width, atoms)
+    out_shape += products(side + len(slots) // ways, ways, width, atoms)
     return pl.pallas_call(
         functools.partial(main_kernel, slots, ways, bases, len(near), bool(early)),
         out_shape=out_shape,
-        in_specs=[VMEM, VMEM, SMEM] + [VMEM] * (len(readouts) + len(near) + len(early)),
+        in_specs=[VMEM, SMEM] + [VMEM] * (len(readouts) + len(near) + len(early)),
         out_specs=[VMEM] * len(out_shape),
         scratch_shapes=[pltpu.VMEM((rows, columns), jnp.bfloat16), pltpu.VMEM((columns, width), jnp.bfloat16)],
         compiler_params=LIMIT,
         name="main",
-    )(*common, *readouts, *near, *early)
-
-
-def call_late(right, kern, ways, atoms):
+    )(own, place, *readouts, *near, *early)
+
+
+def call_late(right, kern, count, ways, atoms):
     rows, width = right.shape
-    columns = kern.shape[1]
-    out_shape = products(columns // (ways * atoms), ways, width, atoms)
+    columns = count * ways * atoms
+    out_shape = products(count, ways, width, atoms)
     return pl.pallas_call(
         late_kernel,
         out_shape=out_shape,
@@ -289,55 +295,60 @@
     return lax.optimization_barrier((block, other))[0]
 
 
-def exchange_small(message, bases, common, readouts):
-    atoms = message.shape[0] - TAIL
+def exchange_small(message, bases, place, readouts):
+    atoms = message.shape[1]
     x1 = swap(message, "gx", 1)
     z1 = swap(message, "gz", 1)
     z3 = swap(message, "gz", 3)
-    x3 = swap(x1, "gx", 2)
+    x3 = swap(after(x1, z1), "gx", 2)
     x1z1 = swap(z1, "gx", 1)
+    x1z3 = swap(z3, "gx", 1)
     x3z1 = swap(x1z1, "gx", 2)
-    x1z3 = swap(z3, "gx", 1)
     x3z3 = swap(x1z3, "gx", 2)
-    near = jnp.stack([x1, x3, z1, z3])
-    near = [message[None], core(message)[None], near, core(near)]
 
     def both(x, z, hops):
         held, other = (0, None) if hops % 2 == 0 else (None, 0)
         return [(x, held, z), (x, other, z)]
-
     near_slots = both(0, 0, 0) + both("1", 0, 1) + both("-1", 0, 2) + both(0, "1", 1) + both(0, "-1", 1)
-    far_slots = both("1", "1", 2) + both("-1", "1", 3) + both("1", "-1", 2) + both("-1", "-1", 3)
-    kern, before = call_early(near_slots, 2, bases, common, near)
-    far1 = jnp.stack([x1z1, x3z1])
-    far = [far1, core(far1)]
-    x1z3, x3z3, _, _ = lax.optimization_barrier((x1z3, x3z3, far[1], before))
-    far3 = jnp.stack([x1z3, x3z3])
-    far += [far3, core(far3)]
-    pred, right, far_held, far_sent = call_main(far_slots, 2, bases, common, readouts, far, before)
+    near = jnp.stack([x1, x3, z1, z3])
+    own, rest = message[None], [core(message)[None], near, core(after(near, x1z3))]
+    side = jnp.stack([x1z1, x3z1])
+    rest += [side, core(after(side, x1z3))]
+    near_slots += both("1", "1", 2) + both("-1", "1", 3)
+    far_slots = both("1", "-1", 2) + both("-1", "-1", 3)
+    kern, before = call_early(near_slots, 2, bases, own, place, rest)
+    x3z3 = after(x3z3, before)
+    far = jnp.stack([x1z3, x3z3])
+    far = [far, core(far)]
+    pred, right, far_held, far_sent = call_main(far_slots, 2, bases, own, place, readouts, far, (before, kern), 2)
     far_sum = far_held + core(far_sent)
-    near_held, near_sent = call_late(right, kern, 2, atoms)
+    near_held, near_sent = call_late(right, kern, 5, 2, atoms)
     near_sum = near_held + core(near_sent)
     back3 = swap(narrow(far_sum[3]), "gx", 2)
     back1 = swap(narrow(jnp.stack([far_sum[1], near_sum[2]])), "gx", 2)
     next3 = narrow(far_sum[2] + back3)
-    next1 = narrow(jnp.stack([far_sum[0], near_sum[1]]) + after(back1, next3))
+    back1 = after(back1, next3)
+    next1 = narrow(far_sum[0] + back1[0])
+    back0 = back1[1]
+    next0 = narrow(near_sum[1] + back0)
     back3 = swap(next3, "gx", 1)
     back1 = swap(next1, "gx", 1)
+    back0 = swap(next0, "gx", 1)
     next3 = narrow(near_sum[4] + back3)
     back1 = after(back1, next3)
-    next1 = narrow(near_sum[3] + back1[0])
+    next1 = narrow(near_sum[3] + back1)
     back3 = swap(next3, "gz", 3)
-    return pred, near_sum[0] + back1[1] + swap(next1, "gz", 1) + back3
-
-
-def exchange_any(message, bases, common, readouts):
+    back1 = swap(next1, "gz", 1)
+    return pred, near_sum[0] + back0 + back1 + back3
+
+
+def exchange_any(message, bases, place, readouts):
     steps_x, steps_y, steps_z = (steps_of(lax.axis_size(a)) for a in AXES)
     near = jnp.concatenate(spread(message[None], "gz"), 0)
     near = jnp.concatenate(spread(near, "gx"), 0)
     near = spread(near, "gy")
     slots = [(x, y, z) for x, z, y in itertools.product(steps_x, steps_z, steps_y)]
-    pred, *parts = call_main(slots, len(near), bases, common, readouts, near)
+    pred, *parts = call_main(slots, len(near), bases, near[0], place, readouts, near[1:])
     back = collect(parts, "gy")
     back = back.reshape(len(steps_x), len(steps_z), *back.shape[1:])
     back = collect([back[0]] + [narrow(back[k]) for k in range(1, len(steps_x))], "gx")
@@ -353,15 +364,14 @@
     place = jnp.stack([lax.axis_index("gx"), lax.axis_index("gz")]).astype(jnp.int32)
     message = pl.pallas_call(
         message_kernel,
-        out_shape=struct(atoms + TAIL, width),
+        out_shape=struct(width + TAIL, atoms),
         in_specs=[VMEM] * 4,
         out_specs=VMEM,
         name="message",
     )(features[0, 0, 0], w_in, offs, count)
-    common = [offs, count, place]
     readouts = [mask.reshape(1, atoms), targets.reshape(3, 1, atoms), radial, readout[None, :]]
     small = tuple(lax.axis_size(a) for a in AXES) == (4, 2, 4)
-    pred, back = (exchange_small if small else exchange_any)(message, bases, common, readouts)
+    pred, back = (exchange_small if small else exchange_any)(message, bases, place, readouts)
     grad = lax.dot_general(
         narrow(back), w_in, (((0,), (1,)), ((), ())), preferred_element_type=jnp.float32
     )

time: 49 us -> 47.6 us (0.971)
  local copies, waits for them, and re-layouts: 1.63 us -> 0.92 us
  starting transfers between devices: 23.4 us -> 22.8 us
    pallas_call x1, Pallas kernels: 3.85 us -> 2.94 us  [call_main(): pl.pallas_call(functools.partial(main_kernel, slots, ways, bases, len(nea...]
    unnamed x16 -> x14, local copies, waits for them, and re-layouts: 1.59 us -> 0.9 us
    ppermute x14 -> x15, waiting for transfers between devices: 10.5 us -> 11.1 us  [swap(): return lax.ppermute(block, AXES, pairs)]
    pallas_call x1, Pallas kernels: 2.38 us -> 2.9 us  [call_early(): pl.pallas_call(functools.partial(early_kernel, slots, ways, bases), out_s...]
    ppermute x14 -> x15, starting transfers between devices: 21.5 us -> 21.4 us  [swap(): return lax.ppermute(block, AXES, pairs)]
  transfers between devices with their start and end apart: 20 -> 21, of which waited for: 9 -> 9; matrix products, arithmetic and copies ran while one was open for 1% -> 1% of each run, Pallas kernels for 7% -> 8%
where the time goes in v4:
time: 47.6 us; the launch traced here: 47.4 us
  starting transfers between devices  22.8 us (48%)
  waiting for transfers between devices  12.4 us (26%)
  Pallas kernels  8.61 us (18%)
  between operations  1.43 us (3%)
  local copies, waits for them, and re-layouts  0.92 us (2%)
  matrix products  0.87 us (2%)
    ppermute x15, starting transfers between devices, swap(): return lax.ppermute(block, AXES, pairs)  21.4 us
    ppermute x15, waiting for transfers between devices, swap(): return lax.ppermute(block, AXES, pairs)  11.1 us
    pallas_call x1, Pallas kernels, call_main(): pl.pallas_call(functools.partial(main_kernel, slots, ways, bases, len(nea...  2.94 us
    pallas_call x1, Pallas kernels, call_early(): pl.pallas_call(functools.partial(early_kernel, slots, ways, bases), out_s...  2.9 us
    pallas_call x1, Pallas kernels, on_device(): pl.pallas_call(message_kernel, out_shape=struct(width + TAIL, atoms), in_...  1.71 us
    ppermute x6, starting transfers between devices, core(): return lax.ppermute(block, 'gy', [(0, 1), (1, 0)])  1.48 us
    ppermute x6, waiting for transfers between devices, core(): return lax.ppermute(block, 'gy', [(0, 1), (1, 0)])  1.25 us
    pallas_call x1, Pallas kernels, call_late(): pl.pallas_call(late_kernel, out_shape=out_shape, in_specs=[VMEM] * 2, out...  1.05 us
  transfers between devices with their start and end apart: 21, of which 9 were waited for; matrix products, arithmetic and copies ran while one was open for 1% of the time, Pallas kernels for 8%

profile of v4, /device:TPU:0, one launch (start us, length us, event | category | flops | bytes accessed | tf_op | source)
XLA Modules:
  0.0 47.4 jit_solution(14415198243383145590)
XLA Ops:
  1.3 1.7 %message.1 = bf16[272,128]{1,0:T(8,128)(2,1)} custom-call(bf16[128,256]{1,0:T(8,128)(2,1)} %bitcast.74, bf16[256,256]{1,0:T(8,128)(2,1)} %w_ref.1, f32[3,1,128]{2,1,0:T(1,128)} %bitcast.75, s32[1,1]{1,0:T(1,128)} %bitcast.59.counts_ref), custom_call_target="tpu_custom_call" | custom-call | tf_op jit(solution)/shard_map/message/pallas_call | solution.py:365
  3.0 2.5 %collective-permute-start.5 = (bf16[272,128]{1,0:T(8,128)(2,1)}, bf16[272,128]{1,0:T(8,128)(2,1)S(1)}, u32[]{:S(2)}, u32[]{:S(2)}) collective-permute-start(bf16[272,128]{1,0:T(8,128)(2,1)} %message.1), channel_id=1, source_target_pairs={{0,5},{1,4},{2,7},{3,6},{4,1},{5,0},{6,3},{7,2},{8,13},{9,12},{10,... | collective-permute-start | bytes 208904 | tf_op jit(solution)/shard_map/ppermute | solution.py:283
  5.5 1.8 %collective-permute-start.4 = (bf16[272,128]{1,0:T(8,128)(2,1)}, bf16[272,128]{1,0:T(8,128)(2,1)S(1)}, u32[]{:S(2)}, u32[]{:S(2)}) collective-permute-start(bf16[272,128]{1,0:T(8,128)(2,1)} %message.1), channel_id=1, source_target_pairs={{0,12},{1,13},{2,14},{3,15},{4,8},{5,9},{6,10},{7,11},{8,4},{9,5},... | collective-permute-start | bytes 208904 | tf_op jit(solution)/shard_map/ppermute | solution.py:283
  7.2 2.0 %collective-permute-start = (bf16[272,128]{1,0:T(8,128)(2,1)}, bf16[272,128]{1,0:T(8,128)(2,1)S(1)}, u32[]{:S(2)}, u32[]{:S(2)}) collective-permute-start(bf16[272,128]{1,0:T(8,128)(2,1)} %message.1), channel_id=1, source_target_pairs={{0,7},{1,6},{2,5},{3,4},{4,3},{5,2},{6,1},{7,0},{8,15},{9,14},{10,... | collective-permute-start | bytes 208904 | tf_op jit(solution)/shard_map/ppermute | solution.py:283
  9.3 0.2 collective-permute-done.4
  9.5 1.7 %collective-permute-start.8 = (bf16[272,128]{1,0:T(8,128)(2,1)S(1)}, bf16[272,128]{1,0:T(8,128)(2,1)S(1)}, u32[]{:S(2)}, u32[]{:S(2)}) collective-permute-start(bf16[272,128]{1,0:T(8,128)(2,1)S(1)} %collective-permute-done.5), channel_id=1, source_target_pairs={{0,12},{1,13},{2,14},{3,15},{4,8},{5,9},{6,10},{7,11},{8,4},{9,5},... | collective-permute-start | bytes 208904 | tf_op jit(solution)/shard_map/ppermute | solution.py:283
  11.2 1.0 %collective-permute-start.6 = (bf16[272,128]{1,0:T(8,128)(2,1)S(1)}, bf16[272,128]{1,0:T(8,128)(2,1)S(1)}, u32[]{:S(2)}, u32[]{:S(2)}) collective-permute-start(bf16[272,128]{1,0:T(8,128)(2,1)S(1)} %collective-permute-done.4), channel_id=1, source_target_pairs={{0,20},{1,21},{2,22},{3,23},{4,16},{5,17},{6,18},{7,19},{8,28},{9,... | collective-permute-start | bytes 208904 | tf_op jit(solution)/shard_map/ppermute | solution.py:283
  12.1 1.7 %collective-permute-done = bf16[272,128]{1,0:T(8,128)(2,1)S(1)} collective-permute-done((bf16[272,128]{1,0:T(8,128)(2,1)}, bf16[272,128]{1,0:T(8,128)(2,1)S(1)}, u32[]{:S(2)}, u32[]{:S(2)}) %collective-permute-start) | collective-permute-done | bytes 69664 | tf_op jit(solution)/shard_map/ppermute | solution.py:283
  13.8 0.2 collective-permute-start.1
  14.0 1.6 %collective-permute-start.9 = (bf16[272,128]{1,0:T(8,128)(2,1)S(1)}, bf16[272,128]{1,0:T(8,128)(2,1)S(1)}, u32[]{:S(2)}, u32[]{:S(2)}) collective-permute-start(bf16[272,128]{1,0:T(8,128)(2,1)S(1)} %collective-permute-done.8), channel_id=1, source_target_pairs={{0,20},{1,21},{2,22},{3,23},{4,16},{5,17},{6,18},{7,19},{8,28},{9,... | collective-permute-start | bytes 208904 | tf_op jit(solution)/shard_map/ppermute | solution.py:283
  15.6 2.4 %collective-permute-done.1 = bf16[272,128]{1,0:T(8,128)(2,1)S(1)} collective-permute-done((bf16[272,128]{1,0:T(8,128)(2,1)S(1)}, bf16[272,128]{1,0:T(8,128)(2,1)S(1)}, u32[]{:S(2)}, u32[]{:S(2)}) %collective-permute-start.1) | collective-permute-done | bytes 69664 | tf_op jit(solution)/shard_map/ppermute | solution.py:283
  18.2 0.5 collective-permute-start.10
  18.8 1.5 %collective-permute-start.2 = (bf16[272,128]{1,0:T(8,128)(2,1)S(1)}, bf16[272,128]{1,0:T(8,128)(2,1)S(1)}, u32[]{:S(2)}, u32[]{:S(2)}) collective-permute-start(bf16[272,128]{1,0:T(8,128)(2,1)S(1)} %collective-permute-done.1), channel_id=1, source_target_pairs={{0,20},{1,21},{2,22},{3,23},{4,16},{5,17},{6,18},{7,19},{8,28},{9,... | collective-permute-start | bytes 208904 | tf_op jit(solution)/shard_map/ppermute | solution.py:283
  20.4 0.9 %copy-done = bf16[272,128]{1,0:T(8,128)(2,1)S(1)} copy-done((bf16[272,128]{1,0:T(8,128)(2,1)S(1)}, bf16[272,128]{1,0:T(8,128)(2,1)}, u32[]{:S(2)}) %copy-start) | copy-done | bytes 69656
  21.3 2.9 %early.1 = (bf16[1152,1792]{1,0:T(8,128)(2,1)S(1)}, f32[1152,256]{1,0:T(8,128)S(1)}) custom-call(bf16[1,272,128]{2,1,0:T(8,128)(2,1)S(1)} %bitcast.60, s32[2]{0:T(128)S(1)} %pad_add_fusion.place_ref, bf16[1,272,128]{2,1,0:T(8,128)(2,1)S(1)} %bitcast.65, bf16[4,272,128]{2,1,0:T(8,128)(2,1)S(1)} %pad_maximum_fusion.refs_1_, ...), custom_call_target="tpu_custom_call" | custom-call | flops 5284823040 | bytes 16515072 | tf_op jit(solution)/shard_map/early/pallas_call | solution.py:225
  24.2 0.2 collective-permute-start.11
  24.4 1.2 %collective-permute-done.11.refs_1_ = bf16[2,272,128]{2,1,0:T(8,128)(2,1)S(1)} collective-permute-done((bf16[2,272,128]{2,1,0:T(8,128)(2,1)S(1)}, bf16[2,272,128]{2,1,0:T(8,128)(2,1)S(1)}, u32[]{:S(2)}, u32[]{:S(2)}) %collective-permute-start.11) | collective-permute-done | bytes 139296 | tf_op jit(solution)/shard_map/ppermute | solution.py:287
  25.7 2.9 %main.1 = (f32[3,1,128]{2,1,0:T(1,128)}, bf16[1152,256]{1,0:T(8,128)(2,1)S(1)}, f32[4,256,128]{2,1,0:T(8,128)S(1)}, bf16[4,256,128]{2,1,0:T(8,128)(2,1)S(1)}) custom-call(bf16[1,272,128]{2,1,0:T(8,128)(2,1)S(1)} %bitcast.61, s32[2]{0:T(128)S(1)} %pad_add_fusion.place_ref, s32[1,128]{1,0:T(1,128)S(1)} %bitcast.64, f32[3,1,128]{2,1,0:T(1,128)S(1)} %bitcast.62, ...), custom_call_target="tpu_custom_call" | custom-call | tf_op jit(solution)/shard_map/main/pallas_call | solution.py:247
  28.8 1.1 %late.1 = (f32[5,256,128]{2,1,0:T(8,128)S(1)}, bf16[5,256,128]{2,1,0:T(8,128)(2,1)S(1)}) custom-call(bf16[1152,256]{1,0:T(8,128)(2,1)S(1)} %get-tuple-element.23.right_ref, bf16[1152,1792]{1,0:T(8,128)(2,1)S(1)} %get-tuple-element.21.refs_3_.kern_ref), custom_call_target="tpu_custom_call" | custom-call | flops 754974720 | bytes 2949120 | tf_op jit(solution)/shard_map/late/pallas_call | solution.py:262
  29.8 0.4 collective-permute-start.12
  30.3 1.1 %collective-permute-start.15 = (bf16[256,128]{1,0:T(8,128)(2,1)S(1)}, bf16[256,128]{1,0:T(8,128)(2,1)S(1)}, u32[]{:S(2)}, u32[]{:S(2)}) collective-permute-start(bf16[256,128]{1,0:T(8,128)(2,1)S(1)} %get-tuple-element.35), channel_id=1, source_target_pairs={{0,20},{1,21},{2,22},{3,23},{4,16},{5,17},{6,18},{7,19},{8,28},{9,... | collective-permute-start | bytes 196616 | tf_op jit(solution)/shard_map/ppermute | solution.py:283
  31.6 1.3 %collective-permute-start.14 = (bf16[2,256,128]{2,1,0:T(8,128)(2,1)S(1)}, bf16[2,256,128]{2,1,0:T(8,128)(2,1)S(1)}, u32[]{:S(2)}, u32[]{:S(2)}) collective-permute-start(bf16[2,256,128]{2,1,0:T(8,128)(2,1)S(1)} %pad_maximum_fusion.3), channel_id=1, source_target_pairs={{0,20},{1,21},{2,22},{3,23},{4,16},{5,17},{6,18},{7,19},{8,28},{9,... | collective-permute-start | bytes 393224 | tf_op jit(solution)/shard_map/ppermute | solution.py:283
  32.9 1.6 %collective-permute-done.15 = bf16[256,128]{1,0:T(8,128)(2,1)S(1)} collective-permute-done((bf16[256,128]{1,0:T(8,128)(2,1)S(1)}, bf16[256,128]{1,0:T(8,128)(2,1)S(1)}, u32[]{:S(2)}, u32[]{:S(2)}) %collective-permute-start.15) | collective-permute-done | bytes 65568 | tf_op jit(solution)/shard_map/ppermute | solution.py:283
  34.5 1.5 %collective-permute-start.18 = (bf16[256,128]{1,0:T(8,128)(2,1)S(1)}, bf16[256,128]{1,0:T(8,128)(2,1)S(1)}, u32[]{:S(2)}, u32[]{:S(2)}) collective-permute-start(bf16[256,128]{1,0:T(8,128)(2,1)S(1)} %fusion.6), channel_id=1, source_target_pairs={{0,12},{1,13},{2,14},{3,15},{4,8},{5,9},{6,10},{7,11},{8,4},{9,5},... | collective-permute-start | bytes 196616 | tf_op jit(solution)/shard_map/ppermute | solution.py:283
  36.0 1.3 %collective-permute-done.14 = bf16[2,256,128]{2,1,0:T(8,128)(2,1)S(1)} collective-permute-done((bf16[2,256,128]{2,1,0:T(8,128)(2,1)S(1)}, bf16[2,256,128]{2,1,0:T(8,128)(2,1)S(1)}, u32[]{:S(2)}, u32[]{:S(2)}) %collective-permute-start.14) | collective-permute-done | bytes 131104 | tf_op jit(solution)/shard_map/ppermute | solution.py:283
  37.3 1.4 %collective-permute-start.17 = (bf16[256,128]{1,0:T(8,128)(2,1)S(1)}, bf16[256,128]{1,0:T(8,128)(2,1)S(1)}, u32[]{:S(2)}, u32[]{:S(2)}) collective-permute-start(bf16[256,128]{1,0:T(8,128)(2,1)S(1)} %get-tuple-element.37), channel_id=1, source_target_pairs={{0,12},{1,13},{2,14},{3,15},{4,8},{5,9},{6,10},{7,11},{8,4},{9,5},... | collective-permute-start | bytes 196616 | tf_op jit(solution)/shard_map/ppermute | solution.py:283
  38.7 2.7 %collective-permute-start.20 = (bf16[256,128]{1,0:T(8,128)(2,1)S(1)}, bf16[256,128]{1,0:T(8,128)(2,1)S(1)}, u32[]{:S(2)}, u32[]{:S(2)}) collective-permute-start(bf16[256,128]{1,0:T(8,128)(2,1)S(1)} %fusion.1), channel_id=1, source_target_pairs={{0,7},{1,6},{2,5},{3,4},{4,3},{5,2},{6,1},{7,0},{8,15},{9,14},{10,... | collective-permute-start | bytes 196616 | tf_op jit(solution)/shard_map/ppermute | solution.py:283
  41.4 0.9 %collective-permute-start.16 = (bf16[256,128]{1,0:T(8,128)(2,1)S(1)}, bf16[256,128]{1,0:T(8,128)(2,1)S(1)}, u32[]{:S(2)}, u32[]{:S(2)}) collective-permute-start(bf16[256,128]{1,0:T(8,128)(2,1)S(1)} %get-tuple-element.36), channel_id=1, source_target_pairs={{0,12},{1,13},{2,14},{3,15},{4,8},{5,9},{6,10},{7,11},{8,4},{9,5},... | collective-permute-start | bytes 196616 | tf_op jit(solution)/shard_map/ppermute | solution.py:283
  42.6 2.1 %collective-permute-done.20 = bf16[256,128]{1,0:T(8,128)(2,1)S(1)} collective-permute-done((bf16[256,128]{1,0:T(8,128)(2,1)S(1)}, bf16[256,128]{1,0:T(8,128)(2,1)S(1)}, u32[]{:S(2)}, u32[]{:S(2)}) %collective-permute-start.20) | collective-permute-done | bytes 65568 | tf_op jit(solution)/shard_map/ppermute | solution.py:283
  44.7 0.6 %collective-permute-done.16 = bf16[256,128]{1,0:T(8,128)(2,1)S(1)} collective-permute-done((bf16[256,128]{1,0:T(8,128)(2,1)S(1)}, bf16[256,128]{1,0:T(8,128)(2,1)S(1)}, u32[]{:S(2)}, u32[]{:S(2)}) %collective-permute-start.16) | collective-permute-done | bytes 65568 | tf_op jit(solution)/shard_map/ppermute | solution.py:283
  45.3 1.3 %collective-permute-done.19 = bf16[256,128]{1,0:T(8,128)(2,1)S(1)} collective-permute-done((bf16[256,128]{1,0:T(8,128)(2,1)S(1)}, bf16[256,128]{1,0:T(8,128)(2,1)S(1)}, u32[]{:S(2)}, u32[]{:S(2)}) %collective-permute-start.19) | collective-permute-done | bytes 65568 | tf_op jit(solution)/shard_map/ppermute | solution.py:283
  46.5 0.9 %convolution_bitcast_fusion = f32[1,1,1,128,256]{4,3,2,1,0:T(8,128)} fusion(bf16[256,256]{1,0:T(8,128)(2,1)S(1)} %copy-done.6, f32[5,256,128]{2,1,0:T(8,128)S(1)} %convert_add_fusion, bf16[256,128]{1,0:T(8,128)(2,1)S(1)} %collective-permute-done.20, bf16[256,128]{1,0:T(8,128)(2,1)S(1)} %collective-permute-done.19, bf16[256,128]{1,0:T(8,128)(2,1)S(1)} %collective-permute-done.16), kind=kOutput, calls=%fused_computation | convolution fusion | flops 17006592 | bytes 589824 | tf_op jit(solution)/shard_map/dot_general | solution.py:375
  (42 shorter events, 1.1 us)
Async XLA Ops:
  3.0 6.3 %collective-permute-start.5 = (bf16[272,128]{1,0:T(8,128)(2,1)}, bf16[272,128]{1,0:T(8,128)(2,1)S(1)}, u32[]{:S(2)}, u32[]{:S(2)}) collective-permute-start(bf16[272,128]{1,0:T(8,128)(2,1)} %message.1), channel_id=1, source_target_pairs={{0,5},{1,4},{2,7},{3,6},{4,1},{5,0},{6,3},{7,2},{8,13},{9,12},{10,... | collective-permute-start | bytes 208904 | tf_op jit(solution)/shard_map/ppermute | solution.py:283
  5.5 4.0 %collective-permute-start.4 = (bf16[272,128]{1,0:T(8,128)(2,1)}, bf16[272,128]{1,0:T(8,128)(2,1)S(1)}, u32[]{:S(2)}, u32[]{:S(2)}) collective-permute-start(bf16[272,128]{1,0:T(8,128)(2,1)} %message.1), channel_id=1, source_target_pairs={{0,12},{1,13},{2,14},{3,15},{4,8},{5,9},{6,10},{7,11},{8,4},{9,5},... | collective-permute-start | bytes 208904 | tf_op jit(solution)/shard_map/ppermute | solution.py:283
  7.2 6.6 %collective-permute-start = (bf16[272,128]{1,0:T(8,128)(2,1)}, bf16[272,128]{1,0:T(8,128)(2,1)S(1)}, u32[]{:S(2)}, u32[]{:S(2)}) collective-permute-start(bf16[272,128]{1,0:T(8,128)(2,1)} %message.1), channel_id=1, source_target_pairs={{0,7},{1,6},{2,5},{3,4},{4,3},{5,2},{6,1},{7,0},{8,15},{9,14},{10,... | collective-permute-start | bytes 208904 | tf_op jit(solution)/shard_map/ppermute | solution.py:283
  9.5 4.5 %collective-permute-start.8 = (bf16[272,128]{1,0:T(8,128)(2,1)S(1)}, bf16[272,128]{1,0:T(8,128)(2,1)S(1)}, u32[]{:S(2)}, u32[]{:S(2)}) collective-permute-start(bf16[272,128]{1,0:T(8,128)(2,1)S(1)} %collective-permute-done.5), channel_id=1, source_target_pairs={{0,12},{1,13},{2,14},{3,15},{4,8},{5,9},{6,10},{7,11},{8,4},{9,5},... | collective-permute-start | bytes 208904 | tf_op jit(solution)/shard_map/ppermute | solution.py:283
  11.2 4.4 %collective-permute-start.6 = (bf16[272,128]{1,0:T(8,128)(2,1)S(1)}, bf16[272,128]{1,0:T(8,128)(2,1)S(1)}, u32[]{:S(2)}, u32[]{:S(2)}) collective-permute-start(bf16[272,128]{1,0:T(8,128)(2,1)S(1)} %collective-permute-done.4), channel_id=1, source_target_pairs={{0,20},{1,21},{2,22},{3,23},{4,16},{5,17},{6,18},{7,19},{8,28},{9,... | collective-permute-start | bytes 208904 | tf_op jit(solution)/shard_map/ppermute | solution.py:283
  13.8 4.2 %collective-permute-start.1 = (bf16[272,128]{1,0:T(8,128)(2,1)S(1)}, bf16[272,128]{1,0:T(8,128)(2,1)S(1)}, u32[]{:S(2)}, u32[]{:S(2)}) collective-permute-start(bf16[272,128]{1,0:T(8,128)(2,1)S(1)} %collective-permute-done), channel_id=1, source_target_pairs={{0,12},{1,13},{2,14},{3,15},{4,8},{5,9},{6,10},{7,11},{8,4},{9,5},... | collective-permute-start | bytes 208904 | tf_op jit(solution)/shard_map/ppermute | solution.py:283
  14.0 4.2 %collective-permute-start.9 = (bf16[272,128]{1,0:T(8,128)(2,1)S(1)}, bf16[272,128]{1,0:T(8,128)(2,1)S(1)}, u32[]{:S(2)}, u32[]{:S(2)}) collective-permute-start(bf16[272,128]{1,0:T(8,128)(2,1)S(1)} %collective-permute-done.8), channel_id=1, source_target_pairs={{0,20},{1,21},{2,22},{3,23},{4,16},{5,17},{6,18},{7,19},{8,28},{9,... | collective-permute-start | bytes 208904 | tf_op jit(solution)/shard_map/ppermute | solution.py:283
  18.0 2.3 %collective-permute-start.7 = (bf16[4,272,128]{2,1,0:T(8,128)(2,1)S(1)}, bf16[4,272,128]{2,1,0:T(8,128)(2,1)S(1)}, u32[]{:S(2)}, u32[]{:S(2)}) collective-permute-start(bf16[4,272,128]{2,1,0:T(8,128)(2,1)S(1)} %pad_maximum_fusion.refs_1_), channel_id=1, source_target_pairs={{0,4},{4,0},{1,5},{5,1},{2,6},{6,2},{3,7},{7,3},{8,12},{12,8},{9,1... | collective-permute-start | bytes 835592 | tf_op jit(solution)/shard_map/ppermute | solution.py:287
  18.2 2.2 %collective-permute-start.10 = (bf16[2,272,128]{2,1,0:T(8,128)(2,1)S(1)}, bf16[2,272,128]{2,1,0:T(8,128)(2,1)S(1)}, u32[]{:S(2)}, u32[]{:S(2)}) collective-permute-start(bf16[2,272,128]{2,1,0:T(8,128)(2,1)S(1)} %pad_maximum_fusion.1.refs_3_), channel_id=1, source_target_pairs={{0,4},{4,0},{1,5},{5,1},{2,6},{6,2},{3,7},{7,3},{8,12},{12,8},{9,1... | collective-permute-start | bytes 417800 | tf_op jit(solution)/shard_map/ppermute | solution.py:287
  18.6 1.7 %collective-permute-start.3 = (bf16[272,128]{1,0:T(8,128)(2,1)}, bf16[272,128]{1,0:T(8,128)(2,1)S(1)}, u32[]{:S(2)}, u32[]{:S(2)}) collective-permute-start(bf16[272,128]{1,0:T(8,128)(2,1)} %message.1), channel_id=1, source_target_pairs={{0,4},{4,0},{1,5},{5,1},{2,6},{6,2},{3,7},{7,3},{8,12},{12,8},{9,1... | collective-permute-start | bytes 208904 | tf_op jit(solution)/shard_map/ppermute | solution.py:287
  18.8 5.3 %collective-permute-start.2 = (bf16[272,128]{1,0:T(8,128)(2,1)S(1)}, bf16[272,128]{1,0:T(8,128)(2,1)S(1)}, u32[]{:S(2)}, u32[]{:S(2)}) collective-permute-start(bf16[272,128]{1,0:T(8,128)(2,1)S(1)} %collective-permute-done.1), channel_id=1, source_target_pairs={{0,20},{1,21},{2,22},{3,23},{4,16},{5,17},{6,18},{7,19},{8,28},{9,... | collective-permute-start | bytes 208904 | tf_op jit(solution)/shard_map/ppermute | solution.py:283
  20.4 0.9 %copy-start = (bf16[272,128]{1,0:T(8,128)(2,1)S(1)}, bf16[272,128]{1,0:T(8,128)(2,1)}, u32[]{:S(2)}) copy-start(bf16[272,128]{1,0:T(8,128)(2,1)} %message.1) | copy-start | bytes 208900
  21.2 4.4 %copy-start.1 = (bf16[272,128]{1,0:T(8,128)(2,1)S(1)}, bf16[272,128]{1,0:T(8,128)(2,1)}, u32[]{:S(2)}) copy-start(bf16[272,128]{1,0:T(8,128)(2,1)} %message.1) | copy-start | bytes 208900
  21.2 4.4 %copy-start.2 = (f32[6,256]{1,0:T(8,128)S(1)}, f32[6,256]{1,0:T(8,128)}, u32[]{:S(2)}) copy-start(f32[6,256]{1,0:T(8,128)} %radial_ref.1) | copy-start | bytes 18436
  21.2 4.4 %copy-start.3 = (f32[1,1,1,3,128]{4,2,3,1,0:T(1,128)S(1)}, f32[1,1,1,3,128]{4,2,3,1,0:T(1,128)}, u32[]{:S(2)}) copy-start(f32[1,1,1,3,128]{4,2,3,1,0:T(1,128)} %param.12) | copy-start | bytes 4612
  21.3 4.4 %copy-start.4 = (f32[256]{0:T(256)S(1)}, f32[256]{0:T(256)}, u32[]{:S(2)}) copy-start(f32[256]{0:T(256)} %param.15) | copy-start | bytes 3076
  21.3 4.4 %copy-start.5 = (s32[1,1,1,128]{3,2,1,0:T(1,128)S(1)}, s32[1,1,1,128]{3,2,1,0:T(1,128)}, u32[]{:S(2)}) copy-start(s32[1,1,1,128]{3,2,1,0:T(1,128)} %param.11) | copy-start | bytes 1540
  24.2 1.4 %collective-permute-start.11 = (bf16[2,272,128]{2,1,0:T(8,128)(2,1)S(1)}, bf16[2,272,128]{2,1,0:T(8,128)(2,1)S(1)}, u32[]{:S(2)}, u32[]{:S(2)}) collective-permute-start(bf16[2,272,128]{2,1,0:T(8,128)(2,1)S(1)} %pad_maximum_fusion.2.refs_0_), channel_id=1, source_target_pairs={{0,4},{4,0},{1,5},{5,1},{2,6},{6,2},{3,7},{7,3},{8,12},{12,8},{9,1... | collective-permute-start | bytes 417800 | tf_op jit(solution)/shard_map/ppermute | solution.py:287
  28.6 1.6 %collective-permute-start.13 = (bf16[4,256,128]{2,1,0:T(8,128)(2,1)S(1)}, bf16[4,256,128]{2,1,0:T(8,128)(2,1)S(1)}, u32[]{:S(2)}, u32[]{:S(2)}) collective-permute-start(bf16[4,256,128]{2,1,0:T(8,128)(2,1)S(1)} %get-tuple-element.27), channel_id=1, source_target_pairs={{0,4},{4,0},{1,5},{5,1},{2,6},{6,2},{3,7},{7,3},{8,12},{12,8},{9,1... | collective-permute-start | bytes 786440 | tf_op jit(solution)/shard_map/ppermute | solution.py:287
  28.8 17.8 %copy-start.6 = (bf16[256,256]{1,0:T(8,128)(2,1)S(1)}, bf16[256,256]{1,0:T(8,128)(2,1)}, u32[]{:S(2)}) copy-start(bf16[256,256]{1,0:T(8,128)(2,1)} %w_ref.1) | copy-start | bytes 393220
  29.8 1.7 %collective-permute-start.12 = (bf16[5,256,128]{2,1,0:T(8,128)(2,1)S(1)}, bf16[5,256,128]{2,1,0:T(8,128)(2,1)S(1)}, u32[]{:S(2)}, u32[]{:S(2)}) collective-permute-start(bf16[5,256,128]{2,1,0:T(8,128)(2,1)S(1)} %get-tuple-element.25), channel_id=1, source_target_pairs={{0,4},{4,0},{1,5},{5,1},{2,6},{6,2},{3,7},{7,3},{8,12},{12,8},{9,1... | collective-permute-start | bytes 983048 | tf_op jit(solution)/shard_map/ppermute | solution.py:287
  30.3 4.1 %collective-permute-start.15 = (bf16[256,128]{1,0:T(8,128)(2,1)S(1)}, bf16[256,128]{1,0:T(8,128)(2,1)S(1)}, u32[]{:S(2)}, u32[]{:S(2)}) collective-permute-start(bf16[256,128]{1,0:T(8,128)(2,1)S(1)} %get-tuple-element.35), channel_id=1, source_target_pairs={{0,20},{1,21},{2,22},{3,23},{4,16},{5,17},{6,18},{7,19},{8,28},{9,... | collective-permute-start | bytes 196616 | tf_op jit(solution)/shard_map/ppermute | solution.py:283
  31.6 5.7 %collective-permute-start.14 = (bf16[2,256,128]{2,1,0:T(8,128)(2,1)S(1)}, bf16[2,256,128]{2,1,0:T(8,128)(2,1)S(1)}, u32[]{:S(2)}, u32[]{:S(2)}) collective-permute-start(bf16[2,256,128]{2,1,0:T(8,128)(2,1)S(1)} %pad_maximum_fusion.3), channel_id=1, source_target_pairs={{0,20},{1,21},{2,22},{3,23},{4,16},{5,17},{6,18},{7,19},{8,28},{9,... | collective-permute-start | bytes 393224 | tf_op jit(solution)/shard_map/ppermute | solution.py:283
  34.5 4.2 %collective-permute-start.18 = (bf16[256,128]{1,0:T(8,128)(2,1)S(1)}, bf16[256,128]{1,0:T(8,128)(2,1)S(1)}, u32[]{:S(2)}, u32[]{:S(2)}) collective-permute-start(bf16[256,128]{1,0:T(8,128)(2,1)S(1)} %fusion.6), channel_id=1, source_target_pairs={{0,12},{1,13},{2,14},{3,15},{4,8},{5,9},{6,10},{7,11},{8,4},{9,5},... | collective-permute-start | bytes 196616 | tf_op jit(solution)/shard_map/ppermute | solution.py:283
  37.3 5.1 %collective-permute-start.17 = (bf16[256,128]{1,0:T(8,128)(2,1)S(1)}, bf16[256,128]{1,0:T(8,128)(2,1)S(1)}, u32[]{:S(2)}, u32[]{:S(2)}) collective-permute-start(bf16[256,128]{1,0:T(8,128)(2,1)S(1)} %get-tuple-element.37), channel_id=1, source_target_pairs={{0,12},{1,13},{2,14},{3,15},{4,8},{5,9},{6,10},{7,11},{8,4},{9,5},... | collective-permute-start | bytes 196616 | tf_op jit(solution)/shard_map/ppermute | solution.py:283
  38.7 5.9 %collective-permute-start.20 = (bf16[256,128]{1,0:T(8,128)(2,1)S(1)}, bf16[256,128]{1,0:T(8,128)(2,1)S(1)}, u32[]{:S(2)}, u32[]{:S(2)}) collective-permute-start(bf16[256,128]{1,0:T(8,128)(2,1)S(1)} %fusion.1), channel_id=1, source_target_pairs={{0,7},{1,6},{2,5},{3,4},{4,3},{5,2},{6,1},{7,0},{8,15},{9,14},{10,... | collective-permute-start | bytes 196616 | tf_op jit(solution)/shard_map/ppermute | solution.py:283
  41.4 3.8 %collective-permute-start.16 = (bf16[256,128]{1,0:T(8,128)(2,1)S(1)}, bf16[256,128]{1,0:T(8,128)(2,1)S(1)}, u32[]{:S(2)}, u32[]{:S(2)}) collective-permute-start(bf16[256,128]{1,0:T(8,128)(2,1)S(1)} %get-tuple-element.36), channel_id=1, source_target_pairs={{0,12},{1,13},{2,14},{3,15},{4,8},{5,9},{6,10},{7,11},{8,4},{9,5},... | collective-permute-start | bytes 196616 | tf_op jit(solution)/shard_map/ppermute | solution.py:283
  42.4 4.1 %collective-permute-start.19 = (bf16[256,128]{1,0:T(8,128)(2,1)S(1)}, bf16[256,128]{1,0:T(8,128)(2,1)S(1)}, u32[]{:S(2)}, u32[]{:S(2)}) collective-permute-start(bf16[256,128]{1,0:T(8,128)(2,1)S(1)} %fusion.4), channel_id=1, source_target_pairs={{0,5},{1,4},{2,7},{3,6},{4,1},{5,0},{6,3},{7,2},{8,13},{9,12},{10,... | collective-permute-start | bytes 196616 | tf_op jit(solution)/shard_map/ppermute | solution.py:283

commit v5 on v4

--- a/solution.py
+++ b/solution.py
@@ -147,11 +147,14 @@
     return [ref.at[k] for group in groups for k in range(group[0].shape[0]) for ref in group]
 
 
-def early_kernel(slots, ways, bases, own_ref, place_ref, *refs):
+def early_kernel(slots, ways, bases, more, own_ref, place_ref, *refs):
     near, (kern_ref, msg_ref, proj_ref) = refs[:-3], refs[-3:]
-    build(slots, bases, own_ref.at[0], place_ref, pick((own_ref,) + near, ways), kern_ref, proj_ref)
+    blocks = pick(near[1:] if more else (own_ref,) + near, ways)
+    build(slots, bases, own_ref.at[0], place_ref, blocks, kern_ref, proj_ref)
     rows = kern_ref.shape[0] // 3
     for m, part in enumerate(gather(kern_ref, proj_ref)):
+        if more:
+            part = part + near[0][m * rows : (m + 1) * rows, :]
         msg_ref[m * rows : (m + 1) * rows, :] = part
 
 
@@ -219,21 +222,22 @@
     return [struct(count, width, atoms, dtype=jnp.float32)] + [struct(count, width, atoms)] * (ways - 1)
 
 
-def call_early(slots, ways, bases, own, place, near):
+def call_early(slots, ways, bases, own, place, near, before=None):
     atoms, width = near[0].shape[2], near[0].shape[1] - TAIL
     rows, columns = (bases + 3) * atoms, len(slots) * atoms
+    more = [] if before is None else [before]
     return pl.pallas_call(
-        functools.partial(early_kernel, slots, ways, bases),
+        functools.partial(early_kernel, slots, ways, bases, bool(more)),
         out_shape=[struct(rows, columns), struct(rows, width, dtype=jnp.float32)],
-        in_specs=[VMEM, SMEM] + [VMEM] * len(near),
+        in_specs=[VMEM, SMEM] + [VMEM] * (len(more) + len(near)),
         out_specs=[VMEM] * 2,
         scratch_shapes=[pltpu.VMEM((columns, width), jnp.bfloat16)],
         compiler_params=LIMIT,
         cost_estimate=pl.CostEstimate(
             flops=10 * rows * columns * width, bytes_accessed=8 * rows * columns, transcendentals=2 * atoms * columns
         ),
-        name="early",
-    )(own, place, *near)
+        name="early" if before is None else "side",
+    )(own, place, *more, *near)
 
 
 def call_main(slots, ways, bases, own, place, readouts, near, before=(), side=0):
@@ -300,7 +304,7 @@
     x1 = swap(message, "gx", 1)
     z1 = swap(message, "gz", 1)
     z3 = swap(message, "gz", 3)
-    x3 = swap(after(x1, z1), "gx", 2)
+    x3 = swap(x1, "gx", 2)
     x1z1 = swap(z1, "gx", 1)
     x1z3 = swap(z3, "gx", 1)
     x3z1 = swap(x1z1, "gx", 2)
@@ -310,17 +314,20 @@
         held, other = (0, None) if hops % 2 == 0 else (None, 0)
         return [(x, held, z), (x, other, z)]
     near_slots = both(0, 0, 0) + both("1", 0, 1) + both("-1", 0, 2) + both(0, "1", 1) + both(0, "-1", 1)
+    side_slots = both("1", "1", 2) + both("-1", "1", 3)
+    far_slots = both("1", "-1", 2) + both("-1", "-1", 3)
     near = jnp.stack([x1, x3, z1, z3])
-    own, rest = message[None], [core(message)[None], near, core(after(near, x1z3))]
+    echo = core(message[None])
+    own, rest = core(echo), [echo, near, core(near)]
+    kern, before = call_early(near_slots, 2, bases, own, place, rest)
     side = jnp.stack([x1z1, x3z1])
-    rest += [side, core(after(side, x1z3))]
-    near_slots += both("1", "1", 2) + both("-1", "1", 3)
-    far_slots = both("1", "-1", 2) + both("-1", "-1", 3)
-    kern, before = call_early(near_slots, 2, bases, own, place, rest)
-    x3z3 = after(x3z3, before)
+    side = [side, core(side)]
+    x1z3, x3z3, _ = lax.optimization_barrier((x1z3, x3z3, before))
+    side[0], side[1], _ = lax.optimization_barrier((side[0], side[1], x3z3))
+    kern_side, before = call_early(side_slots, 2, bases, own, place, side, before)
     far = jnp.stack([x1z3, x3z3])
     far = [far, core(far)]
-    pred, right, far_held, far_sent = call_main(far_slots, 2, bases, own, place, readouts, far, (before, kern), 2)
+    pred, right, far_held, far_sent = call_main(far_slots, 2, bases, own, place, readouts, far, (before, kern_side), 2)
     far_sum = far_held + core(far_sent)
     near_held, near_sent = call_late(right, kern, 5, 2, atoms)
     near_sum = near_held + core(near_sent)

time: 47.6 us -> 47.2 us (level)
  waiting for transfers between devices: 12.4 us -> 11 us
  Pallas kernels: 8.61 us -> 9.66 us
  local copies, waits for them, and re-layouts: 0.92 us -> 0.05 us
  starting transfers between devices: 22.8 us -> 23.6 us
    ppermute x6 -> x7, waiting for transfers between devices: 1.25 us -> 0.1 us  [core(): return lax.ppermute(block, 'gy', [(0, 1), (1, 0)])]
    pallas_call x1 -> x2, Pallas kernels: 2.9 us -> 3.93 us  [call_early(): pl.pallas_call(functools.partial(early_kernel, slots, ways, bases, bool(m...]
    unnamed x14 -> x10, local copies, waits for them, and re-layouts: 0.9 us -> 0.03 us
    ppermute x6 -> x7, starting transfers between devices: 1.48 us -> 1.99 us  [core(): return lax.ppermute(block, 'gy', [(0, 1), (1, 0)])]
  transfers between devices with their start and end apart: 21 -> 22, of which waited for: 9 -> 9; matrix products, arithmetic and copies ran while one was open for 1% -> 1% of each run, Pallas kernels for 8% -> 11%
where the time goes in v5:
time: 47.2 us; the launch traced here: 47 us
  starting transfers between devices  23.6 us (50%)
  waiting for transfers between devices  11 us (23%)
  Pallas kernels  9.66 us (20%)
  between operations  1.48 us (3%)
  matrix products  0.87 us (2%)
    ppermute x15, starting transfers between devices, swap(): return lax.ppermute(block, AXES, pairs)  21.6 us
    ppermute x15, waiting for transfers between devices, swap(): return lax.ppermute(block, AXES, pairs)  10.9 us
    pallas_call x2, Pallas kernels, call_early(): pl.pallas_call(functools.partial(early_kernel, slots, ways, bases, bool(m...  3.93 us
    pallas_call x1, Pallas kernels, call_main(): pl.pallas_call(functools.partial(main_kernel, slots, ways, bases, len(nea...  2.96 us
    ppermute x7, starting transfers between devices, core(): return lax.ppermute(block, 'gy', [(0, 1), (1, 0)])  1.99 us
    pallas_call x1, Pallas kernels, on_device(): pl.pallas_call(message_kernel, out_shape=struct(width + TAIL, atoms), in_...  1.71 us
    pallas_call x1, Pallas kernels, call_late(): pl.pallas_call(late_kernel, out_shape=out_shape, in_specs=[VMEM] * 2, out...  1.06 us
  transfers between devices with their start and end apart: 22, of which 9 were waited for; matrix products, arithmetic and copies ran while one was open for 1% of the time, Pallas kernels for 11%

profile of v5, /device:TPU:0, one launch (start us, length us, event | category | flops | bytes accessed | tf_op | source)
XLA Modules:
  0.0 47.0 jit_solution(16308326156842109273)
XLA Ops:
  1.3 1.7 %message.1 = bf16[272,128]{1,0:T(8,128)(2,1)} custom-call(bf16[128,256]{1,0:T(8,128)(2,1)} %bitcast.71, bf16[256,256]{1,0:T(8,128)(2,1)} %w_ref.1, f32[3,1,128]{2,1,0:T(1,128)} %bitcast.72, s32[1,1]{1,0:T(1,128)} %bitcast.58.counts_ref), custom_call_target="tpu_custom_call" | custom-call | tf_op jit(solution)/shard_map/message/pallas_call | solution.py:372
  3.0 2.4 %collective-permute-start.5 = (bf16[272,128]{1,0:T(8,128)(2,1)}, bf16[272,128]{1,0:T(8,128)(2,1)S(1)}, u32[]{:S(2)}, u32[]{:S(2)}) collective-permute-start(bf16[272,128]{1,0:T(8,128)(2,1)} %message.1), channel_id=1, source_target_pairs={{0,12},{1,13},{2,14},{3,15},{4,8},{5,9},{6,10},{7,11},{8,4},{9,5},... | collective-permute-start | bytes 208904 | tf_op jit(solution)/shard_map/ppermute | solution.py:287
  5.4 1.9 %collective-permute-start.7 = (bf16[272,128]{1,0:T(8,128)(2,1)}, bf16[272,128]{1,0:T(8,128)(2,1)S(1)}, u32[]{:S(2)}, u32[]{:S(2)}) collective-permute-start(bf16[272,128]{1,0:T(8,128)(2,1)} %message.1), channel_id=1, source_target_pairs={{0,5},{1,4},{2,7},{3,6},{4,1},{5,0},{6,3},{7,2},{8,13},{9,12},{10,... | collective-permute-start | bytes 208904 | tf_op jit(solution)/shard_map/ppermute | solution.py:287
  7.2 2.0 %collective-permute-start.2 = (bf16[272,128]{1,0:T(8,128)(2,1)}, bf16[272,128]{1,0:T(8,128)(2,1)S(1)}, u32[]{:S(2)}, u32[]{:S(2)}) collective-permute-start(bf16[272,128]{1,0:T(8,128)(2,1)} %message.1), channel_id=1, source_target_pairs={{0,7},{1,6},{2,5},{3,4},{4,3},{5,2},{6,1},{7,0},{8,15},{9,14},{10,... | collective-permute-start | bytes 208904 | tf_op jit(solution)/shard_map/ppermute | solution.py:287
  9.3 1.7 %collective-permute-start.6 = (bf16[272,128]{1,0:T(8,128)(2,1)S(1)}, bf16[272,128]{1,0:T(8,128)(2,1)S(1)}, u32[]{:S(2)}, u32[]{:S(2)}) collective-permute-start(bf16[272,128]{1,0:T(8,128)(2,1)S(1)} %collective-permute-done.5), channel_id=1, source_target_pairs={{0,20},{1,21},{2,22},{3,23},{4,16},{5,17},{6,18},{7,19},{8,28},{9,... | collective-permute-start | bytes 208904 | tf_op jit(solution)/shard_map/ppermute | solution.py:287
  10.9 0.9 %collective-permute-start.10 = (bf16[272,128]{1,0:T(8,128)(2,1)S(1)}, bf16[272,128]{1,0:T(8,128)(2,1)S(1)}, u32[]{:S(2)}, u32[]{:S(2)}) collective-permute-start(bf16[272,128]{1,0:T(8,128)(2,1)S(1)} %collective-permute-done.7), channel_id=1, source_target_pairs={{0,12},{1,13},{2,14},{3,15},{4,8},{5,9},{6,10},{7,11},{8,4},{9,5},... | collective-permute-start | bytes 208904 | tf_op jit(solution)/shard_map/ppermute | solution.py:287
  11.9 1.9 %collective-permute-done.2 = bf16[272,128]{1,0:T(8,128)(2,1)S(1)} collective-permute-done((bf16[272,128]{1,0:T(8,128)(2,1)}, bf16[272,128]{1,0:T(8,128)(2,1)S(1)}, u32[]{:S(2)}, u32[]{:S(2)}) %collective-permute-start.2) | collective-permute-done | bytes 69664 | tf_op jit(solution)/shard_map/ppermute | solution.py:287
  13.9 0.5 collective-permute-start
  14.4 1.0 %collective-permute-start.3 = (bf16[272,128]{1,0:T(8,128)(2,1)S(1)}, bf16[272,128]{1,0:T(8,128)(2,1)S(1)}, u32[]{:S(2)}, u32[]{:S(2)}) collective-permute-start(bf16[272,128]{1,0:T(8,128)(2,1)S(1)} %collective-permute-done.2), channel_id=1, source_target_pairs={{0,12},{1,13},{2,14},{3,15},{4,8},{5,9},{6,10},{7,11},{8,4},{9,5},... | collective-permute-start | bytes 208904 | tf_op jit(solution)/shard_map/ppermute | solution.py:287
  15.4 1.2 %collective-permute-start.11 = (bf16[272,128]{1,0:T(8,128)(2,1)S(1)}, bf16[272,128]{1,0:T(8,128)(2,1)S(1)}, u32[]{:S(2)}, u32[]{:S(2)}) collective-permute-start(bf16[272,128]{1,0:T(8,128)(2,1)S(1)} %collective-permute-done.10), channel_id=1, source_target_pairs={{0,20},{1,21},{2,22},{3,23},{4,16},{5,17},{6,18},{7,19},{8,28},{9,... | collective-permute-start | bytes 208904 | tf_op jit(solution)/shard_map/ppermute | solution.py:287
  16.7 0.2 collective-permute-start.1
  16.9 1.7 %collective-permute-done.3 = bf16[272,128]{1,0:T(8,128)(2,1)S(1)} collective-permute-done((bf16[272,128]{1,0:T(8,128)(2,1)S(1)}, bf16[272,128]{1,0:T(8,128)(2,1)S(1)}, u32[]{:S(2)}, u32[]{:S(2)}) %collective-permute-start.3) | collective-permute-done | bytes 69664 | tf_op jit(solution)/shard_map/ppermute | solution.py:287
  18.6 1.5 %collective-permute-start.4 = (bf16[272,128]{1,0:T(8,128)(2,1)S(1)}, bf16[272,128]{1,0:T(8,128)(2,1)S(1)}, u32[]{:S(2)}, u32[]{:S(2)}) collective-permute-start(bf16[272,128]{1,0:T(8,128)(2,1)S(1)} %collective-permute-done.3), channel_id=1, source_target_pairs={{0,20},{1,21},{2,22},{3,23},{4,16},{5,17},{6,18},{7,19},{8,28},{9,... | collective-permute-start | bytes 208904 | tf_op jit(solution)/shard_map/ppermute | solution.py:287
  20.1 0.2 collective-permute-start.12
  20.4 2.5 %early.1 = (bf16[1152,1280]{1,0:T(8,128)(2,1)S(1)}, f32[1152,256]{1,0:T(8,128)S(1)}) custom-call(bf16[1,272,128]{2,1,0:T(8,128)(2,1)S(1)} %collective-permute-done.1.own_ref, s32[2]{0:T(128)S(1)} %pad_add_fusion.place_ref, bf16[1,272,128]{2,1,0:T(8,128)(2,1)S(1)} %collective-permute-done.refs_0_, bf16[4,272,128]{2,1,0:T(8,128)(2,1)S(1)} %pad_maximum_fusion.refs_1_, ...), custom_call_target="tpu_custom_call" | custom-call | flops 3774873600 | bytes 11796480 | tf_op jit(solution)/shard_map/early/pallas_call | solution.py:229
  22.9 0.4 collective-permute-start.9
  23.4 1.4 %side.1 = (bf16[1152,512]{1,0:T(8,128)(2,1)S(1)}, f32[1152,256]{1,0:T(8,128)S(1)}) custom-call(bf16[1,272,128]{2,1,0:T(8,128)(2,1)S(1)} %collective-permute-done.1.own_ref, s32[2]{0:T(128)S(1)} %pad_add_fusion.place_ref, f32[1152,256]{1,0:T(8,128)S(1)} %get-tuple-element.18.refs_0_, bf16[2,272,128]{2,1,0:T(8,128)(2,1)S(1)} %pad_maximum_fusion.2.refs_1_, ...), custom_call_target="tpu_custom_call" | custom-call | flops 1509949440 | bytes 4718592 | tf_op jit(solution)/shard_map/side/pallas_call | solution.py:229
  24.9 3.0 %main.1 = (f32[3,1,128]{2,1,0:T(1,128)}, bf16[1152,256]{1,0:T(8,128)(2,1)S(1)}, f32[4,256,128]{2,1,0:T(8,128)S(1)}, bf16[4,256,128]{2,1,0:T(8,128)(2,1)S(1)}) custom-call(bf16[1,272,128]{2,1,0:T(8,128)(2,1)S(1)} %collective-permute-done.1.own_ref, s32[2]{0:T(128)S(1)} %pad_add_fusion.place_ref, s32[1,128]{1,0:T(1,128)S(1)} %bitcast.61, ...), custom_call_target="tpu_custom_call" | custom-call | tf_op jit(solution)/shard_map/main/pallas_call | solution.py:251
  28.0 1.1 %late.1 = (f32[5,256,128]{2,1,0:T(8,128)S(1)}, bf16[5,256,128]{2,1,0:T(8,128)(2,1)S(1)}) custom-call(bf16[1152,256]{1,0:T(8,128)(2,1)S(1)} %get-tuple-element.26.right_ref, bf16[1152,1280]{1,0:T(8,128)(2,1)S(1)} %get-tuple-element.27.kern_ref), custom_call_target="tpu_custom_call" | custom-call | flops 754974720 | bytes 2949120 | tf_op jit(solution)/shard_map/late/pallas_call | solution.py:266
  29.1 0.4 collective-permute-start.13
  29.6 1.1 %collective-permute-start.16 = (bf16[256,128]{1,0:T(8,128)(2,1)S(1)}, bf16[256,128]{1,0:T(8,128)(2,1)S(1)}, u32[]{:S(2)}, u32[]{:S(2)}) collective-permute-start(bf16[256,128]{1,0:T(8,128)(2,1)S(1)} %get-tuple-element.39), channel_id=1, source_target_pairs={{0,20},{1,21},{2,22},{3,23},{4,16},{5,17},{6,18},{7,19},{8,28},{9,... | collective-permute-start | bytes 196616 | tf_op jit(solution)/shard_map/ppermute | solution.py:287
  30.9 1.2 %collective-permute-start.15 = (bf16[2,256,128]{2,1,0:T(8,128)(2,1)S(1)}, bf16[2,256,128]{2,1,0:T(8,128)(2,1)S(1)}, u32[]{:S(2)}, u32[]{:S(2)}) collective-permute-start(bf16[2,256,128]{2,1,0:T(8,128)(2,1)S(1)} %pad_maximum_fusion.3), channel_id=1, source_target_pairs={{0,20},{1,21},{2,22},{3,23},{4,16},{5,17},{6,18},{7,19},{8,28},{9,... | collective-permute-start | bytes 393224 | tf_op jit(solution)/shard_map/ppermute | solution.py:287
  32.1 1.6 %collective-permute-done.16 = bf16[256,128]{1,0:T(8,128)(2,1)S(1)} collective-permute-done((bf16[256,128]{1,0:T(8,128)(2,1)S(1)}, bf16[256,128]{1,0:T(8,128)(2,1)S(1)}, u32[]{:S(2)}, u32[]{:S(2)}) %collective-permute-start.16) | collective-permute-done | bytes 65568 | tf_op jit(solution)/shard_map/ppermute | solution.py:287
  33.7 1.2 %collective-permute-start.19 = (bf16[256,128]{1,0:T(8,128)(2,1)S(1)}, bf16[256,128]{1,0:T(8,128)(2,1)S(1)}, u32[]{:S(2)}, u32[]{:S(2)}) collective-permute-start(bf16[256,128]{1,0:T(8,128)(2,1)S(1)} %fusion.6), channel_id=1, source_target_pairs={{0,12},{1,13},{2,14},{3,15},{4,8},{5,9},{6,10},{7,11},{8,4},{9,5},... | collective-permute-start | bytes 196616 | tf_op jit(solution)/shard_map/ppermute | solution.py:287
  35.0 1.5 %collective-permute-done.15 = bf16[2,256,128]{2,1,0:T(8,128)(2,1)S(1)} collective-permute-done((bf16[2,256,128]{2,1,0:T(8,128)(2,1)S(1)}, bf16[2,256,128]{2,1,0:T(8,128)(2,1)S(1)}, u32[]{:S(2)}, u32[]{:S(2)}) %collective-permute-start.15) | collective-permute-done | bytes 131104 | tf_op jit(solution)/shard_map/ppermute | solution.py:287
  36.5 0.9 %collective-permute-start.18 = (bf16[256,128]{1,0:T(8,128)(2,1)S(1)}, bf16[256,128]{1,0:T(8,128)(2,1)S(1)}, u32[]{:S(2)}, u32[]{:S(2)}) collective-permute-start(bf16[256,128]{1,0:T(8,128)(2,1)S(1)} %get-tuple-element.41), channel_id=1, source_target_pairs={{0,12},{1,13},{2,14},{3,15},{4,8},{5,9},{6,10},{7,11},{8,4},{9,5},... | collective-permute-start | bytes 196616 | tf_op jit(solution)/shard_map/ppermute | solution.py:287
  37.5 3.5 %collective-permute-start.21 = (bf16[256,128]{1,0:T(8,128)(2,1)S(1)}, bf16[256,128]{1,0:T(8,128)(2,1)S(1)}, u32[]{:S(2)}, u32[]{:S(2)}) collective-permute-start(bf16[256,128]{1,0:T(8,128)(2,1)S(1)} %fusion.1), channel_id=1, source_target_pairs={{0,7},{1,6},{2,5},{3,4},{4,3},{5,2},{6,1},{7,0},{8,15},{9,14},{10,... | collective-permute-start | bytes 196616 | tf_op jit(solution)/shard_map/ppermute | solution.py:287
  41.0 0.9 %collective-permute-start.17 = (bf16[256,128]{1,0:T(8,128)(2,1)S(1)}, bf16[256,128]{1,0:T(8,128)(2,1)S(1)}, u32[]{:S(2)}, u32[]{:S(2)}) collective-permute-start(bf16[256,128]{1,0:T(8,128)(2,1)S(1)} %get-tuple-element.40), channel_id=1, source_target_pairs={{0,12},{1,13},{2,14},{3,15},{4,8},{5,9},{6,10},{7,11},{8,4},{9,5},... | collective-permute-start | bytes 196616 | tf_op jit(solution)/shard_map/ppermute | solution.py:287
  42.0 1.5 %collective-permute-done.21 = bf16[256,128]{1,0:T(8,128)(2,1)S(1)} collective-permute-done((bf16[256,128]{1,0:T(8,128)(2,1)S(1)}, bf16[256,128]{1,0:T(8,128)(2,1)S(1)}, u32[]{:S(2)}, u32[]{:S(2)}) %collective-permute-start.21) | collective-permute-done | bytes 65568 | tf_op jit(solution)/shard_map/ppermute | solution.py:287
  43.5 1.3 %collective-permute-done.17 = bf16[256,128]{1,0:T(8,128)(2,1)S(1)} collective-permute-done((bf16[256,128]{1,0:T(8,128)(2,1)S(1)}, bf16[256,128]{1,0:T(8,128)(2,1)S(1)}, u32[]{:S(2)}, u32[]{:S(2)}) %collective-permute-start.17) | collective-permute-done | bytes 65568 | tf_op jit(solution)/shard_map/ppermute | solution.py:287
  44.8 1.3 %collective-permute-done.20 = bf16[256,128]{1,0:T(8,128)(2,1)S(1)} collective-permute-done((bf16[256,128]{1,0:T(8,128)(2,1)S(1)}, bf16[256,128]{1,0:T(8,128)(2,1)S(1)}, u32[]{:S(2)}, u32[]{:S(2)}) %collective-permute-start.20) | collective-permute-done | bytes 65568 | tf_op jit(solution)/shard_map/ppermute | solution.py:287
  46.1 0.9 %convolution_bitcast_fusion = f32[1,1,1,128,256]{4,3,2,1,0:T(8,128)} fusion(bf16[256,256]{1,0:T(8,128)(2,1)S(1)} %copy-done.4, f32[5,256,128]{2,1,0:T(8,128)S(1)} %convert_add_fusion, bf16[256,128]{1,0:T(8,128)(2,1)S(1)} %collective-permute-done.21, bf16[256,128]{1,0:T(8,128)(2,1)S(1)} %collective-permute-done.20, bf16[256,128]{1,0:T(8,128)(2,1)S(1)} %collective-permute-done.17), kind=kOutput, calls=%fused_computation | convolution fusion | flops 17006592 | bytes 589824 | tf_op jit(solution)/shard_map/dot_general | solution.py:382
  (41 shorter events, 1.0 us)
Async XLA Ops:
  3.0 6.3 %collective-permute-start.5 = (bf16[272,128]{1,0:T(8,128)(2,1)}, bf16[272,128]{1,0:T(8,128)(2,1)S(1)}, u32[]{:S(2)}, u32[]{:S(2)}) collective-permute-start(bf16[272,128]{1,0:T(8,128)(2,1)} %message.1), channel_id=1, source_target_pairs={{0,12},{1,13},{2,14},{3,15},{4,8},{5,9},{6,10},{7,11},{8,4},{9,5},... | collective-permute-start | bytes 208904 | tf_op jit(solution)/shard_map/ppermute | solution.py:287
  5.4 5.6 %collective-permute-start.7 = (bf16[272,128]{1,0:T(8,128)(2,1)}, bf16[272,128]{1,0:T(8,128)(2,1)S(1)}, u32[]{:S(2)}, u32[]{:S(2)}) collective-permute-start(bf16[272,128]{1,0:T(8,128)(2,1)} %message.1), channel_id=1, source_target_pairs={{0,5},{1,4},{2,7},{3,6},{4,1},{5,0},{6,3},{7,2},{8,13},{9,12},{10,... | collective-permute-start | bytes 208904 | tf_op jit(solution)/shard_map/ppermute | solution.py:287
  7.2 6.6 %collective-permute-start.2 = (bf16[272,128]{1,0:T(8,128)(2,1)}, bf16[272,128]{1,0:T(8,128)(2,1)S(1)}, u32[]{:S(2)}, u32[]{:S(2)}) collective-permute-start(bf16[272,128]{1,0:T(8,128)(2,1)} %message.1), channel_id=1, source_target_pairs={{0,7},{1,6},{2,5},{3,4},{4,3},{5,2},{6,1},{7,0},{8,15},{9,14},{10,... | collective-permute-start | bytes 208904 | tf_op jit(solution)/shard_map/ppermute | solution.py:287
  9.3 4.5 %collective-permute-start.6 = (bf16[272,128]{1,0:T(8,128)(2,1)S(1)}, bf16[272,128]{1,0:T(8,128)(2,1)S(1)}, u32[]{:S(2)}, u32[]{:S(2)}) collective-permute-start(bf16[272,128]{1,0:T(8,128)(2,1)S(1)} %collective-permute-done.5), channel_id=1, source_target_pairs={{0,20},{1,21},{2,22},{3,23},{4,16},{5,17},{6,18},{7,19},{8,28},{9,... | collective-permute-start | bytes 208904 | tf_op jit(solution)/shard_map/ppermute | solution.py:287
  10.9 4.5 %collective-permute-start.10 = (bf16[272,128]{1,0:T(8,128)(2,1)S(1)}, bf16[272,128]{1,0:T(8,128)(2,1)S(1)}, u32[]{:S(2)}, u32[]{:S(2)}) collective-permute-start(bf16[272,128]{1,0:T(8,128)(2,1)S(1)} %collective-permute-done.7), channel_id=1, source_target_pairs={{0,12},{1,13},{2,14},{3,15},{4,8},{5,9},{6,10},{7,11},{8,4},{9,5},... | collective-permute-start | bytes 208904 | tf_op jit(solution)/shard_map/ppermute | solution.py:287
  13.8 6.5 %collective-permute-start.8 = (bf16[4,272,128]{2,1,0:T(8,128)(2,1)S(1)}, bf16[4,272,128]{2,1,0:T(8,128)(2,1)S(1)}, u32[]{:S(2)}, u32[]{:S(2)}) collective-permute-start(bf16[4,272,128]{2,1,0:T(8,128)(2,1)S(1)} %pad_maximum_fusion.refs_1_), channel_id=1, source_target_pairs={{0,4},{4,0},{1,5},{5,1},{2,6},{6,2},{3,7},{7,3},{8,12},{12,8},{9,1... | collective-permute-start | bytes 835592 | tf_op jit(solution)/shard_map/ppermute | solution.py:291
  13.9 2.8 %collective-permute-start = (bf16[1,272,128]{2,1,0:T(8,128)(2,1)}, bf16[1,272,128]{2,1,0:T(8,128)(2,1)S(1)}, u32[]{:S(2)}, u32[]{:S(2)}) collective-permute-start(bf16[1,272,128]{2,1,0:T(8,128)(2,1)} %bitcast.66), channel_id=1, source_target_pairs={{0,4},{4,0},{1,5},{5,1},{2,6},{6,2},{3,7},{7,3},{8,12},{12,8},{9,1... | collective-permute-start | bytes 208904 | tf_op jit(solution)/shard_map/ppermute | solution.py:291
  14.4 4.2 %collective-permute-start.3 = (bf16[272,128]{1,0:T(8,128)(2,1)S(1)}, bf16[272,128]{1,0:T(8,128)(2,1)S(1)}, u32[]{:S(2)}, u32[]{:S(2)}) collective-permute-start(bf16[272,128]{1,0:T(8,128)(2,1)S(1)} %collective-permute-done.2), channel_id=1, source_target_pairs={{0,12},{1,13},{2,14},{3,15},{4,8},{5,9},{6,10},{7,11},{8,4},{9,5},... | collective-permute-start | bytes 208904 | tf_op jit(solution)/shard_map/ppermute | solution.py:287
  15.4 4.7 %collective-permute-start.11 = (bf16[272,128]{1,0:T(8,128)(2,1)S(1)}, bf16[272,128]{1,0:T(8,128)(2,1)S(1)}, u32[]{:S(2)}, u32[]{:S(2)}) collective-permute-start(bf16[272,128]{1,0:T(8,128)(2,1)S(1)} %collective-permute-done.10), channel_id=1, source_target_pairs={{0,20},{1,21},{2,22},{3,23},{4,16},{5,17},{6,18},{7,19},{8,28},{9,... | collective-permute-start | bytes 208904 | tf_op jit(solution)/shard_map/ppermute | solution.py:287
  16.7 3.6 %collective-permute-start.1 = (bf16[1,272,128]{2,1,0:T(8,128)(2,1)S(1)}, bf16[1,272,128]{2,1,0:T(8,128)(2,1)S(1)}, u32[]{:S(2)}, u32[]{:S(2)}) collective-permute-start(bf16[1,272,128]{2,1,0:T(8,128)(2,1)S(1)} %collective-permute-done.refs_0_), channel_id=1, source_target_pairs={{0,4},{4,0},{1,5},{5,1},{2,6},{6,2},{3,7},{7,3},{8,12},{12,8},{9,1... | collective-permute-start | bytes 208904 | tf_op jit(solution)/shard_map/ppermute | solution.py:291
  18.6 4.2 %collective-permute-start.4 = (bf16[272,128]{1,0:T(8,128)(2,1)S(1)}, bf16[272,128]{1,0:T(8,128)(2,1)S(1)}, u32[]{:S(2)}, u32[]{:S(2)}) collective-permute-start(bf16[272,128]{1,0:T(8,128)(2,1)S(1)} %collective-permute-done.3), channel_id=1, source_target_pairs={{0,20},{1,21},{2,22},{3,23},{4,16},{5,17},{6,18},{7,19},{8,28},{9,... | collective-permute-start | bytes 208904 | tf_op jit(solution)/shard_map/ppermute | solution.py:287
  20.1 2.7 %collective-permute-start.12 = (bf16[2,272,128]{2,1,0:T(8,128)(2,1)S(1)}, bf16[2,272,128]{2,1,0:T(8,128)(2,1)S(1)}, u32[]{:S(2)}, u32[]{:S(2)}) collective-permute-start(bf16[2,272,128]{2,1,0:T(8,128)(2,1)S(1)} %pad_maximum_fusion.2.refs_1_), channel_id=1, source_target_pairs={{0,4},{4,0},{1,5},{5,1},{2,6},{6,2},{3,7},{7,3},{8,12},{12,8},{9,1... | collective-permute-start | bytes 417800 | tf_op jit(solution)/shard_map/ppermute | solution.py:291
  22.9 1.9 %copy-start = (f32[6,256]{1,0:T(8,128)S(1)}, f32[6,256]{1,0:T(8,128)}, u32[]{:S(2)}) copy-start(f32[6,256]{1,0:T(8,128)} %radial_ref.1) | copy-start | bytes 18436
  22.9 1.9 %copy-start.1 = (f32[1,1,1,3,128]{4,2,3,1,0:T(1,128)S(1)}, f32[1,1,1,3,128]{4,2,3,1,0:T(1,128)}, u32[]{:S(2)}) copy-start(f32[1,1,1,3,128]{4,2,3,1,0:T(1,128)} %param.12) | copy-start | bytes 4612
  22.9 1.9 %copy-start.2 = (f32[256]{0:T(256)S(1)}, f32[256]{0:T(256)}, u32[]{:S(2)}) copy-start(f32[256]{0:T(256)} %param.15) | copy-start | bytes 3076
  22.9 1.9 %copy-start.3 = (s32[1,1,1,128]{3,2,1,0:T(1,128)S(1)}, s32[1,1,1,128]{3,2,1,0:T(1,128)}, u32[]{:S(2)}) copy-start(s32[1,1,1,128]{3,2,1,0:T(1,128)} %param.11) | copy-start | bytes 1540
  22.9 1.9 %collective-permute-start.9 = (bf16[2,272,128]{2,1,0:T(8,128)(2,1)S(1)}, bf16[2,272,128]{2,1,0:T(8,128)(2,1)S(1)}, u32[]{:S(2)}, u32[]{:S(2)}) collective-permute-start(bf16[2,272,128]{2,1,0:T(8,128)(2,1)S(1)} %pad_maximum_fusion.1.refs_0_), channel_id=1, source_target_pairs={{0,4},{4,0},{1,5},{5,1},{2,6},{6,2},{3,7},{7,3},{8,12},{12,8},{9,1... | collective-permute-start | bytes 417800 | tf_op jit(solution)/shard_map/ppermute | solution.py:291
  27.8 1.6 %collective-permute-start.14 = (bf16[4,256,128]{2,1,0:T(8,128)(2,1)S(1)}, bf16[4,256,128]{2,1,0:T(8,128)(2,1)S(1)}, u32[]{:S(2)}, u32[]{:S(2)}) collective-permute-start(bf16[4,256,128]{2,1,0:T(8,128)(2,1)S(1)} %get-tuple-element.31), channel_id=1, source_target_pairs={{0,4},{4,0},{1,5},{5,1},{2,6},{6,2},{3,7},{7,3},{8,12},{12,8},{9,1... | collective-permute-start | bytes 786440 | tf_op jit(solution)/shard_map/ppermute | solution.py:291
  29.1 1.7 %collective-permute-start.13 = (bf16[5,256,128]{2,1,0:T(8,128)(2,1)S(1)}, bf16[5,256,128]{2,1,0:T(8,128)(2,1)S(1)}, u32[]{:S(2)}, u32[]{:S(2)}) collective-permute-start(bf16[5,256,128]{2,1,0:T(8,128)(2,1)S(1)} %get-tuple-element.29), channel_id=1, source_target_pairs={{0,4},{4,0},{1,5},{5,1},{2,6},{6,2},{3,7},{7,3},{8,12},{12,8},{9,1... | collective-permute-start | bytes 983048 | tf_op jit(solution)/shard_map/ppermute | solution.py:291
  29.6 4.1 %collective-permute-start.16 = (bf16[256,128]{1,0:T(8,128)(2,1)S(1)}, bf16[256,128]{1,0:T(8,128)(2,1)S(1)}, u32[]{:S(2)}, u32[]{:S(2)}) collective-permute-start(bf16[256,128]{1,0:T(8,128)(2,1)S(1)} %get-tuple-element.39), channel_id=1, source_target_pairs={{0,20},{1,21},{2,22},{3,23},{4,16},{5,17},{6,18},{7,19},{8,28},{9,... | collective-permute-start | bytes 196616 | tf_op jit(solution)/shard_map/ppermute | solution.py:287
  30.8 15.3 %copy-start.4 = (bf16[256,256]{1,0:T(8,128)(2,1)S(1)}, bf16[256,256]{1,0:T(8,128)(2,1)}, u32[]{:S(2)}) copy-start(bf16[256,256]{1,0:T(8,128)(2,1)} %w_ref.1) | copy-start | bytes 393220
  30.9 5.6 %collective-permute-start.15 = (bf16[2,256,128]{2,1,0:T(8,128)(2,1)S(1)}, bf16[2,256,128]{2,1,0:T(8,128)(2,1)S(1)}, u32[]{:S(2)}, u32[]{:S(2)}) collective-permute-start(bf16[2,256,128]{2,1,0:T(8,128)(2,1)S(1)} %pad_maximum_fusion.3), channel_id=1, source_target_pairs={{0,20},{1,21},{2,22},{3,23},{4,16},{5,17},{6,18},{7,19},{8,28},{9,... | collective-permute-start | bytes 393224 | tf_op jit(solution)/shard_map/ppermute | solution.py:287
  33.7 3.8 %collective-permute-start.19 = (bf16[256,128]{1,0:T(8,128)(2,1)S(1)}, bf16[256,128]{1,0:T(8,128)(2,1)S(1)}, u32[]{:S(2)}, u32[]{:S(2)}) collective-permute-start(bf16[256,128]{1,0:T(8,128)(2,1)S(1)} %fusion.6), channel_id=1, source_target_pairs={{0,12},{1,13},{2,14},{3,15},{4,8},{5,9},{6,10},{7,11},{8,4},{9,5},... | collective-permute-start | bytes 196616 | tf_op jit(solution)/shard_map/ppermute | solution.py:287
  36.5 5.4 %collective-permute-start.18 = (bf16[256,128]{1,0:T(8,128)(2,1)S(1)}, bf16[256,128]{1,0:T(8,128)(2,1)S(1)}, u32[]{:S(2)}, u32[]{:S(2)}) collective-permute-start(bf16[256,128]{1,0:T(8,128)(2,1)S(1)} %get-tuple-element.41), channel_id=1, source_target_pairs={{0,12},{1,13},{2,14},{3,15},{4,8},{5,9},{6,10},{7,11},{8,4},{9,5},... | collective-permute-start | bytes 196616 | tf_op jit(solution)/shard_map/ppermute | solution.py:287
  37.5 6.0 %collective-permute-start.21 = (bf16[256,128]{1,0:T(8,128)(2,1)S(1)}, bf16[256,128]{1,0:T(8,128)(2,1)S(1)}, u32[]{:S(2)}, u32[]{:S(2)}) collective-permute-start(bf16[256,128]{1,0:T(8,128)(2,1)S(1)} %fusion.1), channel_id=1, source_target_pairs={{0,7},{1,6},{2,5},{3,4},{4,3},{5,2},{6,1},{7,0},{8,15},{9,14},{10,... | collective-permute-start | bytes 196616 | tf_op jit(solution)/shard_map/ppermute | solution.py:287
  41.0 3.8 %collective-permute-start.17 = (bf16[256,128]{1,0:T(8,128)(2,1)S(1)}, bf16[256,128]{1,0:T(8,128)(2,1)S(1)}, u32[]{:S(2)}, u32[]{:S(2)}) collective-permute-start(bf16[256,128]{1,0:T(8,128)(2,1)S(1)} %get-tuple-element.40), channel_id=1, source_target_pairs={{0,12},{1,13},{2,14},{3,15},{4,8},{5,9},{6,10},{7,11},{8,4},{9,5},... | collective-permute-start | bytes 196616 | tf_op jit(solution)/shard_map/ppermute | solution.py:287
  41.9 4.2 %collective-permute-start.20 = (bf16[256,128]{1,0:T(8,128)(2,1)S(1)}, bf16[256,128]{1,0:T(8,128)(2,1)S(1)}, u32[]{:S(2)}, u32[]{:S(2)}) collective-permute-start(bf16[256,128]{1,0:T(8,128)(2,1)S(1)} %fusion.4), channel_id=1, source_target_pairs={{0,5},{1,4},{2,7},{3,6},{4,1},{5,0},{6,3},{7,2},{8,13},{9,12},{10,... | collective-permute-start | bytes 196616 | tf_op jit(solution)/shard_map/ppermute | solution.py:287

commit v6 on v5

--- a/solution.py
+++ b/solution.py
@@ -336,17 +336,16 @@
     next3 = narrow(far_sum[2] + back3)
     back1 = after(back1, next3)
     next1 = narrow(far_sum[0] + back1[0])
-    back0 = back1[1]
-    next0 = narrow(near_sum[1] + back0)
+    next0 = narrow(near_sum[1] + back1[1])
     back3 = swap(next3, "gx", 1)
     back1 = swap(next1, "gx", 1)
     back0 = swap(next0, "gx", 1)
     next3 = narrow(near_sum[4] + back3)
-    back1 = after(back1, next3)
-    next1 = narrow(near_sum[3] + back1)
+    next1 = narrow(near_sum[3] + after(back1, next3))
+    start = near_sum[0] + back0
     back3 = swap(next3, "gz", 3)
-    back1 = swap(next1, "gz", 1)
-    return pred, near_sum[0] + back0 + back1 + back3
+    back1 = swap(after(next1, start), "gz", 1)
+    return pred, start + back1 + back3
 
 
 def exchange_any(message, bases, place, readouts):

time: 47.2 us -> 46.7 us (0.989)
  waiting for transfers between devices: 11 us -> 9.45 us
  starting transfers between devices: 23.6 us -> 24.7 us
    ppermute x15, waiting for transfers between devices: 10.9 us -> 9.4 us  [swap(): return lax.ppermute(block, AXES, pairs)]
    ppermute x15, starting transfers between devices: 21.6 us -> 22.7 us  [swap(): return lax.ppermute(block, AXES, pairs)]
  transfers between devices with their start and end apart: 22 -> 22, of which waited for: 9 -> 7; matrix products, arithmetic and copies ran while one was open for 1% -> 1% of each run, Pallas kernels for 11% -> 11%
where the time goes in v6:
time: 46.7 us; the launch traced here: 46.6 us
  starting transfers between devices  24.7 us (53%)
  Pallas kernels  9.62 us (21%)
  waiting for transfers between devices  9.45 us (20%)
  between operations  1.48 us (3%)
  matrix products  0.86 us (2%)
    ppermute x15, starting transfers between devices, swap(): return lax.ppermute(block, AXES, pairs)  22.7 us
    ppermute x15, waiting for transfers between devices, swap(): return lax.ppermute(block, AXES, pairs)  9.4 us
    pallas_call x2, Pallas kernels, call_early(): pl.pallas_call(functools.partial(early_kernel, slots, ways, bases, bool(m...  3.89 us
    pallas_call x1, Pallas kernels, call_main(): pl.pallas_call(functools.partial(main_kernel, slots, ways, bases, len(nea...  2.96 us
    ppermute x7, starting transfers between devices, core(): return lax.ppermute(block, 'gy', [(0, 1), (1, 0)])  1.99 us
    pallas_call x1, Pallas kernels, on_device(): pl.pallas_call(message_kernel, out_shape=struct(width + TAIL, atoms), in_...  1.71 us
    pallas_call x1, Pallas kernels, call_late(): pl.pallas_call(late_kernel, out_shape=out_shape, in_specs=[VMEM] * 2, out...  1.05 us
  transfers between devices with their start and end apart: 22, of which 7 were waited for; matrix products, arithmetic and copies ran while one was open for 1% of the time, Pallas kernels for 11%

profile of v6, /device:TPU:0, one launch (start us, length us, event | category | flops | bytes accessed | tf_op | source)
XLA Modules:
  0.0 46.6 jit_solution(10625600526431940658)
XLA Ops:
  1.3 1.7 %message.1 = bf16[272,128]{1,0:T(8,128)(2,1)} custom-call(bf16[128,256]{1,0:T(8,128)(2,1)} %bitcast.64, bf16[256,256]{1,0:T(8,128)(2,1)} %w_ref.1, f32[3,1,128]{2,1,0:T(1,128)} %bitcast.65, s32[1,1]{1,0:T(1,128)} %bitcast.51.counts_ref), custom_call_target="tpu_custom_call" | custom-call | tf_op jit(solution)/shard_map/message/pallas_call | solution.py:371
  3.0 2.4 %collective-permute-start.5 = (bf16[272,128]{1,0:T(8,128)(2,1)}, bf16[272,128]{1,0:T(8,128)(2,1)S(1)}, u32[]{:S(2)}, u32[]{:S(2)}) collective-permute-start(bf16[272,128]{1,0:T(8,128)(2,1)} %message.1), channel_id=1, source_target_pairs={{0,12},{1,13},{2,14},{3,15},{4,8},{5,9},{6,10},{7,11},{8,4},{9,5},... | collective-permute-start | bytes 208904 | tf_op jit(solution)/shard_map/ppermute | solution.py:287
  5.4 1.9 %collective-permute-start.7 = (bf16[272,128]{1,0:T(8,128)(2,1)}, bf16[272,128]{1,0:T(8,128)(2,1)S(1)}, u32[]{:S(2)}, u32[]{:S(2)}) collective-permute-start(bf16[272,128]{1,0:T(8,128)(2,1)} %message.1), channel_id=1, source_target_pairs={{0,5},{1,4},{2,7},{3,6},{4,1},{5,0},{6,3},{7,2},{8,13},{9,12},{10,... | collective-permute-start | bytes 208904 | tf_op jit(solution)/shard_map/ppermute | solution.py:287
  7.2 2.0 %collective-permute-start.2 = (bf16[272,128]{1,0:T(8,128)(2,1)}, bf16[272,128]{1,0:T(8,128)(2,1)S(1)}, u32[]{:S(2)}, u32[]{:S(2)}) collective-permute-start(bf16[272,128]{1,0:T(8,128)(2,1)} %message.1), channel_id=1, source_target_pairs={{0,7},{1,6},{2,5},{3,4},{4,3},{5,2},{6,1},{7,0},{8,15},{9,14},{10,... | collective-permute-start | bytes 208904 | tf_op jit(solution)/shard_map/ppermute | solution.py:287
  9.3 1.7 %collective-permute-start.6 = (bf16[272,128]{1,0:T(8,128)(2,1)S(1)}, bf16[272,128]{1,0:T(8,128)(2,1)S(1)}, u32[]{:S(2)}, u32[]{:S(2)}) collective-permute-start(bf16[272,128]{1,0:T(8,128)(2,1)S(1)} %collective-permute-done.5), channel_id=1, source_target_pairs={{0,20},{1,21},{2,22},{3,23},{4,16},{5,17},{6,18},{7,19},{8,28},{9,... | collective-permute-start | bytes 208904 | tf_op jit(solution)/shard_map/ppermute | solution.py:287
  10.9 0.9 %collective-permute-start.10 = (bf16[272,128]{1,0:T(8,128)(2,1)S(1)}, bf16[272,128]{1,0:T(8,128)(2,1)S(1)}, u32[]{:S(2)}, u32[]{:S(2)}) collective-permute-start(bf16[272,128]{1,0:T(8,128)(2,1)S(1)} %collective-permute-done.7), channel_id=1, source_target_pairs={{0,12},{1,13},{2,14},{3,15},{4,8},{5,9},{6,10},{7,11},{8,4},{9,5},... | collective-permute-start | bytes 208904 | tf_op jit(solution)/shard_map/ppermute | solution.py:287
  11.9 1.9 %collective-permute-done.2 = bf16[272,128]{1,0:T(8,128)(2,1)S(1)} collective-permute-done((bf16[272,128]{1,0:T(8,128)(2,1)}, bf16[272,128]{1,0:T(8,128)(2,1)S(1)}, u32[]{:S(2)}, u32[]{:S(2)}) %collective-permute-start.2) | collective-permute-done | bytes 69664 | tf_op jit(solution)/shard_map/ppermute | solution.py:287
  13.9 0.5 collective-permute-start
  14.4 1.0 %collective-permute-start.3 = (bf16[272,128]{1,0:T(8,128)(2,1)S(1)}, bf16[272,128]{1,0:T(8,128)(2,1)S(1)}, u32[]{:S(2)}, u32[]{:S(2)}) collective-permute-start(bf16[272,128]{1,0:T(8,128)(2,1)S(1)} %collective-permute-done.2), channel_id=1, source_target_pairs={{0,12},{1,13},{2,14},{3,15},{4,8},{5,9},{6,10},{7,11},{8,4},{9,5},... | collective-permute-start | bytes 208904 | tf_op jit(solution)/shard_map/ppermute | solution.py:287
  15.4 1.2 %collective-permute-start.11 = (bf16[272,128]{1,0:T(8,128)(2,1)S(1)}, bf16[272,128]{1,0:T(8,128)(2,1)S(1)}, u32[]{:S(2)}, u32[]{:S(2)}) collective-permute-start(bf16[272,128]{1,0:T(8,128)(2,1)S(1)} %collective-permute-done.10), channel_id=1, source_target_pairs={{0,20},{1,21},{2,22},{3,23},{4,16},{5,17},{6,18},{7,19},{8,28},{9,... | collective-permute-start | bytes 208904 | tf_op jit(solution)/shard_map/ppermute | solution.py:287
  16.7 0.2 collective-permute-start.1
  16.9 1.7 %collective-permute-done.3 = bf16[272,128]{1,0:T(8,128)(2,1)S(1)} collective-permute-done((bf16[272,128]{1,0:T(8,128)(2,1)S(1)}, bf16[272,128]{1,0:T(8,128)(2,1)S(1)}, u32[]{:S(2)}, u32[]{:S(2)}) %collective-permute-start.3) | collective-permute-done | bytes 69664 | tf_op jit(solution)/shard_map/ppermute | solution.py:287
  18.6 1.5 %collective-permute-start.4 = (bf16[272,128]{1,0:T(8,128)(2,1)S(1)}, bf16[272,128]{1,0:T(8,128)(2,1)S(1)}, u32[]{:S(2)}, u32[]{:S(2)}) collective-permute-start(bf16[272,128]{1,0:T(8,128)(2,1)S(1)} %collective-permute-done.3), channel_id=1, source_target_pairs={{0,20},{1,21},{2,22},{3,23},{4,16},{5,17},{6,18},{7,19},{8,28},{9,... | collective-permute-start | bytes 208904 | tf_op jit(solution)/shard_map/ppermute | solution.py:287
  20.1 0.2 collective-permute-start.12
  20.4 2.5 %early.1 = (bf16[1152,1280]{1,0:T(8,128)(2,1)S(1)}, f32[1152,256]{1,0:T(8,128)S(1)}) custom-call(bf16[1,272,128]{2,1,0:T(8,128)(2,1)S(1)} %collective-permute-done.1.own_ref, s32[2]{0:T(128)S(1)} %pad_add_fusion.place_ref, bf16[1,272,128]{2,1,0:T(8,128)(2,1)S(1)} %collective-permute-done.refs_0_, bf16[4,272,128]{2,1,0:T(8,128)(2,1)S(1)} %pad_maximum_fusion.refs_1_, ...), custom_call_target="tpu_custom_call" | custom-call | flops 3774873600 | bytes 11796480 | tf_op jit(solution)/shard_map/early/pallas_call | solution.py:229
  22.9 0.4 collective-permute-start.9
  23.4 1.4 %side.1 = (bf16[1152,512]{1,0:T(8,128)(2,1)S(1)}, f32[1152,256]{1,0:T(8,128)S(1)}) custom-call(bf16[1,272,128]{2,1,0:T(8,128)(2,1)S(1)} %collective-permute-done.1.own_ref, s32[2]{0:T(128)S(1)} %pad_add_fusion.place_ref, f32[1152,256]{1,0:T(8,128)S(1)} %get-tuple-element.19.refs_0_, bf16[2,272,128]{2,1,0:T(8,128)(2,1)S(1)} %pad_maximum_fusion.2.refs_1_, ...), custom_call_target="tpu_custom_call" | custom-call | flops 1509949440 | bytes 4718592 | tf_op jit(solution)/shard_map/side/pallas_call | solution.py:229
  24.8 3.0 %main.1 = (f32[3,1,128]{2,1,0:T(1,128)}, bf16[1152,256]{1,0:T(8,128)(2,1)S(1)}, f32[4,256,128]{2,1,0:T(8,128)S(1)}, bf16[4,256,128]{2,1,0:T(8,128)(2,1)S(1)}) custom-call(bf16[1,272,128]{2,1,0:T(8,128)(2,1)S(1)} %collective-permute-done.1.own_ref, s32[2]{0:T(128)S(1)} %pad_add_fusion.place_ref, s32[1,128]{1,0:T(1,128)S(1)} %bitcast.54, ...), custom_call_target="tpu_custom_call" | custom-call | tf_op jit(solution)/shard_map/main/pallas_call | solution.py:251
  27.9 1.1 %late.1 = (f32[5,256,128]{2,1,0:T(8,128)S(1)}, bf16[5,256,128]{2,1,0:T(8,128)(2,1)S(1)}) custom-call(bf16[1152,256]{1,0:T(8,128)(2,1)S(1)} %get-tuple-element.27.right_ref, bf16[1152,1280]{1,0:T(8,128)(2,1)S(1)} %get-tuple-element.28.kern_ref), custom_call_target="tpu_custom_call" | custom-call | flops 754974720 | bytes 2949120 | tf_op jit(solution)/shard_map/late/pallas_call | solution.py:266
  29.0 0.4 collective-permute-start.13
  29.5 1.1 %collective-permute-start.16 = (bf16[256,128]{1,0:T(8,128)(2,1)S(1)}, bf16[256,128]{1,0:T(8,128)(2,1)S(1)}, u32[]{:S(2)}, u32[]{:S(2)}) collective-permute-start(bf16[256,128]{1,0:T(8,128)(2,1)S(1)} %get-tuple-element.43), channel_id=1, source_target_pairs={{0,20},{1,21},{2,22},{3,23},{4,16},{5,17},{6,18},{7,19},{8,28},{9,... | collective-permute-start | bytes 196616 | tf_op jit(solution)/shard_map/ppermute | solution.py:287
  30.8 1.3 %collective-permute-start.15 = (bf16[2,256,128]{2,1,0:T(8,128)(2,1)S(1)}, bf16[2,256,128]{2,1,0:T(8,128)(2,1)S(1)}, u32[]{:S(2)}, u32[]{:S(2)}) collective-permute-start(bf16[2,256,128]{2,1,0:T(8,128)(2,1)S(1)} %pad_maximum_fusion.3), channel_id=1, source_target_pairs={{0,20},{1,21},{2,22},{3,23},{4,16},{5,17},{6,18},{7,19},{8,28},{9,... | collective-permute-start | bytes 393224 | tf_op jit(solution)/shard_map/ppermute | solution.py:287
  32.1 1.6 %collective-permute-done.16 = bf16[256,128]{1,0:T(8,128)(2,1)S(1)} collective-permute-done((bf16[256,128]{1,0:T(8,128)(2,1)S(1)}, bf16[256,128]{1,0:T(8,128)(2,1)S(1)}, u32[]{:S(2)}, u32[]{:S(2)}) %collective-permute-start.16) | collective-permute-done | bytes 65568 | tf_op jit(solution)/shard_map/ppermute | solution.py:287
  33.7 1.2 %collective-permute-start.19 = (bf16[256,128]{1,0:T(8,128)(2,1)S(1)}, bf16[256,128]{1,0:T(8,128)(2,1)S(1)}, u32[]{:S(2)}, u32[]{:S(2)}) collective-permute-start(bf16[256,128]{1,0:T(8,128)(2,1)S(1)} %fusion.6), channel_id=1, source_target_pairs={{0,12},{1,13},{2,14},{3,15},{4,8},{5,9},{6,10},{7,11},{8,4},{9,5},... | collective-permute-start | bytes 196616 | tf_op jit(solution)/shard_map/ppermute | solution.py:287
  34.9 1.5 %collective-permute-done.15 = bf16[2,256,128]{2,1,0:T(8,128)(2,1)S(1)} collective-permute-done((bf16[2,256,128]{2,1,0:T(8,128)(2,1)S(1)}, bf16[2,256,128]{2,1,0:T(8,128)(2,1)S(1)}, u32[]{:S(2)}, u32[]{:S(2)}) %collective-permute-start.15) | collective-permute-done | bytes 131104 | tf_op jit(solution)/shard_map/ppermute | solution.py:287
  36.5 0.9 %collective-permute-start.18 = (bf16[256,128]{1,0:T(8,128)(2,1)S(1)}, bf16[256,128]{1,0:T(8,128)(2,1)S(1)}, u32[]{:S(2)}, u32[]{:S(2)}) collective-permute-start(bf16[256,128]{1,0:T(8,128)(2,1)S(1)} %get-tuple-element.44), channel_id=1, source_target_pairs={{0,12},{1,13},{2,14},{3,15},{4,8},{5,9},{6,10},{7,11},{8,4},{9,5},... | collective-permute-start | bytes 196616 | tf_op jit(solution)/shard_map/ppermute | solution.py:287
  37.4 0.9 %collective-permute-start.17 = (bf16[256,128]{1,0:T(8,128)(2,1)S(1)}, bf16[256,128]{1,0:T(8,128)(2,1)S(1)}, u32[]{:S(2)}, u32[]{:S(2)}) collective-permute-start(bf16[256,128]{1,0:T(8,128)(2,1)S(1)} %get-tuple-element.45), channel_id=1, source_target_pairs={{0,12},{1,13},{2,14},{3,15},{4,8},{5,9},{6,10},{7,11},{8,4},{9,5},... | collective-permute-start | bytes 196616 | tf_op jit(solution)/shard_map/ppermute | solution.py:287
  38.3 3.3 %collective-permute-start.21 = (bf16[256,128]{1,0:T(8,128)(2,1)S(1)}, bf16[256,128]{1,0:T(8,128)(2,1)S(1)}, u32[]{:S(2)}, u32[]{:S(2)}) collective-permute-start(bf16[256,128]{1,0:T(8,128)(2,1)S(1)} %fusion.1), channel_id=1, source_target_pairs={{0,7},{1,6},{2,5},{3,4},{4,3},{5,2},{6,1},{7,0},{8,15},{9,14},{10,... | collective-permute-start | bytes 196616 | tf_op jit(solution)/shard_map/ppermute | solution.py:287
  41.8 1.3 %collective-permute-start.20 = (bf16[256,128]{1,0:T(8,128)(2,1)S(1)}, bf16[256,128]{1,0:T(8,128)(2,1)S(1)}, u32[]{:S(2)}, u32[]{:S(2)}) collective-permute-start(bf16[256,128]{1,0:T(8,128)(2,1)S(1)} %get-tuple-element.35), channel_id=1, source_target_pairs={{0,5},{1,4},{2,7},{3,6},{4,1},{5,0},{6,3},{7,2},{8,13},{9,12},{10,... | collective-permute-start | bytes 196616 | tf_op jit(solution)/shard_map/ppermute | solution.py:287
  43.1 0.9 %collective-permute-done.21 = bf16[256,128]{1,0:T(8,128)(2,1)S(1)} collective-permute-done((bf16[256,128]{1,0:T(8,128)(2,1)S(1)}, bf16[256,128]{1,0:T(8,128)(2,1)S(1)}, u32[]{:S(2)}, u32[]{:S(2)}) %collective-permute-start.21) | collective-permute-done | bytes 65568 | tf_op jit(solution)/shard_map/ppermute | solution.py:287
  44.1 1.6 %collective-permute-done.20 = bf16[256,128]{1,0:T(8,128)(2,1)S(1)} collective-permute-done((bf16[256,128]{1,0:T(8,128)(2,1)S(1)}, bf16[256,128]{1,0:T(8,128)(2,1)S(1)}, u32[]{:S(2)}, u32[]{:S(2)}) %collective-permute-start.20) | collective-permute-done | bytes 65568 | tf_op jit(solution)/shard_map/ppermute | solution.py:287
  45.7 0.9 %convolution_bitcast_fusion = f32[1,1,1,128,256]{4,3,2,1,0:T(8,128)} fusion(bf16[256,256]{1,0:T(8,128)(2,1)S(1)} %copy-done.4, bf16[256,128]{1,0:T(8,128)(2,1)S(1)} %collective-permute-done.21, f32[256,128]{1,0:T(8,128)S(1)} %get-tuple-element.41, bf16[256,128]{1,0:T(8,128)(2,1)S(1)} %collective-permute-done.20), kind=kOutput, calls=%fused_computation | convolution fusion | flops 16941056 | bytes 524288 | tf_op jit(solution)/shard_map/dot_general | solution.py:381
  (41 shorter events, 1.0 us)
Async XLA Ops:
  3.0 6.3 %collective-permute-start.5 = (bf16[272,128]{1,0:T(8,128)(2,1)}, bf16[272,128]{1,0:T(8,128)(2,1)S(1)}, u32[]{:S(2)}, u32[]{:S(2)}) collective-permute-start(bf16[272,128]{1,0:T(8,128)(2,1)} %message.1), channel_id=1, source_target_pairs={{0,12},{1,13},{2,14},{3,15},{4,8},{5,9},{6,10},{7,11},{8,4},{9,5},... | collective-permute-start | bytes 208904 | tf_op jit(solution)/shard_map/ppermute | solution.py:287
  5.4 5.6 %collective-permute-start.7 = (bf16[272,128]{1,0:T(8,128)(2,1)}, bf16[272,128]{1,0:T(8,128)(2,1)S(1)}, u32[]{:S(2)}, u32[]{:S(2)}) collective-permute-start(bf16[272,128]{1,0:T(8,128)(2,1)} %message.1), channel_id=1, source_target_pairs={{0,5},{1,4},{2,7},{3,6},{4,1},{5,0},{6,3},{7,2},{8,13},{9,12},{10,... | collective-permute-start | bytes 208904 | tf_op jit(solution)/shard_map/ppermute | solution.py:287
  7.2 6.6 %collective-permute-start.2 = (bf16[272,128]{1,0:T(8,128)(2,1)}, bf16[272,128]{1,0:T(8,128)(2,1)S(1)}, u32[]{:S(2)}, u32[]{:S(2)}) collective-permute-start(bf16[272,128]{1,0:T(8,128)(2,1)} %message.1), channel_id=1, source_target_pairs={{0,7},{1,6},{2,5},{3,4},{4,3},{5,2},{6,1},{7,0},{8,15},{9,14},{10,... | collective-permute-start | bytes 208904 | tf_op jit(solution)/shard_map/ppermute | solution.py:287
  9.3 4.5 %collective-permute-start.6 = (bf16[272,128]{1,0:T(8,128)(2,1)S(1)}, bf16[272,128]{1,0:T(8,128)(2,1)S(1)}, u32[]{:S(2)}, u32[]{:S(2)}) collective-permute-start(bf16[272,128]{1,0:T(8,128)(2,1)S(1)} %collective-permute-done.5), channel_id=1, source_target_pairs={{0,20},{1,21},{2,22},{3,23},{4,16},{5,17},{6,18},{7,19},{8,28},{9,... | collective-permute-start | bytes 208904 | tf_op jit(solution)/shard_map/ppermute | solution.py:287
  10.9 4.5 %collective-permute-start.10 = (bf16[272,128]{1,0:T(8,128)(2,1)S(1)}, bf16[272,128]{1,0:T(8,128)(2,1)S(1)}, u32[]{:S(2)}, u32[]{:S(2)}) collective-permute-start(bf16[272,128]{1,0:T(8,128)(2,1)S(1)} %collective-permute-done.7), channel_id=1, source_target_pairs={{0,12},{1,13},{2,14},{3,15},{4,8},{5,9},{6,10},{7,11},{8,4},{9,5},... | collective-permute-start | bytes 208904 | tf_op jit(solution)/shard_map/ppermute | solution.py:287
  13.8 6.5 %collective-permute-start.8 = (bf16[4,272,128]{2,1,0:T(8,128)(2,1)S(1)}, bf16[4,272,128]{2,1,0:T(8,128)(2,1)S(1)}, u32[]{:S(2)}, u32[]{:S(2)}) collective-permute-start(bf16[4,272,128]{2,1,0:T(8,128)(2,1)S(1)} %pad_maximum_fusion.refs_1_), channel_id=1, source_target_pairs={{0,4},{4,0},{1,5},{5,1},{2,6},{6,2},{3,7},{7,3},{8,12},{12,8},{9,1... | collective-permute-start | bytes 835592 | tf_op jit(solution)/shard_map/ppermute | solution.py:291
  13.9 2.8 %collective-permute-start = (bf16[1,272,128]{2,1,0:T(8,128)(2,1)}, bf16[1,272,128]{2,1,0:T(8,128)(2,1)S(1)}, u32[]{:S(2)}, u32[]{:S(2)}) collective-permute-start(bf16[1,272,128]{2,1,0:T(8,128)(2,1)} %bitcast.59), channel_id=1, source_target_pairs={{0,4},{4,0},{1,5},{5,1},{2,6},{6,2},{3,7},{7,3},{8,12},{12,8},{9,1... | collective-permute-start | bytes 208904 | tf_op jit(solution)/shard_map/ppermute | solution.py:291
  14.4 4.2 %collective-permute-start.3 = (bf16[272,128]{1,0:T(8,128)(2,1)S(1)}, bf16[272,128]{1,0:T(8,128)(2,1)S(1)}, u32[]{:S(2)}, u32[]{:S(2)}) collective-permute-start(bf16[272,128]{1,0:T(8,128)(2,1)S(1)} %collective-permute-done.2), channel_id=1, source_target_pairs={{0,12},{1,13},{2,14},{3,15},{4,8},{5,9},{6,10},{7,11},{8,4},{9,5},... | collective-permute-start | bytes 208904 | tf_op jit(solution)/shard_map/ppermute | solution.py:287
  15.4 4.7 %collective-permute-start.11 = (bf16[272,128]{1,0:T(8,128)(2,1)S(1)}, bf16[272,128]{1,0:T(8,128)(2,1)S(1)}, u32[]{:S(2)}, u32[]{:S(2)}) collective-permute-start(bf16[272,128]{1,0:T(8,128)(2,1)S(1)} %collective-permute-done.10), channel_id=1, source_target_pairs={{0,20},{1,21},{2,22},{3,23},{4,16},{5,17},{6,18},{7,19},{8,28},{9,... | collective-permute-start | bytes 208904 | tf_op jit(solution)/shard_map/ppermute | solution.py:287
  16.7 3.6 %collective-permute-start.1 = (bf16[1,272,128]{2,1,0:T(8,128)(2,1)S(1)}, bf16[1,272,128]{2,1,0:T(8,128)(2,1)S(1)}, u32[]{:S(2)}, u32[]{:S(2)}) collective-permute-start(bf16[1,272,128]{2,1,0:T(8,128)(2,1)S(1)} %collective-permute-done.refs_0_), channel_id=1, source_target_pairs={{0,4},{4,0},{1,5},{5,1},{2,6},{6,2},{3,7},{7,3},{8,12},{12,8},{9,1... | collective-permute-start | bytes 208904 | tf_op jit(solution)/shard_map/ppermute | solution.py:291
  18.6 4.2 %collective-permute-start.4 = (bf16[272,128]{1,0:T(8,128)(2,1)S(1)}, bf16[272,128]{1,0:T(8,128)(2,1)S(1)}, u32[]{:S(2)}, u32[]{:S(2)}) collective-permute-start(bf16[272,128]{1,0:T(8,128)(2,1)S(1)} %collective-permute-done.3), channel_id=1, source_target_pairs={{0,20},{1,21},{2,22},{3,23},{4,16},{5,17},{6,18},{7,19},{8,28},{9,... | collective-permute-start | bytes 208904 | tf_op jit(solution)/shard_map/ppermute | solution.py:287
  20.1 2.7 %collective-permute-start.12 = (bf16[2,272,128]{2,1,0:T(8,128)(2,1)S(1)}, bf16[2,272,128]{2,1,0:T(8,128)(2,1)S(1)}, u32[]{:S(2)}, u32[]{:S(2)}) collective-permute-start(bf16[2,272,128]{2,1,0:T(8,128)(2,1)S(1)} %pad_maximum_fusion.2.refs_1_), channel_id=1, source_target_pairs={{0,4},{4,0},{1,5},{5,1},{2,6},{6,2},{3,7},{7,3},{8,12},{12,8},{9,1... | collective-permute-start | bytes 417800 | tf_op jit(solution)/shard_map/ppermute | solution.py:291
  22.9 1.9 %copy-start = (f32[6,256]{1,0:T(8,128)S(1)}, f32[6,256]{1,0:T(8,128)}, u32[]{:S(2)}) copy-start(f32[6,256]{1,0:T(8,128)} %radial_ref.1) | copy-start | bytes 18436
  22.9 1.9 %copy-start.1 = (f32[1,1,1,3,128]{4,2,3,1,0:T(1,128)S(1)}, f32[1,1,1,3,128]{4,2,3,1,0:T(1,128)}, u32[]{:S(2)}) copy-start(f32[1,1,1,3,128]{4,2,3,1,0:T(1,128)} %param.12) | copy-start | bytes 4612
  22.9 1.9 %copy-start.2 = (f32[256]{0:T(256)S(1)}, f32[256]{0:T(256)}, u32[]{:S(2)}) copy-start(f32[256]{0:T(256)} %param.15) | copy-start | bytes 3076
  22.9 1.9 %copy-start.3 = (s32[1,1,1,128]{3,2,1,0:T(1,128)S(1)}, s32[1,1,1,128]{3,2,1,0:T(1,128)}, u32[]{:S(2)}) copy-start(s32[1,1,1,128]{3,2,1,0:T(1,128)} %param.11) | copy-start | bytes 1540
  22.9 1.9 %collective-permute-start.9 = (bf16[2,272,128]{2,1,0:T(8,128)(2,1)S(1)}, bf16[2,272,128]{2,1,0:T(8,128)(2,1)S(1)}, u32[]{:S(2)}, u32[]{:S(2)}) collective-permute-start(bf16[2,272,128]{2,1,0:T(8,128)(2,1)S(1)} %pad_maximum_fusion.1.refs_0_), channel_id=1, source_target_pairs={{0,4},{4,0},{1,5},{5,1},{2,6},{6,2},{3,7},{7,3},{8,12},{12,8},{9,1... | collective-permute-start | bytes 417800 | tf_op jit(solution)/shard_map/ppermute | solution.py:291
  27.8 1.6 %collective-permute-start.14 = (bf16[4,256,128]{2,1,0:T(8,128)(2,1)S(1)}, bf16[4,256,128]{2,1,0:T(8,128)(2,1)S(1)}, u32[]{:S(2)}, u32[]{:S(2)}) collective-permute-start(bf16[4,256,128]{2,1,0:T(8,128)(2,1)S(1)} %get-tuple-element.32), channel_id=1, source_target_pairs={{0,4},{4,0},{1,5},{5,1},{2,6},{6,2},{3,7},{7,3},{8,12},{12,8},{9,1... | collective-permute-start | bytes 786440 | tf_op jit(solution)/shard_map/ppermute | solution.py:291
  29.0 1.7 %collective-permute-start.13 = (bf16[5,256,128]{2,1,0:T(8,128)(2,1)S(1)}, bf16[5,256,128]{2,1,0:T(8,128)(2,1)S(1)}, u32[]{:S(2)}, u32[]{:S(2)}) collective-permute-start(bf16[5,256,128]{2,1,0:T(8,128)(2,1)S(1)} %get-tuple-element.30), channel_id=1, source_target_pairs={{0,4},{4,0},{1,5},{5,1},{2,6},{6,2},{3,7},{7,3},{8,12},{12,8},{9,1... | collective-permute-start | bytes 983048 | tf_op jit(solution)/shard_map/ppermute | solution.py:291
  29.5 4.1 %collective-permute-start.16 = (bf16[256,128]{1,0:T(8,128)(2,1)S(1)}, bf16[256,128]{1,0:T(8,128)(2,1)S(1)}, u32[]{:S(2)}, u32[]{:S(2)}) collective-permute-start(bf16[256,128]{1,0:T(8,128)(2,1)S(1)} %get-tuple-element.43), channel_id=1, source_target_pairs={{0,20},{1,21},{2,22},{3,23},{4,16},{5,17},{6,18},{7,19},{8,28},{9,... | collective-permute-start | bytes 196616 | tf_op jit(solution)/shard_map/ppermute | solution.py:287
  30.8 14.9 %copy-start.4 = (bf16[256,256]{1,0:T(8,128)(2,1)S(1)}, bf16[256,256]{1,0:T(8,128)(2,1)}, u32[]{:S(2)}) copy-start(bf16[256,256]{1,0:T(8,128)(2,1)} %w_ref.1) | copy-start | bytes 393220
  30.8 5.6 %collective-permute-start.15 = (bf16[2,256,128]{2,1,0:T(8,128)(2,1)S(1)}, bf16[2,256,128]{2,1,0:T(8,128)(2,1)S(1)}, u32[]{:S(2)}, u32[]{:S(2)}) collective-permute-start(bf16[2,256,128]{2,1,0:T(8,128)(2,1)S(1)} %pad_maximum_fusion.3), channel_id=1, source_target_pairs={{0,20},{1,21},{2,22},{3,23},{4,16},{5,17},{6,18},{7,19},{8,28},{9,... | collective-permute-start | bytes 393224 | tf_op jit(solution)/shard_map/ppermute | solution.py:287
  33.7 4.6 %collective-permute-start.19 = (bf16[256,128]{1,0:T(8,128)(2,1)S(1)}, bf16[256,128]{1,0:T(8,128)(2,1)S(1)}, u32[]{:S(2)}, u32[]{:S(2)}) collective-permute-start(bf16[256,128]{1,0:T(8,128)(2,1)S(1)} %fusion.6), channel_id=1, source_target_pairs={{0,12},{1,13},{2,14},{3,15},{4,8},{5,9},{6,10},{7,11},{8,4},{9,5},... | collective-permute-start | bytes 196616 | tf_op jit(solution)/shard_map/ppermute | solution.py:287
  36.5 5.1 %collective-permute-start.18 = (bf16[256,128]{1,0:T(8,128)(2,1)S(1)}, bf16[256,128]{1,0:T(8,128)(2,1)S(1)}, u32[]{:S(2)}, u32[]{:S(2)}) collective-permute-start(bf16[256,128]{1,0:T(8,128)(2,1)S(1)} %get-tuple-element.44), channel_id=1, source_target_pairs={{0,12},{1,13},{2,14},{3,15},{4,8},{5,9},{6,10},{7,11},{8,4},{9,5},... | collective-permute-start | bytes 196616 | tf_op jit(solution)/shard_map/ppermute | solution.py:287
  37.4 4.4 %collective-permute-start.17 = (bf16[256,128]{1,0:T(8,128)(2,1)S(1)}, bf16[256,128]{1,0:T(8,128)(2,1)S(1)}, u32[]{:S(2)}, u32[]{:S(2)}) collective-permute-start(bf16[256,128]{1,0:T(8,128)(2,1)S(1)} %get-tuple-element.45), channel_id=1, source_target_pairs={{0,12},{1,13},{2,14},{3,15},{4,8},{5,9},{6,10},{7,11},{8,4},{9,5},... | collective-permute-start | bytes 196616 | tf_op jit(solution)/shard_map/ppermute | solution.py:287
  38.3 5.7 %collective-permute-start.21 = (bf16[256,128]{1,0:T(8,128)(2,1)S(1)}, bf16[256,128]{1,0:T(8,128)(2,1)S(1)}, u32[]{:S(2)}, u32[]{:S(2)}) collective-permute-start(bf16[256,128]{1,0:T(8,128)(2,1)S(1)} %fusion.1), channel_id=1, source_target_pairs={{0,7},{1,6},{2,5},{3,4},{4,3},{5,2},{6,1},{7,0},{8,15},{9,14},{10,... | collective-permute-start | bytes 196616 | tf_op jit(solution)/shard_map/ppermute | solution.py:287
  41.8 3.9 %collective-permute-start.20 = (bf16[256,128]{1,0:T(8,128)(2,1)S(1)}, bf16[256,128]{1,0:T(8,128)(2,1)S(1)}, u32[]{:S(2)}, u32[]{:S(2)}) collective-permute-start(bf16[256,128]{1,0:T(8,128)(2,1)S(1)} %get-tuple-element.35), channel_id=1, source_target_pairs={{0,5},{1,4},{2,7},{3,6},{4,1},{5,0},{6,3},{7,2},{8,13},{9,12},{10,... | collective-permute-start | bytes 196616 | tf_op jit(solution)/shard_map/ppermute | solution.py:287

commit v7 on v6

--- a/solution.py
+++ b/solution.py
@@ -341,8 +341,8 @@
     back1 = swap(next1, "gx", 1)
     back0 = swap(next0, "gx", 1)
     next3 = narrow(near_sum[4] + back3)
+    start = near_sum[0] + after(back0, next3)
     next1 = narrow(near_sum[3] + after(back1, next3))
-    start = near_sum[0] + back0
     back3 = swap(next3, "gz", 3)
     back1 = swap(after(next1, start), "gz", 1)
     return pred, start + back1 + back3

time: 46.7 us -> 46.7 us (level)
  no operation moved by 1% of the time
where the time goes in v7:
time: 46.7 us; the launch traced here: 46.6 us
  starting transfers between devices  24.7 us (53%)
  Pallas kernels  9.62 us (21%)
  waiting for transfers between devices  9.45 us (20%)
  between operations  1.48 us (3%)
  matrix products  0.86 us (2%)
    ppermute x15, starting transfers between devices, swap(): return lax.ppermute(block, AXES, pairs)  22.7 us
    ppermute x15, waiting for transfers between devices, swap(): return lax.ppermute(block, AXES, pairs)  9.4 us
    pallas_call x2, Pallas kernels, call_early(): pl.pallas_call(functools.partial(early_kernel, slots, ways, bases, bool(m...  3.89 us
    pallas_call x1, Pallas kernels, call_main(): pl.pallas_call(functools.partial(main_kernel, slots, ways, bases, len(nea...  2.96 us
    ppermute x7, starting transfers between devices, core(): return lax.ppermute(block, 'gy', [(0, 1), (1, 0)])  1.99 us
    pallas_call x1, Pallas kernels, on_device(): pl.pallas_call(message_kernel, out_shape=struct(width + TAIL, atoms), in_...  1.71 us
    pallas_call x1, Pallas kernels, call_late(): pl.pallas_call(late_kernel, out_shape=out_shape, in_specs=[VMEM] * 2, out...  1.05 us
  transfers between devices with their start and end apart: 22, of which 7 were waited for; matrix products, arithmetic and copies ran while one was open for 1% of the time, Pallas kernels for 11%

profile of v7, /device:TPU:0, one launch (start us, length us, event | category | flops | bytes accessed | tf_op | source)
XLA Modules:
  0.0 46.6 jit_solution(9882179668445904165)
XLA Ops:
  1.3 1.7 %message.1 = bf16[272,128]{1,0:T(8,128)(2,1)} custom-call(bf16[128,256]{1,0:T(8,128)(2,1)} %bitcast.64, bf16[256,256]{1,0:T(8,128)(2,1)} %w_ref.1, f32[3,1,128]{2,1,0:T(1,128)} %bitcast.65, s32[1,1]{1,0:T(1,128)} %bitcast.51.counts_ref), custom_call_target="tpu_custom_call" | custom-call | tf_op jit(solution)/shard_map/message/pallas_call | solution.py:371
  3.0 2.4 %collective-permute-start.5 = (bf16[272,128]{1,0:T(8,128)(2,1)}, bf16[272,128]{1,0:T(8,128)(2,1)S(1)}, u32[]{:S(2)}, u32[]{:S(2)}) collective-permute-start(bf16[272,128]{1,0:T(8,128)(2,1)} %message.1), channel_id=1, source_target_pairs={{0,12},{1,13},{2,14},{3,15},{4,8},{5,9},{6,10},{7,11},{8,4},{9,5},... | collective-permute-start | bytes 208904 | tf_op jit(solution)/shard_map/ppermute | solution.py:287
  5.4 1.9 %collective-permute-start.7 = (bf16[272,128]{1,0:T(8,128)(2,1)}, bf16[272,128]{1,0:T(8,128)(2,1)S(1)}, u32[]{:S(2)}, u32[]{:S(2)}) collective-permute-start(bf16[272,128]{1,0:T(8,128)(2,1)} %message.1), channel_id=1, source_target_pairs={{0,5},{1,4},{2,7},{3,6},{4,1},{5,0},{6,3},{7,2},{8,13},{9,12},{10,... | collective-permute-start | bytes 208904 | tf_op jit(solution)/shard_map/ppermute | solution.py:287
  7.2 2.0 %collective-permute-start.2 = (bf16[272,128]{1,0:T(8,128)(2,1)}, bf16[272,128]{1,0:T(8,128)(2,1)S(1)}, u32[]{:S(2)}, u32[]{:S(2)}) collective-permute-start(bf16[272,128]{1,0:T(8,128)(2,1)} %message.1), channel_id=1, source_target_pairs={{0,7},{1,6},{2,5},{3,4},{4,3},{5,2},{6,1},{7,0},{8,15},{9,14},{10,... | collective-permute-start | bytes 208904 | tf_op jit(solution)/shard_map/ppermute | solution.py:287
  9.3 1.7 %collective-permute-start.6 = (bf16[272,128]{1,0:T(8,128)(2,1)S(1)}, bf16[272,128]{1,0:T(8,128)(2,1)S(1)}, u32[]{:S(2)}, u32[]{:S(2)}) collective-permute-start(bf16[272,128]{1,0:T(8,128)(2,1)S(1)} %collective-permute-done.5), channel_id=1, source_target_pairs={{0,20},{1,21},{2,22},{3,23},{4,16},{5,17},{6,18},{7,19},{8,28},{9,... | collective-permute-start | bytes 208904 | tf_op jit(solution)/shard_map/ppermute | solution.py:287
  10.9 0.9 %collective-permute-start.10 = (bf16[272,128]{1,0:T(8,128)(2,1)S(1)}, bf16[272,128]{1,0:T(8,128)(2,1)S(1)}, u32[]{:S(2)}, u32[]{:S(2)}) collective-permute-start(bf16[272,128]{1,0:T(8,128)(2,1)S(1)} %collective-permute-done.7), channel_id=1, source_target_pairs={{0,12},{1,13},{2,14},{3,15},{4,8},{5,9},{6,10},{7,11},{8,4},{9,5},... | collective-permute-start | bytes 208904 | tf_op jit(solution)/shard_map/ppermute | solution.py:287
  11.9 1.9 %collective-permute-done.2 = bf16[272,128]{1,0:T(8,128)(2,1)S(1)} collective-permute-done((bf16[272,128]{1,0:T(8,128)(2,1)}, bf16[272,128]{1,0:T(8,128)(2,1)S(1)}, u32[]{:S(2)}, u32[]{:S(2)}) %collective-permute-start.2) | collective-permute-done | bytes 69664 | tf_op jit(solution)/shard_map/ppermute | solution.py:287
  13.9 0.5 collective-permute-start
  14.4 1.0 %collective-permute-start.3 = (bf16[272,128]{1,0:T(8,128)(2,1)S(1)}, bf16[272,128]{1,0:T(8,128)(2,1)S(1)}, u32[]{:S(2)}, u32[]{:S(2)}) collective-permute-start(bf16[272,128]{1,0:T(8,128)(2,1)S(1)} %collective-permute-done.2), channel_id=1, source_target_pairs={{0,12},{1,13},{2,14},{3,15},{4,8},{5,9},{6,10},{7,11},{8,4},{9,5},... | collective-permute-start | bytes 208904 | tf_op jit(solution)/shard_map/ppermute | solution.py:287
  15.4 1.2 %collective-permute-start.11 = (bf16[272,128]{1,0:T(8,128)(2,1)S(1)}, bf16[272,128]{1,0:T(8,128)(2,1)S(1)}, u32[]{:S(2)}, u32[]{:S(2)}) collective-permute-start(bf16[272,128]{1,0:T(8,128)(2,1)S(1)} %collective-permute-done.10), channel_id=1, source_target_pairs={{0,20},{1,21},{2,22},{3,23},{4,16},{5,17},{6,18},{7,19},{8,28},{9,... | collective-permute-start | bytes 208904 | tf_op jit(solution)/shard_map/ppermute | solution.py:287
  16.7 0.2 collective-permute-start.1
  16.9 1.7 %collective-permute-done.3 = bf16[272,128]{1,0:T(8,128)(2,1)S(1)} collective-permute-done((bf16[272,128]{1,0:T(8,128)(2,1)S(1)}, bf16[272,128]{1,0:T(8,128)(2,1)S(1)}, u32[]{:S(2)}, u32[]{:S(2)}) %collective-permute-start.3) | collective-permute-done | bytes 69664 | tf_op jit(solution)/shard_map/ppermute | solution.py:287
  18.6 1.5 %collective-permute-start.4 = (bf16[272,128]{1,0:T(8,128)(2,1)S(1)}, bf16[272,128]{1,0:T(8,128)(2,1)S(1)}, u32[]{:S(2)}, u32[]{:S(2)}) collective-permute-start(bf16[272,128]{1,0:T(8,128)(2,1)S(1)} %collective-permute-done.3), channel_id=1, source_target_pairs={{0,20},{1,21},{2,22},{3,23},{4,16},{5,17},{6,18},{7,19},{8,28},{9,... | collective-permute-start | bytes 208904 | tf_op jit(solution)/shard_map/ppermute | solution.py:287
  20.1 0.2 collective-permute-start.12
  20.4 2.5 %early.1 = (bf16[1152,1280]{1,0:T(8,128)(2,1)S(1)}, f32[1152,256]{1,0:T(8,128)S(1)}) custom-call(bf16[1,272,128]{2,1,0:T(8,128)(2,1)S(1)} %collective-permute-done.1.own_ref, s32[2]{0:T(128)S(1)} %pad_add_fusion.place_ref, bf16[1,272,128]{2,1,0:T(8,128)(2,1)S(1)} %collective-permute-done.refs_0_, bf16[4,272,128]{2,1,0:T(8,128)(2,1)S(1)} %pad_maximum_fusion.refs_1_, ...), custom_call_target="tpu_custom_call" | custom-call | flops 3774873600 | bytes 11796480 | tf_op jit(solution)/shard_map/early/pallas_call | solution.py:229
  22.9 0.4 collective-permute-start.9
  23.4 1.4 %side.1 = (bf16[1152,512]{1,0:T(8,128)(2,1)S(1)}, f32[1152,256]{1,0:T(8,128)S(1)}) custom-call(bf16[1,272,128]{2,1,0:T(8,128)(2,1)S(1)} %collective-permute-done.1.own_ref, s32[2]{0:T(128)S(1)} %pad_add_fusion.place_ref, f32[1152,256]{1,0:T(8,128)S(1)} %get-tuple-element.20.refs_0_, bf16[2,272,128]{2,1,0:T(8,128)(2,1)S(1)} %pad_maximum_fusion.2.refs_1_, ...), custom_call_target="tpu_custom_call" | custom-call | flops 1509949440 | bytes 4718592 | tf_op jit(solution)/shard_map/side/pallas_call | solution.py:229
  24.8 3.0 %main.1 = (f32[3,1,128]{2,1,0:T(1,128)}, bf16[1152,256]{1,0:T(8,128)(2,1)S(1)}, f32[4,256,128]{2,1,0:T(8,128)S(1)}, bf16[4,256,128]{2,1,0:T(8,128)(2,1)S(1)}) custom-call(bf16[1,272,128]{2,1,0:T(8,128)(2,1)S(1)} %collective-permute-done.1.own_ref, s32[2]{0:T(128)S(1)} %pad_add_fusion.place_ref, s32[1,128]{1,0:T(1,128)S(1)} %bitcast.54, ...), custom_call_target="tpu_custom_call" | custom-call | tf_op jit(solution)/shard_map/main/pallas_call | solution.py:251
  27.9 1.1 %late.1 = (f32[5,256,128]{2,1,0:T(8,128)S(1)}, bf16[5,256,128]{2,1,0:T(8,128)(2,1)S(1)}) custom-call(bf16[1152,256]{1,0:T(8,128)(2,1)S(1)} %get-tuple-element.28.right_ref, bf16[1152,1280]{1,0:T(8,128)(2,1)S(1)} %get-tuple-element.29.kern_ref), custom_call_target="tpu_custom_call" | custom-call | flops 754974720 | bytes 2949120 | tf_op jit(solution)/shard_map/late/pallas_call | solution.py:266
  29.0 0.4 collective-permute-start.13
  29.5 1.1 %collective-permute-start.16 = (bf16[256,128]{1,0:T(8,128)(2,1)S(1)}, bf16[256,128]{1,0:T(8,128)(2,1)S(1)}, u32[]{:S(2)}, u32[]{:S(2)}) collective-permute-start(bf16[256,128]{1,0:T(8,128)(2,1)S(1)} %get-tuple-element.45), channel_id=1, source_target_pairs={{0,20},{1,21},{2,22},{3,23},{4,16},{5,17},{6,18},{7,19},{8,28},{9,... | collective-permute-start | bytes 196616 | tf_op jit(solution)/shard_map/ppermute | solution.py:287
  30.8 1.3 %collective-permute-start.15 = (bf16[2,256,128]{2,1,0:T(8,128)(2,1)S(1)}, bf16[2,256,128]{2,1,0:T(8,128)(2,1)S(1)}, u32[]{:S(2)}, u32[]{:S(2)}) collective-permute-start(bf16[2,256,128]{2,1,0:T(8,128)(2,1)S(1)} %pad_maximum_fusion.3), channel_id=1, source_target_pairs={{0,20},{1,21},{2,22},{3,23},{4,16},{5,17},{6,18},{7,19},{8,28},{9,... | collective-permute-start | bytes 393224 | tf_op jit(solution)/shard_map/ppermute | solution.py:287
  32.1 1.6 %collective-permute-done.16 = bf16[256,128]{1,0:T(8,128)(2,1)S(1)} collective-permute-done((bf16[256,128]{1,0:T(8,128)(2,1)S(1)}, bf16[256,128]{1,0:T(8,128)(2,1)S(1)}, u32[]{:S(2)}, u32[]{:S(2)}) %collective-permute-start.16) | collective-permute-done | bytes 65568 | tf_op jit(solution)/shard_map/ppermute | solution.py:287
  33.7 1.2 %collective-permute-start.18 = (bf16[256,128]{1,0:T(8,128)(2,1)S(1)}, bf16[256,128]{1,0:T(8,128)(2,1)S(1)}, u32[]{:S(2)}, u32[]{:S(2)}) collective-permute-start(bf16[256,128]{1,0:T(8,128)(2,1)S(1)} %fusion.6), channel_id=1, source_target_pairs={{0,12},{1,13},{2,14},{3,15},{4,8},{5,9},{6,10},{7,11},{8,4},{9,5},... | collective-permute-start | bytes 196616 | tf_op jit(solution)/shard_map/ppermute | solution.py:287
  34.9 1.5 %collective-permute-done.15 = bf16[2,256,128]{2,1,0:T(8,128)(2,1)S(1)} collective-permute-done((bf16[2,256,128]{2,1,0:T(8,128)(2,1)S(1)}, bf16[2,256,128]{2,1,0:T(8,128)(2,1)S(1)}, u32[]{:S(2)}, u32[]{:S(2)}) %collective-permute-start.15) | collective-permute-done | bytes 131104 | tf_op jit(solution)/shard_map/ppermute | solution.py:287
  36.5 0.9 %collective-permute-start.17 = (bf16[256,128]{1,0:T(8,128)(2,1)S(1)}, bf16[256,128]{1,0:T(8,128)(2,1)S(1)}, u32[]{:S(2)}, u32[]{:S(2)}) collective-permute-start(bf16[256,128]{1,0:T(8,128)(2,1)S(1)} %get-tuple-element.47), channel_id=1, source_target_pairs={{0,12},{1,13},{2,14},{3,15},{4,8},{5,9},{6,10},{7,11},{8,4},{9,5},... | collective-permute-start | bytes 196616 | tf_op jit(solution)/shard_map/ppermute | solution.py:287
  37.4 0.9 %collective-permute-start.19 = (bf16[256,128]{1,0:T(8,128)(2,1)S(1)}, bf16[256,128]{1,0:T(8,128)(2,1)S(1)}, u32[]{:S(2)}, u32[]{:S(2)}) collective-permute-start(bf16[256,128]{1,0:T(8,128)(2,1)S(1)} %get-tuple-element.46), channel_id=1, source_target_pairs={{0,12},{1,13},{2,14},{3,15},{4,8},{5,9},{6,10},{7,11},{8,4},{9,5},... | collective-permute-start | bytes 196616 | tf_op jit(solution)/shard_map/ppermute | solution.py:287
  38.3 3.3 %collective-permute-start.21 = (bf16[256,128]{1,0:T(8,128)(2,1)S(1)}, bf16[256,128]{1,0:T(8,128)(2,1)S(1)}, u32[]{:S(2)}, u32[]{:S(2)}) collective-permute-start(bf16[256,128]{1,0:T(8,128)(2,1)S(1)} %fusion.4), channel_id=1, source_target_pairs={{0,7},{1,6},{2,5},{3,4},{4,3},{5,2},{6,1},{7,0},{8,15},{9,14},{10,... | collective-permute-start | bytes 196616 | tf_op jit(solution)/shard_map/ppermute | solution.py:287
  41.8 1.3 %collective-permute-start.20 = (bf16[256,128]{1,0:T(8,128)(2,1)S(1)}, bf16[256,128]{1,0:T(8,128)(2,1)S(1)}, u32[]{:S(2)}, u32[]{:S(2)}) collective-permute-start(bf16[256,128]{1,0:T(8,128)(2,1)S(1)} %get-tuple-element.37), channel_id=1, source_target_pairs={{0,5},{1,4},{2,7},{3,6},{4,1},{5,0},{6,3},{7,2},{8,13},{9,12},{10,... | collective-permute-start | bytes 196616 | tf_op jit(solution)/shard_map/ppermute | solution.py:287
  43.1 0.9 %collective-permute-done.21 = bf16[256,128]{1,0:T(8,128)(2,1)S(1)} collective-permute-done((bf16[256,128]{1,0:T(8,128)(2,1)S(1)}, bf16[256,128]{1,0:T(8,128)(2,1)S(1)}, u32[]{:S(2)}, u32[]{:S(2)}) %collective-permute-start.21) | collective-permute-done | bytes 65568 | tf_op jit(solution)/shard_map/ppermute | solution.py:287
  44.1 1.6 %collective-permute-done.20 = bf16[256,128]{1,0:T(8,128)(2,1)S(1)} collective-permute-done((bf16[256,128]{1,0:T(8,128)(2,1)S(1)}, bf16[256,128]{1,0:T(8,128)(2,1)S(1)}, u32[]{:S(2)}, u32[]{:S(2)}) %collective-permute-start.20) | collective-permute-done | bytes 65568 | tf_op jit(solution)/shard_map/ppermute | solution.py:287
  45.7 0.9 %convolution_bitcast_fusion = f32[1,1,1,128,256]{4,3,2,1,0:T(8,128)} fusion(bf16[256,256]{1,0:T(8,128)(2,1)S(1)} %copy-done.4, bf16[256,128]{1,0:T(8,128)(2,1)S(1)} %collective-permute-done.21, f32[256,128]{1,0:T(8,128)S(1)} %get-tuple-element.43, bf16[256,128]{1,0:T(8,128)(2,1)S(1)} %collective-permute-done.20), kind=kOutput, calls=%fused_computation | convolution fusion | flops 16941056 | bytes 524288 | tf_op jit(solution)/shard_map/dot_general | solution.py:381
  (41 shorter events, 1.0 us)
Async XLA Ops:
  3.0 6.3 %collective-permute-start.5 = (bf16[272,128]{1,0:T(8,128)(2,1)}, bf16[272,128]{1,0:T(8,128)(2,1)S(1)}, u32[]{:S(2)}, u32[]{:S(2)}) collective-permute-start(bf16[272,128]{1,0:T(8,128)(2,1)} %message.1), channel_id=1, source_target_pairs={{0,12},{1,13},{2,14},{3,15},{4,8},{5,9},{6,10},{7,11},{8,4},{9,5},... | collective-permute-start | bytes 208904 | tf_op jit(solution)/shard_map/ppermute | solution.py:287
  5.4 5.6 %collective-permute-start.7 = (bf16[272,128]{1,0:T(8,128)(2,1)}, bf16[272,128]{1,0:T(8,128)(2,1)S(1)}, u32[]{:S(2)}, u32[]{:S(2)}) collective-permute-start(bf16[272,128]{1,0:T(8,128)(2,1)} %message.1), channel_id=1, source_target_pairs={{0,5},{1,4},{2,7},{3,6},{4,1},{5,0},{6,3},{7,2},{8,13},{9,12},{10,... | collective-permute-start | bytes 208904 | tf_op jit(solution)/shard_map/ppermute | solution.py:287
  7.2 6.6 %collective-permute-start.2 = (bf16[272,128]{1,0:T(8,128)(2,1)}, bf16[272,128]{1,0:T(8,128)(2,1)S(1)}, u32[]{:S(2)}, u32[]{:S(2)}) collective-permute-start(bf16[272,128]{1,0:T(8,128)(2,1)} %message.1), channel_id=1, source_target_pairs={{0,7},{1,6},{2,5},{3,4},{4,3},{5,2},{6,1},{7,0},{8,15},{9,14},{10,... | collective-permute-start | bytes 208904 | tf_op jit(solution)/shard_map/ppermute | solution.py:287
  9.3 4.5 %collective-permute-start.6 = (bf16[272,128]{1,0:T(8,128)(2,1)S(1)}, bf16[272,128]{1,0:T(8,128)(2,1)S(1)}, u32[]{:S(2)}, u32[]{:S(2)}) collective-permute-start(bf16[272,128]{1,0:T(8,128)(2,1)S(1)} %collective-permute-done.5), channel_id=1, source_target_pairs={{0,20},{1,21},{2,22},{3,23},{4,16},{5,17},{6,18},{7,19},{8,28},{9,... | collective-permute-start | bytes 208904 | tf_op jit(solution)/shard_map/ppermute | solution.py:287
  10.9 4.5 %collective-permute-start.10 = (bf16[272,128]{1,0:T(8,128)(2,1)S(1)}, bf16[272,128]{1,0:T(8,128)(2,1)S(1)}, u32[]{:S(2)}, u32[]{:S(2)}) collective-permute-start(bf16[272,128]{1,0:T(8,128)(2,1)S(1)} %collective-permute-done.7), channel_id=1, source_target_pairs={{0,12},{1,13},{2,14},{3,15},{4,8},{5,9},{6,10},{7,11},{8,4},{9,5},... | collective-permute-start | bytes 208904 | tf_op jit(solution)/shard_map/ppermute | solution.py:287
  13.8 6.5 %collective-permute-start.8 = (bf16[4,272,128]{2,1,0:T(8,128)(2,1)S(1)}, bf16[4,272,128]{2,1,0:T(8,128)(2,1)S(1)}, u32[]{:S(2)}, u32[]{:S(2)}) collective-permute-start(bf16[4,272,128]{2,1,0:T(8,128)(2,1)S(1)} %pad_maximum_fusion.refs_1_), channel_id=1, source_target_pairs={{0,4},{4,0},{1,5},{5,1},{2,6},{6,2},{3,7},{7,3},{8,12},{12,8},{9,1... | collective-permute-start | bytes 835592 | tf_op jit(solution)/shard_map/ppermute | solution.py:291
  13.9 2.8 %collective-permute-start = (bf16[1,272,128]{2,1,0:T(8,128)(2,1)}, bf16[1,272,128]{2,1,0:T(8,128)(2,1)S(1)}, u32[]{:S(2)}, u32[]{:S(2)}) collective-permute-start(bf16[1,272,128]{2,1,0:T(8,128)(2,1)} %bitcast.59), channel_id=1, source_target_pairs={{0,4},{4,0},{1,5},{5,1},{2,6},{6,2},{3,7},{7,3},{8,12},{12,8},{9,1... | collective-permute-start | bytes 208904 | tf_op jit(solution)/shard_map/ppermute | solution.py:291
  14.4 4.2 %collective-permute-start.3 = (bf16[272,128]{1,0:T(8,128)(2,1)S(1)}, bf16[272,128]{1,0:T(8,128)(2,1)S(1)}, u32[]{:S(2)}, u32[]{:S(2)}) collective-permute-start(bf16[272,128]{1,0:T(8,128)(2,1)S(1)} %collective-permute-done.2), channel_id=1, source_target_pairs={{0,12},{1,13},{2,14},{3,15},{4,8},{5,9},{6,10},{7,11},{8,4},{9,5},... | collective-permute-start | bytes 208904 | tf_op jit(solution)/shard_map/ppermute | solution.py:287
  15.4 4.7 %collective-permute-start.11 = (bf16[272,128]{1,0:T(8,128)(2,1)S(1)}, bf16[272,128]{1,0:T(8,128)(2,1)S(1)}, u32[]{:S(2)}, u32[]{:S(2)}) collective-permute-start(bf16[272,128]{1,0:T(8,128)(2,1)S(1)} %collective-permute-done.10), channel_id=1, source_target_pairs={{0,20},{1,21},{2,22},{3,23},{4,16},{5,17},{6,18},{7,19},{8,28},{9,... | collective-permute-start | bytes 208904 | tf_op jit(solution)/shard_map/ppermute | solution.py:287
  16.7 3.6 %collective-permute-start.1 = (bf16[1,272,128]{2,1,0:T(8,128)(2,1)S(1)}, bf16[1,272,128]{2,1,0:T(8,128)(2,1)S(1)}, u32[]{:S(2)}, u32[]{:S(2)}) collective-permute-start(bf16[1,272,128]{2,1,0:T(8,128)(2,1)S(1)} %collective-permute-done.refs_0_), channel_id=1, source_target_pairs={{0,4},{4,0},{1,5},{5,1},{2,6},{6,2},{3,7},{7,3},{8,12},{12,8},{9,1... | collective-permute-start | bytes 208904 | tf_op jit(solution)/shard_map/ppermute | solution.py:291
  18.6 4.2 %collective-permute-start.4 = (bf16[272,128]{1,0:T(8,128)(2,1)S(1)}, bf16[272,128]{1,0:T(8,128)(2,1)S(1)}, u32[]{:S(2)}, u32[]{:S(2)}) collective-permute-start(bf16[272,128]{1,0:T(8,128)(2,1)S(1)} %collective-permute-done.3), channel_id=1, source_target_pairs={{0,20},{1,21},{2,22},{3,23},{4,16},{5,17},{6,18},{7,19},{8,28},{9,... | collective-permute-start | bytes 208904 | tf_op jit(solution)/shard_map/ppermute | solution.py:287
  20.1 2.7 %collective-permute-start.12 = (bf16[2,272,128]{2,1,0:T(8,128)(2,1)S(1)}, bf16[2,272,128]{2,1,0:T(8,128)(2,1)S(1)}, u32[]{:S(2)}, u32[]{:S(2)}) collective-permute-start(bf16[2,272,128]{2,1,0:T(8,128)(2,1)S(1)} %pad_maximum_fusion.2.refs_1_), channel_id=1, source_target_pairs={{0,4},{4,0},{1,5},{5,1},{2,6},{6,2},{3,7},{7,3},{8,12},{12,8},{9,1... | collective-permute-start | bytes 417800 | tf_op jit(solution)/shard_map/ppermute | solution.py:291
  22.9 1.9 %copy-start = (f32[6,256]{1,0:T(8,128)S(1)}, f32[6,256]{1,0:T(8,128)}, u32[]{:S(2)}) copy-start(f32[6,256]{1,0:T(8,128)} %radial_ref.1) | copy-start | bytes 18436
  22.9 1.9 %copy-start.1 = (f32[1,1,1,3,128]{4,2,3,1,0:T(1,128)S(1)}, f32[1,1,1,3,128]{4,2,3,1,0:T(1,128)}, u32[]{:S(2)}) copy-start(f32[1,1,1,3,128]{4,2,3,1,0:T(1,128)} %param.12) | copy-start | bytes 4612
  22.9 1.9 %copy-start.2 = (f32[256]{0:T(256)S(1)}, f32[256]{0:T(256)}, u32[]{:S(2)}) copy-start(f32[256]{0:T(256)} %param.15) | copy-start | bytes 3076
  22.9 1.9 %copy-start.3 = (s32[1,1,1,128]{3,2,1,0:T(1,128)S(1)}, s32[1,1,1,128]{3,2,1,0:T(1,128)}, u32[]{:S(2)}) copy-start(s32[1,1,1,128]{3,2,1,0:T(1,128)} %param.11) | copy-start | bytes 1540
  22.9 1.9 %collective-permute-start.9 = (bf16[2,272,128]{2,1,0:T(8,128)(2,1)S(1)}, bf16[2,272,128]{2,1,0:T(8,128)(2,1)S(1)}, u32[]{:S(2)}, u32[]{:S(2)}) collective-permute-start(bf16[2,272,128]{2,1,0:T(8,128)(2,1)S(1)} %pad_maximum_fusion.1.refs_0_), channel_id=1, source_target_pairs={{0,4},{4,0},{1,5},{5,1},{2,6},{6,2},{3,7},{7,3},{8,12},{12,8},{9,1... | collective-permute-start | bytes 417800 | tf_op jit(solution)/shard_map/ppermute | solution.py:291
  27.8 1.6 %collective-permute-start.14 = (bf16[4,256,128]{2,1,0:T(8,128)(2,1)S(1)}, bf16[4,256,128]{2,1,0:T(8,128)(2,1)S(1)}, u32[]{:S(2)}, u32[]{:S(2)}) collective-permute-start(bf16[4,256,128]{2,1,0:T(8,128)(2,1)S(1)} %get-tuple-element.33), channel_id=1, source_target_pairs={{0,4},{4,0},{1,5},{5,1},{2,6},{6,2},{3,7},{7,3},{8,12},{12,8},{9,1... | collective-permute-start | bytes 786440 | tf_op jit(solution)/shard_map/ppermute | solution.py:291
  29.0 1.7 %collective-permute-start.13 = (bf16[5,256,128]{2,1,0:T(8,128)(2,1)S(1)}, bf16[5,256,128]{2,1,0:T(8,128)(2,1)S(1)}, u32[]{:S(2)}, u32[]{:S(2)}) collective-permute-start(bf16[5,256,128]{2,1,0:T(8,128)(2,1)S(1)} %get-tuple-element.31), channel_id=1, source_target_pairs={{0,4},{4,0},{1,5},{5,1},{2,6},{6,2},{3,7},{7,3},{8,12},{12,8},{9,1... | collective-permute-start | bytes 983048 | tf_op jit(solution)/shard_map/ppermute | solution.py:291
  29.5 4.1 %collective-permute-start.16 = (bf16[256,128]{1,0:T(8,128)(2,1)S(1)}, bf16[256,128]{1,0:T(8,128)(2,1)S(1)}, u32[]{:S(2)}, u32[]{:S(2)}) collective-permute-start(bf16[256,128]{1,0:T(8,128)(2,1)S(1)} %get-tuple-element.45), channel_id=1, source_target_pairs={{0,20},{1,21},{2,22},{3,23},{4,16},{5,17},{6,18},{7,19},{8,28},{9,... | collective-permute-start | bytes 196616 | tf_op jit(solution)/shard_map/ppermute | solution.py:287
  30.8 14.9 %copy-start.4 = (bf16[256,256]{1,0:T(8,128)(2,1)S(1)}, bf16[256,256]{1,0:T(8,128)(2,1)}, u32[]{:S(2)}) copy-start(bf16[256,256]{1,0:T(8,128)(2,1)} %w_ref.1) | copy-start | bytes 393220
  30.8 5.6 %collective-permute-start.15 = (bf16[2,256,128]{2,1,0:T(8,128)(2,1)S(1)}, bf16[2,256,128]{2,1,0:T(8,128)(2,1)S(1)}, u32[]{:S(2)}, u32[]{:S(2)}) collective-permute-start(bf16[2,256,128]{2,1,0:T(8,128)(2,1)S(1)} %pad_maximum_fusion.3), channel_id=1, source_target_pairs={{0,20},{1,21},{2,22},{3,23},{4,16},{5,17},{6,18},{7,19},{8,28},{9,... | collective-permute-start | bytes 393224 | tf_op jit(solution)/shard_map/ppermute | solution.py:287
  33.7 4.6 %collective-permute-start.18 = (bf16[256,128]{1,0:T(8,128)(2,1)S(1)}, bf16[256,128]{1,0:T(8,128)(2,1)S(1)}, u32[]{:S(2)}, u32[]{:S(2)}) collective-permute-start(bf16[256,128]{1,0:T(8,128)(2,1)S(1)} %fusion.6), channel_id=1, source_target_pairs={{0,12},{1,13},{2,14},{3,15},{4,8},{5,9},{6,10},{7,11},{8,4},{9,5},... | collective-permute-start | bytes 196616 | tf_op jit(solution)/shard_map/ppermute | solution.py:287
  36.5 5.1 %collective-permute-start.17 = (bf16[256,128]{1,0:T(8,128)(2,1)S(1)}, bf16[256,128]{1,0:T(8,128)(2,1)S(1)}, u32[]{:S(2)}, u32[]{:S(2)}) collective-permute-start(bf16[256,128]{1,0:T(8,128)(2,1)S(1)} %get-tuple-element.47), channel_id=1, source_target_pairs={{0,12},{1,13},{2,14},{3,15},{4,8},{5,9},{6,10},{7,11},{8,4},{9,5},... | collective-permute-start | bytes 196616 | tf_op jit(solution)/shard_map/ppermute | solution.py:287
  37.4 4.4 %collective-permute-start.19 = (bf16[256,128]{1,0:T(8,128)(2,1)S(1)}, bf16[256,128]{1,0:T(8,128)(2,1)S(1)}, u32[]{:S(2)}, u32[]{:S(2)}) collective-permute-start(bf16[256,128]{1,0:T(8,128)(2,1)S(1)} %get-tuple-element.46), channel_id=1, source_target_pairs={{0,12},{1,13},{2,14},{3,15},{4,8},{5,9},{6,10},{7,11},{8,4},{9,5},... | collective-permute-start | bytes 196616 | tf_op jit(solution)/shard_map/ppermute | solution.py:287
  38.3 5.7 %collective-permute-start.21 = (bf16[256,128]{1,0:T(8,128)(2,1)S(1)}, bf16[256,128]{1,0:T(8,128)(2,1)S(1)}, u32[]{:S(2)}, u32[]{:S(2)}) collective-permute-start(bf16[256,128]{1,0:T(8,128)(2,1)S(1)} %fusion.4), channel_id=1, source_target_pairs={{0,7},{1,6},{2,5},{3,4},{4,3},{5,2},{6,1},{7,0},{8,15},{9,14},{10,... | collective-permute-start | bytes 196616 | tf_op jit(solution)/shard_map/ppermute | solution.py:287
  41.8 3.9 %collective-permute-start.20 = (bf16[256,128]{1,0:T(8,128)(2,1)S(1)}, bf16[256,128]{1,0:T(8,128)(2,1)S(1)}, u32[]{:S(2)}, u32[]{:S(2)}) collective-permute-start(bf16[256,128]{1,0:T(8,128)(2,1)S(1)} %get-tuple-element.37), channel_id=1, source_target_pairs={{0,5},{1,4},{2,7},{3,6},{4,1},{5,0},{6,3},{7,2},{8,13},{9,12},{10,... | collective-permute-start | bytes 196616 | tf_op jit(solution)/shard_map/ppermute | solution.py:287
